TPU v7x, 768 devices: a whole 4x8x12 slice. The times are simulated.
768 devices in a mesh: tile: 24 (over z, core), lev: 32 (over y, x).
Axes of the slice: x: 4, y: 8, z: 12, core: 2. Of those that a mesh axis runs over, the one named last changes fastest.
Arguments:
- adj_arrival: float32 [128, 4, 192, 512], P('lev', None, 'tile'), may hold values from -6 to 6
- vert_coef: float32 [3, 128, 192, 512], P(None, 'lev', 'tile'), may hold values from 0.1 to 0.9
- stencil_weight: bfloat16 [192, 4, 16, 512], P('tile'), may hold values from -1.5 to 1.5
- stencil_cols: int32 [192, 4, 16, 512], P('tile'), may hold values from 0 to 511, as said below
- dep_owner: int32 [192, 4], P('tile'), may hold values from 0 to 23, all different within a row; in each aligned block of 8 rows (0 to 7, 8 to 15, ...) at most 2 rows name the same one
- dep_slot: int32 [192, 4], P('tile'), may hold values from 0 to 7
Outputs:
- adj_departure: float32 [128, 4, 192, 512], P('lev', None, 'tile')
Inputs may be any that keep to these rules, and one draw needn't show every extreme that they name: `dep_owner`: each row holds 4 different owners. Among the rows of one tile (aligned blocks of 8 rows) no owner is named more than 2 times, a bound that some block reaches. `stencil_cols`: the 16 source columns of a departure point form a 4 by 4 patch of columns, rows of 16 columns apart, taken cyclically within the block.
All inputs are finite; a program needn't handle non-finite values.
Results may differ from a plain program's by a relative error of at most 0.0029.
Values sent between devices are 32-bit elements; how exact they have to be, the bound alone decides.
No kernel may reach another device: no remote copies, remote signals or barrier semaphores. Data moves between devices by JAX's collectives and lax.ppermute only.
A program may use at most 32 MiB of HBM per device.

v0:
```python
import jax
import jax.numpy as jnp
from jax import lax
from jax.sharding import PartitionSpec as P


def extended(array, sides, width):
    for axis, dim in sides:
        devices, length = (lax.axis_size(axis), array.shape[dim])
        up = [(i, (i + 1) % devices) for i in range(devices - 1)]
        down = [(j, i) for i, j in up]
        last = lax.slice_in_dim(array, length - width, length, axis=dim)
        first = lax.slice_in_dim(array, 0, width, axis=dim)
        before = lax.ppermute(last, axis, up)
        after = lax.ppermute(first, axis, down)
        array = jnp.concatenate([before, array, after], axis=dim)
    return array


def shards(adj_arrival, vert_coef, stencil_weight, stencil_cols, dep_owner, dep_slot):
    lev_dev, fields, blk_dev, cols = adj_arrival.shape
    tiles = lax.axis_size("tile")
    deps = dep_owner.shape[1]
    points = stencil_weight.shape[2]
    items = blk_dev * deps
    rows = lev_dev * fields
    below = vert_coef[0][:, None]
    middle = vert_coef[1][:, None]
    above = vert_coef[2][:, None]
    stacked = jnp.stack([below * adj_arrival, above * adj_arrival], 0)
    padded = extended(stacked, (("lev", 1),), 1)
    vert_adj = padded[0, 2:] + middle * adj_arrival + padded[1, :-2]
    vert_low = vert_adj.astype(jnp.bfloat16).reshape(rows, blk_dev, cols)
    block_major = jnp.transpose(vert_low, (1, 0, 2)).astype(jnp.float32)
    dest_ids = lax.broadcasted_iota(jnp.int32, (1, cols, 1), 1)

    def per_block(carry, packed):
        weights, columns, block_in = packed
        mapping = jnp.zeros((deps, cols, cols), jnp.float32)
        for point in range(points):
            hit = columns[:, point][:, None, :] == dest_ids
            mapping = mapping + jnp.where(
                hit, weights[:, point].astype(jnp.float32)[:, None, :], 0.0
            )
        result = jnp.einsum("kdc,rc->krd", mapping, block_in, precision=lax.Precision.HIGHEST)
        return (carry, result)

    _, pieces = lax.scan(per_block, 0, (stencil_weight, stencil_cols, block_major))
    contrib = pieces.reshape(items, rows * cols)
    owner = dep_owner.reshape(items)
    slot = dep_slot.reshape(items)
    target = owner * blk_dev + slot
    places = lax.broadcasted_iota(jnp.int32, (tiles * blk_dev, items), 0)
    picker = (places == target[None, :]).astype(jnp.float32)
    outgoing = jnp.dot(picker, contrib, precision=lax.Precision.HIGHEST).reshape(
        tiles, blk_dev, rows * cols
    )
    incoming = lax.all_to_all(outgoing, "tile", split_axis=0, concat_axis=0, tiled=True)
    gathered = incoming.sum(0)
    result = gathered.reshape(blk_dev, lev_dev, fields, cols)
    return jnp.transpose(result, (1, 2, 0, 3))


def solution(mesh):
    in_specs = (
        P("lev", None, "tile", None),
        P(None, "lev", "tile", None),
        P("tile", None, None, None),
        P("tile", None, None, None),
        P("tile", None),
        P("tile", None),
    )
    out_specs = P("lev", None, "tile", None)
    return jax.shard_map(shards, mesh=mesh, in_specs=in_specs, out_specs=out_specs, check_vma=False)
```

profile of v0, /device:TPU:32, one launch (start us, length us, event | category | flops | bytes accessed | tf_op | source)
XLA Modules:
  0.0 366.6 jit_solution(15271259754486629400)
XLA Ops:
  0.0 0.9 slice_bitcast_fusion.32
  0.9 1.0 multiply_bitcast_fusion.1
  2.0 4.6 %collective-permute-start = (f32[2,1,4,8,512]{4,3,2,1,0:T(8,128)S(1)}, f32[2,1,4,8,512]{4,3,2,1,0:T(8,128)S(1)}, u32[]{:S(2)}, u32[]{:S(2)}) collective-permute-start(f32[2,1,4,8,512]{4,3,2,1,0:T(8,128)S(1)} %get-tuple-element.177), channel_id=1, source_target_pairs={{1,0},{2,1},{3,2},{4,3},{5,4},{6,5},{7,6},{8,7},{9,8},{10,9},{11,1... | collective-permute-start | bytes 393224 | tf_op jit(solution)/shard_map/ppermute | solution.py:15
  6.5 1.9 collective-permute-start.1
  8.4 0.7 multiply_add_fusion.1
  9.2 0.1 copy.11
  9.2 0.1 add.69
  9.3 0.0 collective-permute-done
  9.3 7.4 %collective-permute-done.1 = f32[2,1,4,8,512]{4,3,2,1,0:T(8,128)S(1)} collective-permute-done((f32[2,1,4,8,512]{4,3,2,1,0:T(8,128)S(1)}, f32[2,1,4,8,512]{4,3,2,1,0:T(8,128)S(1)}, u32[]{:S(2)}, u32[]{:S(2)}) %collective-permute-start.1) | collective-permute-done | bytes 131104 | tf_op jit(solution)/shard_map/ppermute | solution.py:14
  16.7 1.0 fusion.95
  17.8 0.2 copy.23
  17.9 116.7 %while.12 = (s32[]{:T(128)}, f32[8,4,16,512]{3,2,1,0:T(8,128)S(1)}, f32[8,16,512]{2,1,0:T(8,128)S(1)}, s32[8,4,16,512]{3,2,1,0:T(8,128)}, bf16[8,4,16,512]{3,2,1,0:T(8,128)(2,1)}, /*index=5*/s32[]{:T(128)}) while((s32[]{:T(128)}, f32[8,4,16,512]{3,2,1,0:T(8,128)S(1)}, f32[8,16,512]{2,1,0:T(8,128)S(1)}, ...), condition=%wide.region_1.2_spmd.clone.clone, body=%wide.region_0.1_spmd.clone.clone.sunk | while | flops 250642432 | bytes 1672277 | solution.py:48
  17.9 0.8 constant_dynamic-slice_fusion.4
  18.8 0.1 copy.26
  18.9 0.9 constant_dynamic-slice_fusion.5
  19.8 0.1 copy.27
  19.9 12.6 %fusion.110 = f32[8,4,16,512]{3,2,1,0:T(8,128)S(1)} fusion(f32[8,4,16,512]{3,2,1,0:T(8,128)S(1)} %get-tuple-element.286, s32[]{:T(128)S(6)} %copy.31, f32[4,512]{1,0:T(4,128)S(1)} %get-tuple-element.247, s32[4,512]{1,0:T(4,128)S(1)} %get-tuple-element.248, f32[4,512]{1,0:T(4,128)S(1)} %get-tuple-element.249, s32[4,512]{1,0:T(4,128)S(1)} %get-tuple-element.250, ...), kind=kOutput, calls=%fused_computation.83.clone.1 | convolution fusion | flops 250609664 | bytes 427008 | tf_op jit(solution)/shard_map/while/body/eval_jaxpr/kdc,rc->krd/dot_general | solution.py:45
  32.5 0.8 constant_dynamic-slice_fusion.4
  33.4 0.1 copy.26
  33.5 0.9 constant_dynamic-slice_fusion.5
  34.4 0.1 copy.27
  34.5 12.6 %fusion.110 = f32[8,4,16,512]{3,2,1,0:T(8,128)S(1)} fusion(f32[8,4,16,512]{3,2,1,0:T(8,128)S(1)} %get-tuple-element.286, s32[]{:T(128)S(6)} %copy.31, f32[4,512]{1,0:T(4,128)S(1)} %get-tuple-element.247, s32[4,512]{1,0:T(4,128)S(1)} %get-tuple-element.248, f32[4,512]{1,0:T(4,128)S(1)} %get-tuple-element.249, s32[4,512]{1,0:T(4,128)S(1)} %get-tuple-element.250, ...), kind=kOutput, calls=%fused_computation.83.clone.1 | convolution fusion | flops 250609664 | bytes 427008 | tf_op jit(solution)/shard_map/while/body/eval_jaxpr/kdc,rc->krd/dot_general | solution.py:45
  47.1 0.8 constant_dynamic-slice_fusion.4
  48.0 0.1 copy.26
  48.0 0.9 constant_dynamic-slice_fusion.5
  49.0 0.1 copy.27
  49.1 12.6 %fusion.110 = f32[8,4,16,512]{3,2,1,0:T(8,128)S(1)} fusion(f32[8,4,16,512]{3,2,1,0:T(8,128)S(1)} %get-tuple-element.286, s32[]{:T(128)S(6)} %copy.31, f32[4,512]{1,0:T(4,128)S(1)} %get-tuple-element.247, s32[4,512]{1,0:T(4,128)S(1)} %get-tuple-element.248, f32[4,512]{1,0:T(4,128)S(1)} %get-tuple-element.249, s32[4,512]{1,0:T(4,128)S(1)} %get-tuple-element.250, ...), kind=kOutput, calls=%fused_computation.83.clone.1 | convolution fusion | flops 250609664 | bytes 427008 | tf_op jit(solution)/shard_map/while/body/eval_jaxpr/kdc,rc->krd/dot_general | solution.py:45
  61.7 0.8 constant_dynamic-slice_fusion.4
  62.6 0.1 copy.26
  62.6 0.9 constant_dynamic-slice_fusion.5
  63.6 0.1 copy.27
  63.7 12.6 %fusion.110 = f32[8,4,16,512]{3,2,1,0:T(8,128)S(1)} fusion(f32[8,4,16,512]{3,2,1,0:T(8,128)S(1)} %get-tuple-element.286, s32[]{:T(128)S(6)} %copy.31, f32[4,512]{1,0:T(4,128)S(1)} %get-tuple-element.247, s32[4,512]{1,0:T(4,128)S(1)} %get-tuple-element.248, f32[4,512]{1,0:T(4,128)S(1)} %get-tuple-element.249, s32[4,512]{1,0:T(4,128)S(1)} %get-tuple-element.250, ...), kind=kOutput, calls=%fused_computation.83.clone.1 | convolution fusion | flops 250609664 | bytes 427008 | tf_op jit(solution)/shard_map/while/body/eval_jaxpr/kdc,rc->krd/dot_general | solution.py:45
  76.3 0.8 constant_dynamic-slice_fusion.4
  77.1 0.1 copy.26
  77.2 0.9 constant_dynamic-slice_fusion.5
  78.2 0.1 copy.27
  78.3 12.6 %fusion.110 = f32[8,4,16,512]{3,2,1,0:T(8,128)S(1)} fusion(f32[8,4,16,512]{3,2,1,0:T(8,128)S(1)} %get-tuple-element.286, s32[]{:T(128)S(6)} %copy.31, f32[4,512]{1,0:T(4,128)S(1)} %get-tuple-element.247, s32[4,512]{1,0:T(4,128)S(1)} %get-tuple-element.248, f32[4,512]{1,0:T(4,128)S(1)} %get-tuple-element.249, s32[4,512]{1,0:T(4,128)S(1)} %get-tuple-element.250, ...), kind=kOutput, calls=%fused_computation.83.clone.1 | convolution fusion | flops 250609664 | bytes 427008 | tf_op jit(solution)/shard_map/while/body/eval_jaxpr/kdc,rc->krd/dot_general | solution.py:45
  90.9 0.8 constant_dynamic-slice_fusion.4
  91.7 0.1 copy.26
  91.8 0.9 constant_dynamic-slice_fusion.5
  92.7 0.1 copy.27
  92.9 12.6 %fusion.110 = f32[8,4,16,512]{3,2,1,0:T(8,128)S(1)} fusion(f32[8,4,16,512]{3,2,1,0:T(8,128)S(1)} %get-tuple-element.286, s32[]{:T(128)S(6)} %copy.31, f32[4,512]{1,0:T(4,128)S(1)} %get-tuple-element.247, s32[4,512]{1,0:T(4,128)S(1)} %get-tuple-element.248, f32[4,512]{1,0:T(4,128)S(1)} %get-tuple-element.249, s32[4,512]{1,0:T(4,128)S(1)} %get-tuple-element.250, ...), kind=kOutput, calls=%fused_computation.83.clone.1 | convolution fusion | flops 250609664 | bytes 427008 | tf_op jit(solution)/shard_map/while/body/eval_jaxpr/kdc,rc->krd/dot_general | solution.py:45
  105.5 0.8 constant_dynamic-slice_fusion.4
  106.3 0.1 copy.26
  106.4 0.9 constant_dynamic-slice_fusion.5
  107.3 0.1 copy.27
  107.5 12.6 %fusion.110 = f32[8,4,16,512]{3,2,1,0:T(8,128)S(1)} fusion(f32[8,4,16,512]{3,2,1,0:T(8,128)S(1)} %get-tuple-element.286, s32[]{:T(128)S(6)} %copy.31, f32[4,512]{1,0:T(4,128)S(1)} %get-tuple-element.247, s32[4,512]{1,0:T(4,128)S(1)} %get-tuple-element.248, f32[4,512]{1,0:T(4,128)S(1)} %get-tuple-element.249, s32[4,512]{1,0:T(4,128)S(1)} %get-tuple-element.250, ...), kind=kOutput, calls=%fused_computation.83.clone.1 | convolution fusion | flops 250609664 | bytes 427008 | tf_op jit(solution)/shard_map/while/body/eval_jaxpr/kdc,rc->krd/dot_general | solution.py:45
  120.1 0.8 constant_dynamic-slice_fusion.4
  120.9 0.1 copy.26
  121.0 0.9 constant_dynamic-slice_fusion.5
  121.9 0.1 copy.27
  122.0 12.6 %fusion.110 = f32[8,4,16,512]{3,2,1,0:T(8,128)S(1)} fusion(f32[8,4,16,512]{3,2,1,0:T(8,128)S(1)} %get-tuple-element.286, s32[]{:T(128)S(6)} %copy.31, f32[4,512]{1,0:T(4,128)S(1)} %get-tuple-element.247, s32[4,512]{1,0:T(4,128)S(1)} %get-tuple-element.248, f32[4,512]{1,0:T(4,128)S(1)} %get-tuple-element.249, s32[4,512]{1,0:T(4,128)S(1)} %get-tuple-element.250, ...), kind=kOutput, calls=%fused_computation.83.clone.1 | convolution fusion | flops 250609664 | bytes 427008 | tf_op jit(solution)/shard_map/while/body/eval_jaxpr/kdc,rc->krd/dot_general | solution.py:45
  134.7 0.2 reshape.82
  134.9 2.7 fusion.98
  137.5 225.3 %all_to_all.5 = f32[24,8,8192]{2,1,0:T(8,128)} all-to-all(f32[24,8,8192]{2,1,0:T(8,128)S(1)} %fusion.98), channel_id=1, replica_groups=mesh['tile'=24,'lev'=32] {'tile'}, dimensions={0} | all-to-all | bytes 12582912 | tf_op jit(solution)/shard_map/all_to_all | solution.py:58
  362.8 3.8 %reduce_sum.9 = f32[8,8192]{1,0:T(8,128)} reduce(f32[24,8,8192]{2,1,0:T(8,128)} %all_to_all.5, f32[]{:T(128)} %constant.22.clone.1), dimensions={0}, to_apply=%region_2.3 | reduce | flops 1507328 | bytes 6553604 | tf_op jit(solution)/shard_map/reduce_sum | solution.py:59
  (20 shorter events, 0.3 us)
Async XLA Ops:
  2.0 7.4 %collective-permute-start = (f32[2,1,4,8,512]{4,3,2,1,0:T(8,128)S(1)}, f32[2,1,4,8,512]{4,3,2,1,0:T(8,128)S(1)}, u32[]{:S(2)}, u32[]{:S(2)}) collective-permute-start(f32[2,1,4,8,512]{4,3,2,1,0:T(8,128)S(1)} %get-tuple-element.177), channel_id=1, source_target_pairs={{1,0},{2,1},{3,2},{4,3},{5,4},{6,5},{7,6},{8,7},{9,8},{10,9},{11,1... | collective-permute-start | bytes 393224 | tf_op jit(solution)/shard_map/ppermute | solution.py:15
  6.5 10.2 %collective-permute-start.1 = (f32[2,1,4,8,512]{4,3,2,1,0:T(8,128)S(1)}, f32[2,1,4,8,512]{4,3,2,1,0:T(8,128)S(1)}, u32[]{:S(2)}, u32[]{:S(2)}) collective-permute-start(f32[2,1,4,8,512]{4,3,2,1,0:T(8,128)S(1)} %get-tuple-element.178), channel_id=1, source_target_pairs={{0,1},{1,2},{2,3},{3,4},{4,5},{5,6},{6,7},{7,8},{8,9},{9,10},{10,1... | collective-permute-start | bytes 393224 | tf_op jit(solution)/shard_map/ppermute | solution.py:14
where the time goes:
time: 367 us
  blocking collectives  225 us (61%)
  matrix products  103 us (28%)
  local copies, waits for them, and re-layouts  16.8 us (5%)
  waiting for transfers between devices  7.37 us (2%)
  other arithmetic  6.7 us (2%)
  starting transfers between devices  6.47 us (2%)
    all_to_all x1, blocking collectives, shards(): lax.all_to_all(outgoing, 'tile', split_axis=0, concat_axis=0, tiled=True)  225 us
    dot_general x8, matrix products, per_block(): jnp.einsum('kdc,rc->krd', mapping, block_in, precision=lax.Precision.HIGH...  101 us
    dynamic_slice x32, local copies, waits for them, and re-layouts, shards(): lax.scan(per_block, 0, (stencil_weight, stencil_cols, block_major))  15.3 us
    ppermute x1, waiting for transfers between devices, extended(): before = lax.ppermute(last, axis, up)  7.37 us
  transfers between devices with their start and end apart: 2, of which 1 were waited for; matrix products, arithmetic and copies ran while one was open for 0% of the time, Pallas kernels for 0%

commit v1 on v0

v1 whole, which is shorter than its diff:
```python
import functools

import jax
import jax.numpy as jnp
from jax import lax
from jax.experimental import pallas as pl
from jax.experimental.pallas import tpu as pltpu
from jax.sharding import PartitionSpec as P

WIN = 32
SPAN = 96
LANES = 128
CAP = 2
MIB = 1024 * 1024


def stage_sizes(far):
    return [2 * CAP] + [4 * CAP] * (far - 1) + [2 * CAP]


def fill_table(chips, owner_ref, slot_ref, table, count):
    blk, deps = owner_ref.shape
    far = chips // 2
    tile = lax.axis_index("tile")
    chip, core = lax.div(tile, 2), lax.rem(tile, 2)
    ahead = 1 - 2 * core
    entries = sum(stage_sizes(far))

    def clear(n, _):
        table[0, n] = jnp.int32(-1)
        table[1, n] = jnp.int32(0)
        return 0

    lax.fori_loop(0, entries, clear, 0)

    def reset(n, _):
        count[n] = jnp.int32(0)
        return 0

    lax.fori_loop(0, 2 * chips, reset, 0)

    def enter(n, _):
        row, k = lax.div(n, deps), lax.rem(n, deps)
        owner = owner_ref[row, k]
        turn = count[owner]
        count[owner] = turn + 1
        away = lax.rem(ahead * (lax.div(owner, 2) - chip) + chips, chips)
        back = away > far
        distance = jnp.where(back, chips - away, away)
        own = (lax.rem(owner, 2) == core).astype(jnp.int32)
        half = jnp.where(back, 1 - own, own)
        start = jnp.where(
            away == 0,
            entries - 2 * CAP,
            jnp.where(away == far, 0, 2 * CAP + (far - 1 - distance) * 4 * CAP + jnp.where(back, 2 * CAP, 0)),
        )
        at = start + half * CAP + turn
        table[0, at] = n
        table[1, at] = slot_ref[row, k]
        return 0

    lax.fori_loop(0, blk * deps, enter, 0)


def place_kernel(chips, owner_ref, slot_ref, w_ref, cols_ref, p_ref, q_ref, table, x_sc, count):
    @pl.when(pl.program_id(0) == 0)
    def _():
        fill_table(chips, owner_ref, slot_ref, table, count)

    deps, points, cols = cols_ref.shape
    place = lax.broadcasted_iota(jnp.int32, (SPAN, LANES), 0).astype(jnp.float32).astype(jnp.bfloat16)
    q_ref[...] = jnp.zeros_like(q_ref)
    for k in range(deps):
        d = cols_ref[k]
        rel = ((d - d[0:1] + cols // 2) & (cols - 1)) - cols // 2
        low = jnp.min(rel, axis=0, keepdims=True)
        base = (d[0:1] + low) & (cols - 1)
        x_sc[k] = (rel - low + (base & (WIN - 1))).astype(jnp.float32).astype(jnp.bfloat16)
        q_ref[0, k:k + 1, :] = base // WIN
        for t in range(cols // LANES):
            part = slice(t * LANES, (t + 1) * LANES)
            x, w = x_sc[k, :, part], w_ref[k, :, part]
            acc = jnp.zeros((SPAN, LANES), jnp.bfloat16)
            for s in range(points):
                acc = jnp.where(place == x[s:s + 1], w[s:s + 1], acc)
            p_ref[k, :, part] = acc


def placed(chips, dep_owner, dep_slot, weight, places):
    blk, deps = dep_owner.shape
    items, points, cols = weight.shape
    entries = sum(stage_sizes(chips // 2))
    smem = pl.BlockSpec(memory_space=pltpu.SMEM)
    return pl.pallas_call(
        functools.partial(place_kernel, chips),
        grid=(blk,),
        in_specs=[
            smem,
            smem,
            pl.BlockSpec((deps, points, cols), lambda a: (a, 0, 0)),
            pl.BlockSpec((deps, points, cols), lambda a: (a, 0, 0)),
        ],
        out_specs=[
            pl.BlockSpec((deps, SPAN, cols), lambda a: (a, 0, 0)),
            pl.BlockSpec((1, 8, cols), lambda a: (a, 0, 0)),
            smem,
        ],
        out_shape=[
            jax.ShapeDtypeStruct((items, SPAN, cols), jnp.bfloat16),
            jax.ShapeDtypeStruct((blk, 8, cols), jnp.int32),
            jax.ShapeDtypeStruct((2, entries), jnp.int32),
        ],
        scratch_shapes=[
            pltpu.VMEM((deps, points, cols), jnp.bfloat16),
            pltpu.SMEM((2 * chips,), jnp.int32),
        ],
        compiler_params=pltpu.CompilerParams(
            dimension_semantics=("arbitrary",), vmem_limit_bytes=8 * MIB
        ),
        cost_estimate=pl.CostEstimate(flops=10000000000, bytes_accessed=5000000, transcendentals=0),
        name="place",
    )(dep_owner, dep_slot, weight, places)


def item_contribution(v, q, p_ref, index, v_sc, p_sc):
    rows, cols = v.shape
    for i in range(cols // WIN):
        v_sc[i * rows:(i + 1) * rows, :] = jnp.where(q == i, v, 0.0).astype(jnp.bfloat16)
    p_sc[0:SPAN, :] = p_ref[index]
    u = lax.dot_general(
        v_sc[...], p_sc[...], (((1,), (1,)), ((), ())), preferred_element_type=jnp.float32
    )
    lane = lax.broadcasted_iota(jnp.int32, (rows, LANES), 1)
    kept, passed = [], []
    for t in range(cols // LANES):
        u0, u1, u2, u3 = (u[(4 * t + j) * rows:(4 * t + j + 1) * rows] for j in range(4))
        kept.append(u0 + pltpu.roll(u1, WIN, 1))
        passed.append(pltpu.roll(u2, 2 * WIN, 1) + pltpu.roll(u3, 3 * WIN, 1))
    return [
        kept[t] + jnp.where(lane >= LANES // 2, passed[t], passed[t - 1]) for t in range(len(kept))
    ]


def stage_kernel(offset, listed, deps, rows, table, v_ref, p_ref, q_ref, *rest):
    outs, (v_sc, p_sc) = rest[:-2], rest[-2:]
    cols = v_ref.shape[-1]
    blk = v_ref.shape[0]
    p_sc[SPAN:, :] = jnp.zeros((LANES - SPAN, cols), jnp.bfloat16)
    for g, out in enumerate(outs):
        first = offset + g * 2 * CAP
        out[...] = jnp.zeros_like(out)
        if listed:
            ids = lax.broadcasted_iota(jnp.int32, (8, cols), 0)
            slots = jnp.zeros((8, cols), jnp.int32)
            for n in range(2 * CAP):
                slots = jnp.where(ids == n, table[1, first + n], slots)
            out[2 * CAP * rows:, :] = slots.astype(jnp.float32)

        def one(n, _):
            index = table[0, first + n]

            @pl.when(index >= 0)
            def _():
                row = lax.div(index, deps)
                v = v_ref[row].astype(jnp.float32)
                q = q_ref[row, pl.ds(lax.rem(index, deps), 1), :]
                parts = item_contribution(v, q, p_ref, index, v_sc, p_sc)
                if listed:
                    at = n * rows
                else:
                    at = (lax.div(n, CAP) * blk + table[1, first + n]) * rows
                at = pl.multiple_of(at, rows)
                for t, part in enumerate(parts):
                    where = (pl.ds(at, rows), slice(t * LANES, (t + 1) * LANES))
                    out[where] = out[where] + part

            return 0

        lax.fori_loop(0, 2 * CAP, one, 0)


def stage(offset, groups, listed, deps, table, v, p, q):
    blk, rows, cols = v.shape
    height = 2 * CAP * rows + 8 if listed else 2 * blk * rows
    vmem = pl.BlockSpec(memory_space=pltpu.VMEM)
    return pl.pallas_call(
        functools.partial(stage_kernel, offset, listed, deps, rows),
        in_specs=[pl.BlockSpec(memory_space=pltpu.SMEM), vmem, vmem, vmem],
        out_specs=[vmem] * groups,
        out_shape=[jax.ShapeDtypeStruct((height, cols), jnp.float32)] * groups,
        scratch_shapes=[
            pltpu.VMEM((cols // WIN * rows, cols), jnp.bfloat16),
            pltpu.VMEM((LANES, cols), jnp.bfloat16),
        ],
        compiler_params=pltpu.CompilerParams(vmem_limit_bytes=10 * MIB),
        cost_estimate=pl.CostEstimate(
            flops=groups * 1700000000, bytes_accessed=500000, transcendentals=0
        ),
        name="stage",
    )(table, v, p, q)


def merge_kernel(blk, rows, own_ref, given_ref, items_ref, *outs):
    width = own_ref.shape[1]
    for half, out in enumerate(outs):
        for c in range(0, width, LANES):
            part = slice(c, c + LANES)
            items = []
            for n in range(half * CAP, half * CAP + CAP):
                at = 2 * CAP * rows + n
                items.append((items_ref[at:at + 1, part], items_ref[n * rows:(n + 1) * rows, part]))
            for b in range(blk):
                at = (half * blk + b) * rows
                total = own_ref[at:at + rows, part] + given_ref[at:at + rows, part]
                for slot, value in items:
                    total = total + jnp.where(slot == float(b), value, 0.0)
                out[b * rows:(b + 1) * rows, part] = total


def merge(blk, rows, own, given, items):
    width = own.shape[1]
    return pl.pallas_call(
        functools.partial(merge_kernel, blk, rows),
        out_shape=[jax.ShapeDtypeStruct((blk * rows, width), jnp.float32)] * 2,
        compiler_params=pltpu.CompilerParams(vmem_limit_bytes=4 * MIB),
        cost_estimate=pl.CostEstimate(flops=1000000, bytes_accessed=1000000, transcendentals=0),
        name="merge",
    )(own, given, items)


def shards(adj_arrival, vert_coef, stencil_weight, stencil_cols, dep_owner, dep_slot):
    lev_dev, fields, blk, cols = adj_arrival.shape
    tiles, levels = lax.axis_size("tile"), lax.axis_size("lev")
    deps, points = stencil_weight.shape[1:3]
    items, rows = blk * deps, lev_dev * fields
    chips = tiles // 2
    far = chips // 2

    first = vert_coef[0, :1, None] * adj_arrival[:1]
    last = vert_coef[2, -1:, None] * adj_arrival[-1:]
    after = lax.ppermute(first, "lev", [(i + 1, i) for i in range(levels - 1)])
    before = lax.ppermute(last, "lev", [(i, i + 1) for i in range(levels - 1)])

    p, q, table = placed(
        chips,
        dep_owner,
        dep_slot,
        stencil_weight.reshape(items, points, cols),
        stencil_cols.reshape(items, points, cols),
    )

    z_low = vert_coef[0, 1:, None] * adj_arrival[1:]
    z_high = vert_coef[2, :-1, None] * adj_arrival[:-1]
    vert_adj = (
        jnp.concatenate([z_low, after], 0)
        + vert_coef[1][:, None] * adj_arrival
        + jnp.concatenate([before, z_high], 0)
    )
    vert_low = vert_adj.astype(jnp.bfloat16).reshape(rows, blk, cols)
    v = jnp.transpose(vert_low, (1, 0, 2))

    sibling = [(t, t ^ 1) for t in range(tiles)]
    ring = [(t, (t + 2 * (1 - 2 * (t % 2))) % tiles) for t in range(tiles)]
    size = blk * rows
    quad = 2 * CAP

    def made(table, at, groups, listed=False):
        return stage(at, groups, listed, deps, table, v, p, q)

    def behind(table, *values):
        return lax.optimization_barrier((table, *values))

    (others,) = made(table, 2 * quad, 1)
    table, others = behind(table, others)
    given = lax.ppermute(others, "tile", sibling)
    (farthest,) = made(table, 0, 1, True)
    table, farthest = behind(table, farthest)
    arrived = lax.ppermute(farthest, "tile", ring)
    (own,) = made(table, quad, 1)
    table, own = behind(table, own)
    totals = list(merge(blk, rows, own, given, arrived))
    for n in range(1, far - 1):
        own, others = made(table, quad + n * 2 * quad, 2)
        table, totals[0] = behind(table, totals[0])
        given = lax.ppermute(others, "tile", sibling)
        here = lax.optimization_barrier([own[:size] + given[:size], own[size:] + given[size:]])
        sums = [lax.ppermute(total, "tile", ring) for total in totals]
        totals = [total + mine for total, mine in zip(sums, here)]
    sums = [lax.ppermute(total, "tile", ring) for total in totals]
    (here,) = made(table, quad + (far - 1) * 2 * quad, 1)
    swapped = lax.ppermute(sums[0] + here[:size], "tile", sibling)
    result = sums[1] + here[size:] + swapped
    result = jnp.transpose(result.reshape(blk, rows, cols), (1, 0, 2))
    return result.reshape(lev_dev, fields, blk, cols)


def solution(mesh):
    in_specs = (
        P("lev", None, "tile", None),
        P(None, "lev", "tile", None),
        P("tile", None, None, None),
        P("tile", None, None, None),
        P("tile", None),
        P("tile", None),
    )
    out_specs = P("lev", None, "tile", None)
    return jax.shard_map(shards, mesh=mesh, in_specs=in_specs, out_specs=out_specs, check_vma=False)
```

time: 367 us -> 114 us (0.31)
  the two profiles are of different devices: /device:TPU:32 before, /device:TPU:33 now
where the time goes in v1:
time: 114 us; the launch traced here: 113 us
  starting transfers between devices  75.2 us (66%)
  Pallas kernels  22.5 us (20%)
  local copies, waits for them, and re-layouts  7.1 us (6%)
  waiting for transfers between devices  5.43 us (5%)
  other arithmetic  2.76 us (2%)
    ppermute x10, starting transfers between devices, shards(): sums = [lax.ppermute(total, 'tile', ring) for total in totals]  32.8 us
    ppermute x1, starting transfers between devices, shards(): arrived = lax.ppermute(farthest, 'tile', ring)  15.2 us
    pallas_call x8, Pallas kernels, stage(): pl.pallas_call(functools.partial(stage_kernel, offset, listed, deps, rows...  14.7 us
    ppermute x5, starting transfers between devices, shards(): given = lax.ppermute(others, 'tile', sibling)  11.3 us
    pallas_call x1, Pallas kernels, placed(): pl.pallas_call(functools.partial(place_kernel, chips), grid=(blk,), in_sp...  7.73 us
    ppermute x1, starting transfers between devices, shards(): swapped = lax.ppermute(sums[0] + here[:size], 'tile', sibling)  7.24 us
    ppermute x1, starting transfers between devices, shards(): after = lax.ppermute(first, 'lev', [(i + 1, i) for i in range(levels - 1)])  5.48 us
    unnamed x8, local copies, waits for them, and re-layouts  3.78 us
  transfers between devices with their start and end apart: 19, of which 4 were waited for; matrix products, arithmetic and copies ran while one was open for 4% of the time, Pallas kernels for 17%

profile of v1, /device:TPU:33, one launch (start us, length us, event | category | flops | bytes accessed | tf_op | source)
XLA Modules:
  0.0 113.4 jit_solution(252158968515346526)
XLA Ops:
  0.0 0.7 slice_bitcast_fusion.3
  0.7 0.9 slice_multiply_fusion.2
  1.6 3.1 %collective-permute-start.1 = (f32[1,4,8,512]{3,2,1,0:T(8,128)S(1)}, f32[1,4,8,512]{3,2,1,0:T(8,128)S(1)}, u32[]{:S(2)}, u32[]{:S(2)}) collective-permute-start(f32[1,4,8,512]{3,2,1,0:T(8,128)S(1)} %get-tuple-element.83), channel_id=1, source_target_pairs={{0,1},{1,2},{2,3},{3,4},{4,5},{5,6},{6,7},{7,8},{8,9},{9,10},{10,1... | collective-permute-start | bytes 196616 | tf_op jit(solution)/shard_map/ppermute | solution.py:242
  4.8 5.5 %collective-permute-start = (f32[1,4,8,512]{3,2,1,0:T(8,128)S(1)}, f32[1,4,8,512]{3,2,1,0:T(8,128)S(1)}, u32[]{:S(2)}, u32[]{:S(2)}) collective-permute-start(f32[1,4,8,512]{3,2,1,0:T(8,128)S(1)} %get-tuple-element.84), channel_id=1, source_target_pairs={{1,0},{2,1},{3,2},{4,3},{5,4},{6,5},{7,6},{8,7},{9,8},{10,9},{11,1... | collective-permute-start | bytes 196616 | tf_op jit(solution)/shard_map/ppermute | solution.py:241
  10.2 0.8 slice_bitcast_fusion.1
  11.1 0.8 copy.7.owner_ref
  11.8 0.8 copy.8.slot_ref
  12.6 1.1 slice_multiply_fusion
  13.6 0.0 copy-start
  13.7 1.2 %copy-done = s32[8,4,16,512]{3,2,1,0:T(8,128)S(1)} copy-done((s32[8,4,16,512]{3,2,1,0:T(8,128)S(1)}, s32[8,4,16,512]{3,2,1,0:T(8,128)}, u32[]{:S(2)}) %copy-start) | copy-done | bytes 1048600
  14.9 1.0 copy-done.1
  15.9 7.7 %place.1 = (bf16[32,96,512]{2,1,0:T(8,128)(2,1)S(1)}, s32[8,8,512]{2,1,0:T(8,128)S(1)}, s32[2,48]{1,0:T(2,128)S(1)}) custom-call(s32[8,4]{1,0:T(8,128)S(1)} %copy.7.owner_ref, s32[8,4]{1,0:T(8,128)S(1)} %copy.8.slot_ref, bf16[32,16,512]{2,1,0:T(8,128)(2,1)S(1)} %bitcast.29, s32[32,16,512]{2,1,0:T(8,128)S(1)} %bitcast.28), custom_call_target="tpu_custom_call" | custom-call | flops 10000000000 | bytes 5000000 | tf_op jit(solution)/shard_map/place/pallas_call | solution.py:94
  23.7 0.8 slice_bitcast_fusion
  24.5 0.0 collective-permute-done.1
  24.5 0.0 collective-permute-done
  24.5 0.1 fusion.2
  24.7 1.8 %stage.8 = f32[256,512]{1,0:T(8,128)S(1)} custom-call(s32[2,48]{1,0:T(2,128)S(1)} %get-tuple-element.72.table, bf16[8,16,512]{2,1,0:T(8,128)(2,1)S(1)} %bitcast.20, bf16[32,96,512]{2,1,0:T(8,128)(2,1)S(1)} %get-tuple-element.41.p_ref, s32[8,8,512]{2,1,0:T(8,128)S(1)} %get-tuple-element.42.q_ref), custom_call_target="tpu_custom_call" | custom-call | flops 1700000000 | bytes 500000 | tf_op jit(solution)/shard_map/stage/pallas_call | solution.py:186
  26.5 1.5 %stage.9 = f32[72,512]{1,0:T(8,128)S(1)} custom-call(s32[2,48]{1,0:T(2,128)S(1)} %get-tuple-element.72.table, bf16[8,16,512]{2,1,0:T(8,128)(2,1)S(1)} %bitcast.21, bf16[32,96,512]{2,1,0:T(8,128)(2,1)S(1)} %get-tuple-element.41.p_ref, s32[8,8,512]{2,1,0:T(8,128)S(1)} %get-tuple-element.42.q_ref), custom_call_target="tpu_custom_call" | custom-call | flops 1700000000 | bytes 500000 | tf_op jit(solution)/shard_map/stage/pallas_call | solution.py:186
  28.0 2.8 %collective-permute-start.2 = (f32[256,512]{1,0:T(8,128)S(1)}, f32[256,512]{1,0:T(8,128)S(1)}, u32[]{:S(2)}, u32[]{:S(2)}) collective-permute-start(f32[256,512]{1,0:T(8,128)S(1)} %stage.8), channel_id=1, source_target_pairs={{0,32},{32,0},{64,96},{96,64},{128,160},{160,128},{192,224},{224,1... | collective-permute-start | bytes 1572872 | tf_op jit(solution)/shard_map/ppermute | solution.py:275
  30.8 1.5 %stage.10.own_ref = f32[256,512]{1,0:T(8,128)S(1)} custom-call(s32[2,48]{1,0:T(2,128)S(1)} %get-tuple-element.72.table, bf16[8,16,512]{2,1,0:T(8,128)(2,1)S(1)} %bitcast.22, bf16[32,96,512]{2,1,0:T(8,128)(2,1)S(1)} %get-tuple-element.41.p_ref, s32[8,8,512]{2,1,0:T(8,128)S(1)} %get-tuple-element.42.q_ref), custom_call_target="tpu_custom_call" | custom-call | flops 1700000000 | bytes 500000 | tf_op jit(solution)/shard_map/stage/pallas_call | solution.py:186
  32.3 1.9 %stage.11 = (f32[256,512]{1,0:T(8,128)S(1)}, f32[256,512]{1,0:T(8,128)S(1)}) custom-call(s32[2,48]{1,0:T(2,128)S(1)} %get-tuple-element.72.table, bf16[8,16,512]{2,1,0:T(8,128)(2,1)S(1)} %bitcast.23, bf16[32,96,512]{2,1,0:T(8,128)(2,1)S(1)} %get-tuple-element.41.p_ref, s32[8,8,512]{2,1,0:T(8,128)S(1)} %get-tuple-element.42.q_ref), custom_call_target="tpu_custom_call" | custom-call | flops 3400000000 | bytes 500000 | tf_op jit(solution)/shard_map/stage/pallas_call | solution.py:186
  34.2 2.2 %collective-permute-start.5 = (f32[256,512]{1,0:T(8,128)S(1)}, f32[256,512]{1,0:T(8,128)S(1)}, u32[]{:S(2)}, u32[]{:S(2)}) collective-permute-start(f32[256,512]{1,0:T(8,128)S(1)} %get-tuple-element.51), channel_id=1, source_target_pairs={{0,32},{32,0},{64,96},{96,64},{128,160},{160,128},{192,224},{224,1... | collective-permute-start | bytes 1572872 | tf_op jit(solution)/shard_map/ppermute | solution.py:285
  36.4 15.2 %collective-permute-start.3 = (f32[72,512]{1,0:T(8,128)S(1)}, f32[72,512]{1,0:T(8,128)S(1)}, u32[]{:S(2)}, u32[]{:S(2)}) collective-permute-start(f32[72,512]{1,0:T(8,128)S(1)} %stage.9), channel_id=1, source_target_pairs={{0,64},{32,736},{64,128},{96,32},{128,192},{160,96},{192,256},{224... | collective-permute-start | bytes 442376 | tf_op jit(solution)/shard_map/ppermute | solution.py:278
  51.6 2.1 %collective-permute-done.3.items_ref = f32[72,512]{1,0:T(8,128)S(1)} collective-permute-done((f32[72,512]{1,0:T(8,128)S(1)}, f32[72,512]{1,0:T(8,128)S(1)}, u32[]{:S(2)}, u32[]{:S(2)}) %collective-permute-start.3) | collective-permute-done | bytes 147488 | tf_op jit(solution)/shard_map/ppermute | solution.py:278
  53.7 0.0 collective-permute-done.2.given_ref
  53.7 0.1 merge.1
  53.8 5.0 %collective-permute-start.9 = (f32[128,512]{1,0:T(8,128)S(1)}, f32[128,512]{1,0:T(8,128)S(1)}, u32[]{:S(2)}, u32[]{:S(2)}) collective-permute-start(f32[128,512]{1,0:T(8,128)S(1)} %get-tuple-element.58), channel_id=1, source_target_pairs={{0,64},{32,736},{64,128},{96,32},{128,192},{160,96},{192,256},{224... | collective-permute-start | bytes 786440 | tf_op jit(solution)/shard_map/ppermute | solution.py:287
  58.8 1.9 %collective-permute-start.4 = (f32[128,512]{1,0:T(8,128)S(1)}, f32[128,512]{1,0:T(8,128)S(1)}, u32[]{:S(2)}, u32[]{:S(2)}) collective-permute-start(f32[128,512]{1,0:T(8,128)S(1)} %get-tuple-element.48), channel_id=1, source_target_pairs={{0,64},{32,736},{64,128},{96,32},{128,192},{160,96},{192,256},{224... | collective-permute-start | bytes 786440 | tf_op jit(solution)/shard_map/ppermute | solution.py:287
  60.8 2.5 %stage.12 = (f32[256,512]{1,0:T(8,128)S(1)}, f32[256,512]{1,0:T(8,128)S(1)}) custom-call(s32[2,48]{1,0:T(2,128)S(1)} %get-tuple-element.72.table, bf16[8,16,512]{2,1,0:T(8,128)(2,1)S(1)} %bitcast.24, bf16[32,96,512]{2,1,0:T(8,128)(2,1)S(1)} %get-tuple-element.41.p_ref, s32[8,8,512]{2,1,0:T(8,128)S(1)} %get-tuple-element.42.q_ref), custom_call_target="tpu_custom_call" | custom-call | flops 3400000000 | bytes 500000 | tf_op jit(solution)/shard_map/stage/pallas_call | solution.py:186
  63.2 1.9 %collective-permute-start.7 = (f32[256,512]{1,0:T(8,128)S(1)}, f32[256,512]{1,0:T(8,128)S(1)}, u32[]{:S(2)}, u32[]{:S(2)}) collective-permute-start(f32[256,512]{1,0:T(8,128)S(1)} %get-tuple-element.56), channel_id=1, source_target_pairs={{0,32},{32,0},{64,96},{96,64},{128,160},{160,128},{192,224},{224,1... | collective-permute-start | bytes 1572872 | tf_op jit(solution)/shard_map/ppermute | solution.py:285
  65.2 0.0 collective-permute-done.5
  65.2 0.1 slice_add_fusion.8
  65.3 0.0 collective-permute-done.9
  65.3 3.3 %collective-permute-start.12 = (f32[128,512]{1,0:T(8,128)S(1)}, f32[128,512]{1,0:T(8,128)S(1)}, u32[]{:S(2)}, u32[]{:S(2)}) collective-permute-start(f32[128,512]{1,0:T(8,128)S(1)} %add.71), channel_id=1, source_target_pairs={{0,64},{32,736},{64,128},{96,32},{128,192},{160,96},{192,256},{224... | collective-permute-start | bytes 786440 | tf_op jit(solution)/shard_map/ppermute | solution.py:287
  68.6 0.0 collective-permute-done.4
  68.6 3.6 %collective-permute-start.6 = (f32[128,512]{1,0:T(8,128)S(1)}, f32[128,512]{1,0:T(8,128)S(1)}, u32[]{:S(2)}, u32[]{:S(2)}) collective-permute-start(f32[128,512]{1,0:T(8,128)S(1)} %add.67), channel_id=1, source_target_pairs={{0,64},{32,736},{64,128},{96,32},{128,192},{160,96},{192,256},{224... | collective-permute-start | bytes 786440 | tf_op jit(solution)/shard_map/ppermute | solution.py:287
  72.3 2.2 %stage.13 = (f32[256,512]{1,0:T(8,128)S(1)}, f32[256,512]{1,0:T(8,128)S(1)}) custom-call(s32[2,48]{1,0:T(2,128)S(1)} %get-tuple-element.72.table, bf16[8,16,512]{2,1,0:T(8,128)(2,1)S(1)} %bitcast.25, bf16[32,96,512]{2,1,0:T(8,128)(2,1)S(1)} %get-tuple-element.41.p_ref, s32[8,8,512]{2,1,0:T(8,128)S(1)} %get-tuple-element.42.q_ref), custom_call_target="tpu_custom_call" | custom-call | flops 3400000000 | bytes 500000 | tf_op jit(solution)/shard_map/stage/pallas_call | solution.py:186
  74.5 1.9 %collective-permute-start.10 = (f32[256,512]{1,0:T(8,128)S(1)}, f32[256,512]{1,0:T(8,128)S(1)}, u32[]{:S(2)}, u32[]{:S(2)}) collective-permute-start(f32[256,512]{1,0:T(8,128)S(1)} %get-tuple-element.62), channel_id=1, source_target_pairs={{0,32},{32,0},{64,96},{96,64},{128,160},{160,128},{192,224},{224,1... | collective-permute-start | bytes 1572872 | tf_op jit(solution)/shard_map/ppermute | solution.py:285
  76.4 0.0 collective-permute-done.7
  76.4 0.1 slice_add_fusion.6
  76.5 0.0 collective-permute-done.12
  76.6 1.9 %stage.14 = (f32[256,512]{1,0:T(8,128)S(1)}, f32[256,512]{1,0:T(8,128)S(1)}) custom-call(s32[2,48]{1,0:T(2,128)S(1)} %get-tuple-element.72.table, bf16[8,16,512]{2,1,0:T(8,128)(2,1)S(1)} %bitcast.26, bf16[32,96,512]{2,1,0:T(8,128)(2,1)S(1)} %get-tuple-element.41.p_ref, s32[8,8,512]{2,1,0:T(8,128)S(1)} %get-tuple-element.42.q_ref), custom_call_target="tpu_custom_call" | custom-call | flops 3400000000 | bytes 500000 | tf_op jit(solution)/shard_map/stage/pallas_call | solution.py:186
  78.4 2.4 %collective-permute-start.13 = (f32[256,512]{1,0:T(8,128)S(1)}, f32[256,512]{1,0:T(8,128)S(1)}, u32[]{:S(2)}, u32[]{:S(2)}) collective-permute-start(f32[256,512]{1,0:T(8,128)S(1)} %get-tuple-element.68), channel_id=1, source_target_pairs={{0,32},{32,0},{64,96},{96,64},{128,160},{160,128},{192,224},{224,1... | collective-permute-start | bytes 1572872 | tf_op jit(solution)/shard_map/ppermute | solution.py:285
  80.9 2.9 %collective-permute-start.15 = (f32[128,512]{1,0:T(8,128)S(1)}, f32[128,512]{1,0:T(8,128)S(1)}, u32[]{:S(2)}, u32[]{:S(2)}) collective-permute-start(f32[128,512]{1,0:T(8,128)S(1)} %add.75), channel_id=1, source_target_pairs={{0,64},{32,736},{64,128},{96,32},{128,192},{160,96},{192,256},{224... | collective-permute-start | bytes 786440 | tf_op jit(solution)/shard_map/ppermute | solution.py:287
  83.8 0.0 collective-permute-done.6
  83.9 2.5 %collective-permute-start.8 = (f32[128,512]{1,0:T(8,128)S(1)}, f32[128,512]{1,0:T(8,128)S(1)}, u32[]{:S(2)}, u32[]{:S(2)}) collective-permute-start(f32[128,512]{1,0:T(8,128)S(1)} %add.70), channel_id=1, source_target_pairs={{0,64},{32,736},{64,128},{96,32},{128,192},{160,96},{192,256},{224... | collective-permute-start | bytes 786440 | tf_op jit(solution)/shard_map/ppermute | solution.py:287
  86.4 0.0 collective-permute-done.10
  86.4 0.1 slice_add_fusion.4
  86.5 1.8 %collective-permute-done.15 = f32[128,512]{1,0:T(8,128)S(1)} collective-permute-done((f32[128,512]{1,0:T(8,128)S(1)}, f32[128,512]{1,0:T(8,128)S(1)}, u32[]{:S(2)}, u32[]{:S(2)}) %collective-permute-start.15) | collective-permute-done | bytes 262176 | tf_op jit(solution)/shard_map/ppermute | solution.py:287
  88.3 3.9 %collective-permute-start.16 = (f32[128,512]{1,0:T(8,128)S(1)}, f32[128,512]{1,0:T(8,128)S(1)}, u32[]{:S(2)}, u32[]{:S(2)}) collective-permute-start(f32[128,512]{1,0:T(8,128)S(1)} %add.79), channel_id=1, source_target_pairs={{0,64},{32,736},{64,128},{96,32},{128,192},{160,96},{192,256},{224... | collective-permute-start | bytes 786440 | tf_op jit(solution)/shard_map/ppermute | solution.py:287
  92.2 0.0 collective-permute-done.8
  92.2 2.7 %collective-permute-start.11 = (f32[128,512]{1,0:T(8,128)S(1)}, f32[128,512]{1,0:T(8,128)S(1)}, u32[]{:S(2)}, u32[]{:S(2)}) collective-permute-start(f32[128,512]{1,0:T(8,128)S(1)} %add.74), channel_id=1, source_target_pairs={{0,64},{32,736},{64,128},{96,32},{128,192},{160,96},{192,256},{224... | collective-permute-start | bytes 786440 | tf_op jit(solution)/shard_map/ppermute | solution.py:287
  95.0 0.0 collective-permute-done.13
  95.0 0.1 slice_add_fusion.2
  95.1 0.4 collective-permute-done.16
  95.5 5.0 %collective-permute-start.17 = (f32[128,512]{1,0:T(8,128)S(1)}, f32[128,512]{1,0:T(8,128)S(1)}, u32[]{:S(2)}, u32[]{:S(2)}) collective-permute-start(f32[128,512]{1,0:T(8,128)S(1)} %add.81), channel_id=1, source_target_pairs={{0,64},{32,736},{64,128},{96,32},{128,192},{160,96},{192,256},{224... | collective-permute-start | bytes 786440 | tf_op jit(solution)/shard_map/ppermute | solution.py:289
  100.5 1.5 %stage.15 = f32[256,512]{1,0:T(8,128)S(1)} custom-call(s32[2,48]{1,0:T(2,128)S(1)} %get-tuple-element.72.table, bf16[8,16,512]{2,1,0:T(8,128)(2,1)S(1)} %bitcast.27, bf16[32,96,512]{2,1,0:T(8,128)(2,1)S(1)} %get-tuple-element.41.p_ref, s32[8,8,512]{2,1,0:T(8,128)S(1)} %get-tuple-element.42.q_ref), custom_call_target="tpu_custom_call" | custom-call | flops 1700000000 | bytes 500000 | tf_op jit(solution)/shard_map/stage/pallas_call | solution.py:186
  102.1 0.0 collective-permute-done.11
  102.1 1.9 %collective-permute-start.14 = (f32[128,512]{1,0:T(8,128)S(1)}, f32[128,512]{1,0:T(8,128)S(1)}, u32[]{:S(2)}, u32[]{:S(2)}) collective-permute-start(f32[128,512]{1,0:T(8,128)S(1)} %add.78), channel_id=1, source_target_pairs={{0,64},{32,736},{64,128},{96,32},{128,192},{160,96},{192,256},{224... | collective-permute-start | bytes 786440 | tf_op jit(solution)/shard_map/ppermute | solution.py:289
  104.1 7.2 %collective-permute-start.18 = (f32[128,512]{1,0:T(8,128)S(1)}, f32[128,512]{1,0:T(8,128)S(1)}, u32[]{:S(2)}, u32[]{:S(2)}) collective-permute-start(f32[128,512]{1,0:T(8,128)S(1)} %slice_add_fusion), channel_id=1, source_target_pairs={{0,32},{32,0},{64,96},{96,64},{128,160},{160,128},{192,224},{224,1... | collective-permute-start | bytes 786440 | tf_op jit(solution)/shard_map/ppermute | solution.py:291
  111.3 0.0 collective-permute-done.14
  111.4 1.1 collective-permute-done.18
  112.5 0.1 fusion
  112.5 0.9 copy.10
  (14 shorter events, 0.4 us)
Async XLA Ops:
  1.6 22.9 %collective-permute-start.1 = (f32[1,4,8,512]{3,2,1,0:T(8,128)S(1)}, f32[1,4,8,512]{3,2,1,0:T(8,128)S(1)}, u32[]{:S(2)}, u32[]{:S(2)}) collective-permute-start(f32[1,4,8,512]{3,2,1,0:T(8,128)S(1)} %get-tuple-element.83), channel_id=1, source_target_pairs={{0,1},{1,2},{2,3},{3,4},{4,5},{5,6},{6,7},{7,8},{8,9},{9,10},{10,1... | collective-permute-start | bytes 196616 | tf_op jit(solution)/shard_map/ppermute | solution.py:242
  4.8 19.8 %collective-permute-start = (f32[1,4,8,512]{3,2,1,0:T(8,128)S(1)}, f32[1,4,8,512]{3,2,1,0:T(8,128)S(1)}, u32[]{:S(2)}, u32[]{:S(2)}) collective-permute-start(f32[1,4,8,512]{3,2,1,0:T(8,128)S(1)} %get-tuple-element.84), channel_id=1, source_target_pairs={{1,0},{2,1},{3,2},{4,3},{5,4},{6,5},{7,6},{8,7},{9,8},{10,9},{11,1... | collective-permute-start | bytes 196616 | tf_op jit(solution)/shard_map/ppermute | solution.py:241
  13.6 1.2 %copy-start = (s32[8,4,16,512]{3,2,1,0:T(8,128)S(1)}, s32[8,4,16,512]{3,2,1,0:T(8,128)}, u32[]{:S(2)}) copy-start(s32[8,4,16,512]{3,2,1,0:T(8,128)} %param.9) | copy-start | bytes 3145732
  14.9 1.0 copy-start.1
  15.9 8.6 %copy-start.2 = (f32[4,4,8,512]{3,2,1,0:T(8,128)S(1)}, f32[4,4,8,512]{3,2,1,0:T(8,128)}, u32[]{:S(2)}) copy-start(f32[4,4,8,512]{3,2,1,0:T(8,128)} %param.6) | copy-start | bytes 786436
  28.0 25.7 %collective-permute-start.2 = (f32[256,512]{1,0:T(8,128)S(1)}, f32[256,512]{1,0:T(8,128)S(1)}, u32[]{:S(2)}, u32[]{:S(2)}) collective-permute-start(f32[256,512]{1,0:T(8,128)S(1)} %stage.8), channel_id=1, source_target_pairs={{0,32},{32,0},{64,96},{96,64},{128,160},{160,128},{192,224},{224,1... | collective-permute-start | bytes 1572872 | tf_op jit(solution)/shard_map/ppermute | solution.py:275
  34.2 30.9 %collective-permute-start.5 = (f32[256,512]{1,0:T(8,128)S(1)}, f32[256,512]{1,0:T(8,128)S(1)}, u32[]{:S(2)}, u32[]{:S(2)}) collective-permute-start(f32[256,512]{1,0:T(8,128)S(1)} %get-tuple-element.51), channel_id=1, source_target_pairs={{0,32},{32,0},{64,96},{96,64},{128,160},{160,128},{192,224},{224,1... | collective-permute-start | bytes 1572872 | tf_op jit(solution)/shard_map/ppermute | solution.py:285
  36.4 17.3 %collective-permute-start.3 = (f32[72,512]{1,0:T(8,128)S(1)}, f32[72,512]{1,0:T(8,128)S(1)}, u32[]{:S(2)}, u32[]{:S(2)}) collective-permute-start(f32[72,512]{1,0:T(8,128)S(1)} %stage.9), channel_id=1, source_target_pairs={{0,64},{32,736},{64,128},{96,32},{128,192},{160,96},{192,256},{224... | collective-permute-start | bytes 442376 | tf_op jit(solution)/shard_map/ppermute | solution.py:278
  53.8 11.4 %collective-permute-start.9 = (f32[128,512]{1,0:T(8,128)S(1)}, f32[128,512]{1,0:T(8,128)S(1)}, u32[]{:S(2)}, u32[]{:S(2)}) collective-permute-start(f32[128,512]{1,0:T(8,128)S(1)} %get-tuple-element.58), channel_id=1, source_target_pairs={{0,64},{32,736},{64,128},{96,32},{128,192},{160,96},{192,256},{224... | collective-permute-start | bytes 786440 | tf_op jit(solution)/shard_map/ppermute | solution.py:287
  58.8 9.8 %collective-permute-start.4 = (f32[128,512]{1,0:T(8,128)S(1)}, f32[128,512]{1,0:T(8,128)S(1)}, u32[]{:S(2)}, u32[]{:S(2)}) collective-permute-start(f32[128,512]{1,0:T(8,128)S(1)} %get-tuple-element.48), channel_id=1, source_target_pairs={{0,64},{32,736},{64,128},{96,32},{128,192},{160,96},{192,256},{224... | collective-permute-start | bytes 786440 | tf_op jit(solution)/shard_map/ppermute | solution.py:287
  63.2 13.2 %collective-permute-start.7 = (f32[256,512]{1,0:T(8,128)S(1)}, f32[256,512]{1,0:T(8,128)S(1)}, u32[]{:S(2)}, u32[]{:S(2)}) collective-permute-start(f32[256,512]{1,0:T(8,128)S(1)} %get-tuple-element.56), channel_id=1, source_target_pairs={{0,32},{32,0},{64,96},{96,64},{128,160},{160,128},{192,224},{224,1... | collective-permute-start | bytes 1572872 | tf_op jit(solution)/shard_map/ppermute | solution.py:285
  65.3 11.2 %collective-permute-start.12 = (f32[128,512]{1,0:T(8,128)S(1)}, f32[128,512]{1,0:T(8,128)S(1)}, u32[]{:S(2)}, u32[]{:S(2)}) collective-permute-start(f32[128,512]{1,0:T(8,128)S(1)} %add.71), channel_id=1, source_target_pairs={{0,64},{32,736},{64,128},{96,32},{128,192},{160,96},{192,256},{224... | collective-permute-start | bytes 786440 | tf_op jit(solution)/shard_map/ppermute | solution.py:287
  68.6 15.2 %collective-permute-start.6 = (f32[128,512]{1,0:T(8,128)S(1)}, f32[128,512]{1,0:T(8,128)S(1)}, u32[]{:S(2)}, u32[]{:S(2)}) collective-permute-start(f32[128,512]{1,0:T(8,128)S(1)} %add.67), channel_id=1, source_target_pairs={{0,64},{32,736},{64,128},{96,32},{128,192},{160,96},{192,256},{224... | collective-permute-start | bytes 786440 | tf_op jit(solution)/shard_map/ppermute | solution.py:287
  74.5 11.9 %collective-permute-start.10 = (f32[256,512]{1,0:T(8,128)S(1)}, f32[256,512]{1,0:T(8,128)S(1)}, u32[]{:S(2)}, u32[]{:S(2)}) collective-permute-start(f32[256,512]{1,0:T(8,128)S(1)} %get-tuple-element.62), channel_id=1, source_target_pairs={{0,32},{32,0},{64,96},{96,64},{128,160},{160,128},{192,224},{224,1... | collective-permute-start | bytes 1572872 | tf_op jit(solution)/shard_map/ppermute | solution.py:285
  78.4 16.5 %collective-permute-start.13 = (f32[256,512]{1,0:T(8,128)S(1)}, f32[256,512]{1,0:T(8,128)S(1)}, u32[]{:S(2)}, u32[]{:S(2)}) collective-permute-start(f32[256,512]{1,0:T(8,128)S(1)} %get-tuple-element.68), channel_id=1, source_target_pairs={{0,32},{32,0},{64,96},{96,64},{128,160},{160,128},{192,224},{224,1... | collective-permute-start | bytes 1572872 | tf_op jit(solution)/shard_map/ppermute | solution.py:285
  80.9 7.4 %collective-permute-start.15 = (f32[128,512]{1,0:T(8,128)S(1)}, f32[128,512]{1,0:T(8,128)S(1)}, u32[]{:S(2)}, u32[]{:S(2)}) collective-permute-start(f32[128,512]{1,0:T(8,128)S(1)} %add.75), channel_id=1, source_target_pairs={{0,64},{32,736},{64,128},{96,32},{128,192},{160,96},{192,256},{224... | collective-permute-start | bytes 786440 | tf_op jit(solution)/shard_map/ppermute | solution.py:287
  83.9 8.3 %collective-permute-start.8 = (f32[128,512]{1,0:T(8,128)S(1)}, f32[128,512]{1,0:T(8,128)S(1)}, u32[]{:S(2)}, u32[]{:S(2)}) collective-permute-start(f32[128,512]{1,0:T(8,128)S(1)} %add.70), channel_id=1, source_target_pairs={{0,64},{32,736},{64,128},{96,32},{128,192},{160,96},{192,256},{224... | collective-permute-start | bytes 786440 | tf_op jit(solution)/shard_map/ppermute | solution.py:287
  88.3 7.2 %collective-permute-start.16 = (f32[128,512]{1,0:T(8,128)S(1)}, f32[128,512]{1,0:T(8,128)S(1)}, u32[]{:S(2)}, u32[]{:S(2)}) collective-permute-start(f32[128,512]{1,0:T(8,128)S(1)} %add.79), channel_id=1, source_target_pairs={{0,64},{32,736},{64,128},{96,32},{128,192},{160,96},{192,256},{224... | collective-permute-start | bytes 786440 | tf_op jit(solution)/shard_map/ppermute | solution.py:287
  92.2 9.8 %collective-permute-start.11 = (f32[128,512]{1,0:T(8,128)S(1)}, f32[128,512]{1,0:T(8,128)S(1)}, u32[]{:S(2)}, u32[]{:S(2)}) collective-permute-start(f32[128,512]{1,0:T(8,128)S(1)} %add.74), channel_id=1, source_target_pairs={{0,64},{32,736},{64,128},{96,32},{128,192},{160,96},{192,256},{224... | collective-permute-start | bytes 786440 | tf_op jit(solution)/shard_map/ppermute | solution.py:287
  95.5 8.5 %collective-permute-start.17 = (f32[128,512]{1,0:T(8,128)S(1)}, f32[128,512]{1,0:T(8,128)S(1)}, u32[]{:S(2)}, u32[]{:S(2)}) collective-permute-start(f32[128,512]{1,0:T(8,128)S(1)} %add.81), channel_id=1, source_target_pairs={{0,64},{32,736},{64,128},{96,32},{128,192},{160,96},{192,256},{224... | collective-permute-start | bytes 786440 | tf_op jit(solution)/shard_map/ppermute | solution.py:289
  102.1 9.2 %collective-permute-start.14 = (f32[128,512]{1,0:T(8,128)S(1)}, f32[128,512]{1,0:T(8,128)S(1)}, u32[]{:S(2)}, u32[]{:S(2)}) collective-permute-start(f32[128,512]{1,0:T(8,128)S(1)} %add.78), channel_id=1, source_target_pairs={{0,64},{32,736},{64,128},{96,32},{128,192},{160,96},{192,256},{224... | collective-permute-start | bytes 786440 | tf_op jit(solution)/shard_map/ppermute | solution.py:289
  104.1 8.4 %collective-permute-start.18 = (f32[128,512]{1,0:T(8,128)S(1)}, f32[128,512]{1,0:T(8,128)S(1)}, u32[]{:S(2)}, u32[]{:S(2)}) collective-permute-start(f32[128,512]{1,0:T(8,128)S(1)} %slice_add_fusion), channel_id=1, source_target_pairs={{0,32},{32,0},{64,96},{96,64},{128,160},{160,128},{192,224},{224,1... | collective-permute-start | bytes 786440 | tf_op jit(solution)/shard_map/ppermute | solution.py:291

commit v2 on v1

v2 whole, which is shorter than its diff:
```python
import functools

import jax
import jax.numpy as jnp
from jax import lax
from jax.experimental import pallas as pl
from jax.experimental.pallas import tpu as pltpu
from jax.sharding import PartitionSpec as P

WIN = 32
SPAN = 96
LANES = 128
CAP = 2
MIB = 1024 * 1024


def stage_sizes(far):
    return [2 * CAP] + [4 * CAP] * (far - 1) + [2 * CAP]


def fill_table(chips, owner_ref, slot_ref, table, count):
    deps, blk = owner_ref.shape
    far = chips // 2
    tile = lax.axis_index("tile")
    chip, core = lax.div(tile, 2), lax.rem(tile, 2)
    ahead = 1 - 2 * core
    entries = sum(stage_sizes(far))

    def clear(n, _):
        table[0, n] = jnp.int32(-1)
        table[1, n] = jnp.int32(0)
        return 0

    lax.fori_loop(0, entries, clear, 0)

    def reset(n, _):
        count[n] = jnp.int32(0)
        return 0

    lax.fori_loop(0, 2 * chips, reset, 0)

    def enter(n, _):
        row, k = lax.div(n, deps), lax.rem(n, deps)
        owner = owner_ref[k, row]
        turn = count[owner]
        count[owner] = turn + 1
        away = lax.rem(ahead * (lax.div(owner, 2) - chip) + chips, chips)
        back = away > far
        distance = jnp.where(back, chips - away, away)
        own = (lax.rem(owner, 2) == core).astype(jnp.int32)
        half = jnp.where(back, 1 - own, own)
        start = jnp.where(
            away == 0,
            entries - 2 * CAP,
            jnp.where(away == far, 0, 2 * CAP + (far - 1 - distance) * 4 * CAP + jnp.where(back, 2 * CAP, 0)),
        )
        at = start + half * CAP + turn
        table[0, at] = n
        table[1, at] = slot_ref[k, row]
        return 0

    lax.fori_loop(0, blk * deps, enter, 0)


def place_kernel(chips, deps, owner_ref, slot_ref, w_hbm, cols_hbm, p_ref, q_ref, table, w_sc, cols_sc, x_sc, count, sems):
    items, points, cols = cols_hbm.shape

    def fetches(a):
        part = pl.ds(a * deps, deps)
        return (
            pltpu.make_async_copy(w_hbm.at[part], w_sc.at[part], sems.at[0, a]),
            pltpu.make_async_copy(cols_hbm.at[part], cols_sc.at[part], sems.at[1, a]),
        )

    for a in range(items // deps):
        for fetch in fetches(a):
            fetch.start()
    fill_table(chips, owner_ref, slot_ref, table, count)
    q_ref[...] = jnp.zeros_like(q_ref)
    place = lax.broadcasted_iota(jnp.int32, (SPAN, LANES), 0).astype(jnp.float32).astype(jnp.bfloat16)

    def block(a, _):
        for fetch in fetches(a):
            fetch.wait()
        for k in range(deps):
            item = a * deps + k
            d = cols_sc[item]
            rel = ((d - d[0:1] + cols // 2) & (cols - 1)) - cols // 2
            low = jnp.min(rel, axis=0, keepdims=True)
            base = (d[0:1] + low) & (cols - 1)
            x_sc[k] = (rel - low + (base & (WIN - 1))).astype(jnp.float32).astype(jnp.bfloat16)
            q_ref[a, k:k + 1, :] = base // WIN
            for t in range(cols // LANES):
                part = slice(t * LANES, (t + 1) * LANES)
                x, w = x_sc[k, :, part], w_sc[item, :, part]
                acc = jnp.zeros((SPAN, LANES), jnp.bfloat16)
                for s in range(points):
                    acc = jnp.where(place == x[s:s + 1], w[s:s + 1], acc)
                p_ref[item, :, part] = acc
        return 0

    lax.fori_loop(0, items // deps, block, 0)


def placed(chips, dep_owner, dep_slot, weight, places):
    blk, deps = dep_owner.shape
    items, points, cols = weight.shape
    entries = sum(stage_sizes(chips // 2))
    smem = pl.BlockSpec(memory_space=pltpu.SMEM)
    vmem = pl.BlockSpec(memory_space=pltpu.VMEM)
    hbm = pl.BlockSpec(memory_space=pltpu.HBM)
    return pl.pallas_call(
        functools.partial(place_kernel, chips, deps),
        in_specs=[smem, smem, hbm, hbm],
        out_specs=[vmem, vmem, smem],
        out_shape=[
            jax.ShapeDtypeStruct((items, SPAN, cols), jnp.bfloat16),
            jax.ShapeDtypeStruct((blk, 8, cols), jnp.int32),
            jax.ShapeDtypeStruct((2, entries), jnp.int32),
        ],
        scratch_shapes=[
            pltpu.VMEM((items, points, cols), jnp.bfloat16),
            pltpu.VMEM((items, points, cols), jnp.int32),
            pltpu.VMEM((deps, points, cols), jnp.bfloat16),
            pltpu.SMEM((2 * chips,), jnp.int32),
            pltpu.SemaphoreType.DMA((2, blk)),
        ],
        compiler_params=pltpu.CompilerParams(vmem_limit_bytes=8 * MIB),
        cost_estimate=pl.CostEstimate(flops=10000000000, bytes_accessed=5000000, transcendentals=0),
        name="place",
    )(dep_owner.T, dep_slot.T, weight, places)


def item_contribution(v, q, p_ref, index, v_sc, p_sc):
    rows, cols = v.shape
    for i in range(cols // WIN):
        v_sc[i * rows:(i + 1) * rows, :] = jnp.where(q == i, v, 0.0).astype(jnp.bfloat16)
    p_sc[0:SPAN, :] = p_ref[index]
    u = lax.dot_general(
        v_sc[...], p_sc[...], (((1,), (1,)), ((), ())), preferred_element_type=jnp.float32
    )
    lane = lax.broadcasted_iota(jnp.int32, (rows, LANES), 1)
    kept, passed = [], []
    for t in range(cols // LANES):
        u0, u1, u2, u3 = (u[(4 * t + j) * rows:(4 * t + j + 1) * rows] for j in range(4))
        kept.append(u0 + pltpu.roll(u1, WIN, 1))
        passed.append(pltpu.roll(u2, 2 * WIN, 1) + pltpu.roll(u3, 3 * WIN, 1))
    return [
        kept[t] + jnp.where(lane >= LANES // 2, passed[t], passed[t - 1]) for t in range(len(kept))
    ]


def stage_kernel(groups, deps, rows, table, v_ref, p_ref, q_ref, *rest):
    outs, (v_sc, p_sc) = rest[:-2], rest[-2:]
    cols = v_ref.shape[-1]
    blk = v_ref.shape[0]
    p_sc[SPAN:, :] = jnp.zeros((LANES - SPAN, cols), jnp.bfloat16)
    for (first, listed), out in zip(groups, outs):
        out[...] = jnp.zeros_like(out)
        if listed:
            ids = lax.broadcasted_iota(jnp.int32, (8, cols), 0)
            slots = jnp.zeros((8, cols), jnp.int32)
            for n in range(2 * CAP):
                slots = jnp.where(ids == n, table[1, first + n], slots)
            out[2 * CAP * rows:, :] = slots.astype(jnp.float32)

        def one(n, _):
            index = table[0, first + n]

            @pl.when(index >= 0)
            def _():
                row = lax.div(index, deps)
                v = v_ref[row].astype(jnp.float32)
                q = q_ref[row, pl.ds(lax.rem(index, deps), 1), :]
                parts = item_contribution(v, q, p_ref, index, v_sc, p_sc)
                if listed:
                    at = n * rows
                else:
                    at = (lax.div(n, CAP) * blk + table[1, first + n]) * rows
                at = pl.multiple_of(at, rows)
                for t, part in enumerate(parts):
                    where = (pl.ds(at, rows), slice(t * LANES, (t + 1) * LANES))
                    out[where] = out[where] + part

            return 0

        lax.fori_loop(0, 2 * CAP, one, 0)


def stage(groups, deps, table, v, p, q):
    blk, rows, cols = v.shape
    heights = [2 * CAP * rows + 8 if listed else 2 * blk * rows for _, listed in groups]
    vmem = pl.BlockSpec(memory_space=pltpu.VMEM)
    return pl.pallas_call(
        functools.partial(stage_kernel, groups, deps, rows),
        in_specs=[pl.BlockSpec(memory_space=pltpu.SMEM), vmem, vmem, vmem],
        out_specs=[vmem] * len(groups),
        out_shape=[jax.ShapeDtypeStruct((height, cols), jnp.float32) for height in heights],
        scratch_shapes=[
            pltpu.VMEM((cols // WIN * rows, cols), jnp.bfloat16),
            pltpu.VMEM((LANES, cols), jnp.bfloat16),
        ],
        compiler_params=pltpu.CompilerParams(vmem_limit_bytes=10 * MIB),
        cost_estimate=pl.CostEstimate(
            flops=len(groups) * 1700000000, bytes_accessed=500000, transcendentals=0
        ),
        name="stage",
    )(table, v, p, q)


def merge_kernel(blk, rows, dense_ref, *refs):
    lists, outs = refs[:-2], refs[-2:]
    width = dense_ref.shape[1]
    for half, out in enumerate(outs):
        for c in range(0, width, LANES):
            part = slice(c, c + LANES)
            items = []
            for ref in lists:
                for n in range(half * CAP, half * CAP + CAP):
                    at = 2 * CAP * rows + n
                    items.append((ref[at:at + 1, part], ref[n * rows:(n + 1) * rows, part]))
            for b in range(blk):
                at = (half * blk + b) * rows
                total = dense_ref[at:at + rows, part]
                for slot, value in items:
                    total = total + jnp.where(slot == float(b), value, 0.0)
                out[b * rows:(b + 1) * rows, part] = total


def merge(blk, rows, dense, *lists):
    width = dense.shape[1]
    return list(pl.pallas_call(
        functools.partial(merge_kernel, blk, rows),
        out_shape=[jax.ShapeDtypeStruct((blk * rows, width), jnp.float32)] * 2,
        compiler_params=pltpu.CompilerParams(vmem_limit_bytes=6 * MIB),
        cost_estimate=pl.CostEstimate(flops=1000000, bytes_accessed=1000000, transcendentals=0),
        name="merge",
    )(dense, *lists))


def edges_kernel(adj0_ref, coef0_ref, adj1_ref, coef1_ref, first_ref, last_ref):
    first_ref[0] = coef0_ref[0] * adj0_ref[0]
    last_ref[0] = coef1_ref[0] * adj1_ref[0]


def edges(adj, coef):
    lev, fields, blk, cols = adj.shape
    shape = (1, fields, blk, cols)
    return pl.pallas_call(
        edges_kernel,
        grid=(1,),
        in_specs=[
            pl.BlockSpec(shape, lambda i: (0, 0, 0, 0)),
            pl.BlockSpec((1, 1, blk, cols), lambda i: (0, 0, 0, 0)),
            pl.BlockSpec(shape, lambda i: (lev - 1, 0, 0, 0)),
            pl.BlockSpec((1, 1, blk, cols), lambda i: (2, lev - 1, 0, 0)),
        ],
        out_specs=[pl.BlockSpec(shape, lambda i: (0, 0, 0, 0))] * 2,
        out_shape=[jax.ShapeDtypeStruct(shape, jnp.float32)] * 2,
        compiler_params=pltpu.CompilerParams(vmem_limit_bytes=60 * MIB),
        name="edges",
    )(adj, coef, adj, coef)


def vertical_kernel(adj_ref, coef_ref, after_ref, before_ref, v_ref):
    lev, fields, blk, cols = adj_ref.shape
    for c in range(0, cols, LANES):
        part = slice(c, c + LANES)
        levels = []
        for m in range(lev):
            low = after_ref[0, :, :, part] if m == lev - 1 else coef_ref[0, m + 1, :, part] * adj_ref[m + 1, :, :, part]
            high = before_ref[0, :, :, part] if m == 0 else coef_ref[2, m - 1, :, part] * adj_ref[m - 1, :, :, part]
            levels.append(low + coef_ref[1, m, :, part] * adj_ref[m, :, :, part] + high)
        whole = jnp.concatenate(levels, 0)
        v_ref[:, :, part] = jnp.swapaxes(whole, 0, 1).astype(jnp.bfloat16)


def vertical(adj, coef, after, before):
    lev, fields, blk, cols = adj.shape
    return pl.pallas_call(
        vertical_kernel,
        out_shape=jax.ShapeDtypeStruct((blk, lev * fields, cols), jnp.bfloat16),
        compiler_params=pltpu.CompilerParams(vmem_limit_bytes=4 * MIB),
        cost_estimate=pl.CostEstimate(flops=1000000, bytes_accessed=1000000, transcendentals=0),
        name="vertical",
    )(adj, coef, after, before)


def shards(adj_arrival, vert_coef, stencil_weight, stencil_cols, dep_owner, dep_slot):
    lev_dev, fields, blk, cols = adj_arrival.shape
    tiles, levels = lax.axis_size("tile"), lax.axis_size("lev")
    deps, points = stencil_weight.shape[1:3]
    items, rows = blk * deps, lev_dev * fields
    chips = tiles // 2
    far = chips // 2

    first, last = edges(adj_arrival, vert_coef)
    after = lax.ppermute(first, "lev", [(i + 1, i) for i in range(levels - 1)])
    before = lax.ppermute(last, "lev", [(i, i + 1) for i in range(levels - 1)])

    p, q, table = placed(
        chips,
        dep_owner,
        dep_slot,
        stencil_weight.reshape(items, points, cols),
        stencil_cols.reshape(items, points, cols),
    )

    v = vertical(adj_arrival, vert_coef, after, before)

    sibling = [(t, t ^ 1) for t in range(tiles)]
    ring = [(t, (t + 2 * (1 - 2 * (t % 2))) % tiles) for t in range(tiles)]
    quad = 2 * CAP

    def made(table, *groups):
        return stage(groups, deps, table, v, p, q)

    def behind(table, value):
        return lax.optimization_barrier((table, value))

    def onward(values, pairs):
        return [lax.ppermute(value, "tile", pairs) for value in values]

    own, others = made(table, (quad, True), (2 * quad, True))
    given = lax.ppermute(others, "tile", sibling)
    table, given = behind(table, given)
    arrived = onward([own, given], ring)
    opposite = None
    for h in range(far - 2, 0, -1):
        at = quad + (far - 1 - h) * 2 * quad
        own, others = made(table, (at, False), (at + quad, True))
        given = lax.ppermute(others, "tile", sibling)
        if h == far - 2:
            totals = merge(blk, rows, own, given, *arrived)
        else:
            totals = [total + mine for total, mine in zip(sums, lax.optimization_barrier(merge(blk, rows, own, given)))]
        table, totals[0] = behind(table, totals[0])
        if h == far - 3:
            (listed,) = made(table, (0, True))
            opposite = lax.ppermute(listed, "tile", [(t, (t + tiles // 2) % tiles) for t in range(tiles)])
        sums = onward(totals, ring)
    (here,) = made(table, (quad + (far - 1) * 2 * quad, False))
    here = lax.optimization_barrier(merge(blk, rows, here, opposite))
    swapped = lax.ppermute(sums[0] + here[0], "tile", sibling)
    result = sums[1] + here[1] + swapped
    result = jnp.transpose(result.reshape(blk, rows, cols), (1, 0, 2))
    return result.reshape(lev_dev, fields, blk, cols)


def solution(mesh):
    in_specs = (
        P("lev", None, "tile", None),
        P(None, "lev", "tile", None),
        P("tile", None, None, None),
        P("tile", None, None, None),
        P("tile", None),
        P("tile", None),
    )
    out_specs = P("lev", None, "tile", None)
    return jax.shard_map(shards, mesh=mesh, in_specs=in_specs, out_specs=out_specs, check_vma=False)
```

time: 114 us -> 116 us (1.018)
  the two profiles are of different devices: /device:TPU:33 before, /device:TPU:31 now
where the time goes in v2:
time: 116 us; the launch traced here: 115 us
  starting transfers between devices  71.4 us (62%)
  Pallas kernels  25.9 us (22%)
  waiting for transfers between devices  12.8 us (11%)
  local copies, waits for them, and re-layouts  4.49 us (4%)
    ppermute x10, starting transfers between devices, onward(): return [lax.ppermute(value, 'tile', pairs) for value in values]  45.1 us
    pallas_call x7, Pallas kernels, stage(): pl.pallas_call(functools.partial(stage_kernel, groups, deps, rows), in_sp...  14 us
    ppermute x5, starting transfers between devices, shards(): given = lax.ppermute(others, 'tile', sibling)  11.5 us
    pallas_call x1, Pallas kernels, placed(): pl.pallas_call(functools.partial(place_kernel, chips, deps), in_specs=[sm...  9.59 us
    ppermute x1, waiting for transfers between devices, shards(): lax.ppermute(listed, 'tile', [(t, (t + tiles // 2) % tiles) for t in rang...  8.81 us
    ppermute x1, starting transfers between devices, shards(): before = lax.ppermute(last, 'lev', [(i, i + 1) for i in range(levels - 1)])  6.15 us
    ppermute x1, starting transfers between devices, shards(): lax.ppermute(listed, 'tile', [(t, (t + tiles // 2) % tiles) for t in rang...  4.01 us
    unnamed x12, local copies, waits for them, and re-layouts  3.63 us
  transfers between devices with their start and end apart: 19, of which 3 were waited for; matrix products, arithmetic and copies ran while one was open for 0% of the time, Pallas kernels for 19%

profile of v2, /device:TPU:31, one launch (start us, length us, event | category | flops | bytes accessed | tf_op | source)
XLA Modules:
  0.0 115.3 jit_solution(11292296931407164114)
XLA Ops:
  0.0 1.5 %edges.1 = (f32[1,4,8,512]{3,2,1,0:T(8,128)}, f32[1,4,8,512]{3,2,1,0:T(8,128)}) custom-call(f32[4,4,8,512]{3,2,1,0:T(8,128)} %adj_ref.1, f32[3,4,8,512]{3,2,1,0:T(8,128)} %coef_ref.1, f32[4,4,8,512]{3,2,1,0:T(8,128)} %adj_ref.1, f32[3,4,8,512]{3,2,1,0:T(8,128)} %coef_ref.1), custom_call_target="tpu_custom_call" | custom-call | tf_op jit(solution)/shard_map/edges/pallas_call | solution.py:249
  1.6 2.4 %collective-permute-start = (f32[1,4,8,512]{3,2,1,0:T(8,128)}, f32[1,4,8,512]{3,2,1,0:T(8,128)S(1)}, u32[]{:S(2)}, u32[]{:S(2)}) collective-permute-start(f32[1,4,8,512]{3,2,1,0:T(8,128)} %get-tuple-element.41), channel_id=1, source_target_pairs={{1,0},{2,1},{3,2},{4,3},{5,4},{6,5},{7,6},{8,7},{9,8},{10,9},{11,1... | collective-permute-start | bytes 196616 | tf_op jit(solution)/shard_map/ppermute | solution.py:298
  4.0 6.1 %collective-permute-start.1 = (f32[1,4,8,512]{3,2,1,0:T(8,128)}, f32[1,4,8,512]{3,2,1,0:T(8,128)S(1)}, u32[]{:S(2)}, u32[]{:S(2)}) collective-permute-start(f32[1,4,8,512]{3,2,1,0:T(8,128)} %get-tuple-element.42), channel_id=1, source_target_pairs={{0,1},{1,2},{2,3},{3,4},{4,5},{5,6},{6,7},{7,8},{8,9},{9,10},{10,1... | collective-permute-start | bytes 196616 | tf_op jit(solution)/shard_map/ppermute | solution.py:299
  10.2 0.0 copy-start.2
  10.2 1.2 %copy-done.2 = s32[8,4,16,512]{3,2,1,0:T(8,128)S(1)} copy-done((s32[8,4,16,512]{3,2,1,0:T(8,128)S(1)}, s32[8,4,16,512]{3,2,1,0:T(8,128)}, u32[]{:S(2)}) %copy-start.2) | copy-done | bytes 1048600
  11.4 0.0 copy-start.3
  11.4 1.0 copy-done.3
  12.4 0.0 copy-start.4
  12.4 0.7 copy-done.4
  13.1 0.7 copy-done.5
  13.8 9.6 %place.1 = (bf16[32,96,512]{2,1,0:T(8,128)(2,1)S(1)}, s32[8,8,512]{2,1,0:T(8,128)S(1)}, s32[2,48]{1,0:T(2,128)S(1)}) custom-call(s32[4,8]{1,0:T(4,128)S(1)} %bitcast.10, s32[4,8]{1,0:T(4,128)S(1)} %bitcast.11, bf16[32,16,512]{2,1,0:T(8,128)(2,1)S(1)} %bitcast.9, s32[32,16,512]{2,1,0:T(8,128)S(1)} %bitcast.8), custom_call_target="tpu_custom_call" | custom-call | flops 10000000000 | bytes 5000000 | tf_op jit(solution)/shard_map/place/pallas_call | solution.py:112
  23.4 0.0 collective-permute-done.after_ref
  23.4 0.0 collective-permute-done.1.before_ref
  23.4 0.0 copy-done
  23.4 0.0 copy-done.1
  23.4 0.1 vertical.1.v_ref
  23.6 2.4 %stage.7 = (f32[72,512]{1,0:T(8,128)S(1)}, f32[72,512]{1,0:T(8,128)S(1)}) custom-call(s32[2,48]{1,0:T(2,128)S(1)} %get-tuple-element.71.table, bf16[8,16,512]{2,1,0:T(8,128)(2,1)S(1)} %vertical.1.v_ref, bf16[32,96,512]{2,1,0:T(8,128)(2,1)S(1)} %get-tuple-element.43.p_ref, s32[8,8,512]{2,1,0:T(8,128)S(1)} %get-tuple-element.44.q_ref), custom_call_target="tpu_custom_call" | custom-call | flops 3400000000 | bytes 500000 | tf_op jit(solution)/shard_map/stage/pallas_call | solution.py:194
  26.0 3.1 %collective-permute-start.2 = (f32[72,512]{1,0:T(8,128)S(1)}, f32[72,512]{1,0:T(8,128)S(1)}, u32[]{:S(2)}, u32[]{:S(2)}) collective-permute-start(f32[72,512]{1,0:T(8,128)S(1)} %get-tuple-element.45), channel_id=1, source_target_pairs={{0,32},{32,0},{64,96},{96,64},{128,160},{160,128},{192,224},{224,1... | collective-permute-start | bytes 442376 | tf_op jit(solution)/shard_map/ppermute | solution.py:325
  29.1 14.0 %collective-permute-start.4 = (f32[72,512]{1,0:T(8,128)S(1)}, f32[72,512]{1,0:T(8,128)S(1)}, u32[]{:S(2)}, u32[]{:S(2)}) collective-permute-start(f32[72,512]{1,0:T(8,128)S(1)} %get-tuple-element.49), channel_id=1, source_target_pairs={{0,64},{32,736},{64,128},{96,32},{128,192},{160,96},{192,256},{224... | collective-permute-start | bytes 442376 | tf_op jit(solution)/shard_map/ppermute | solution.py:322
  43.1 0.0 collective-permute-done.2
  43.2 1.9 %stage.8 = (f32[256,512]{1,0:T(8,128)S(1)}, f32[72,512]{1,0:T(8,128)S(1)}) custom-call(s32[2,48]{1,0:T(2,128)S(1)} %get-tuple-element.71.table, bf16[8,16,512]{2,1,0:T(8,128)(2,1)S(1)} %vertical.1.v_ref, bf16[32,96,512]{2,1,0:T(8,128)(2,1)S(1)} %get-tuple-element.43.p_ref, s32[8,8,512]{2,1,0:T(8,128)S(1)} %get-tuple-element.44.q_ref), custom_call_target="tpu_custom_call" | custom-call | flops 3400000000 | bytes 500000 | tf_op jit(solution)/shard_map/stage/pallas_call | solution.py:194
  45.0 1.9 %collective-permute-start.3 = (f32[72,512]{1,0:T(8,128)S(1)}, f32[72,512]{1,0:T(8,128)S(1)}, u32[]{:S(2)}, u32[]{:S(2)}) collective-permute-start(f32[72,512]{1,0:T(8,128)S(1)} %get-tuple-element.48), channel_id=1, source_target_pairs={{0,32},{32,0},{64,96},{96,64},{128,160},{160,128},{192,224},{224,1... | collective-permute-start | bytes 442376 | tf_op jit(solution)/shard_map/ppermute | solution.py:332
  46.9 3.1 %collective-permute-start.5 = (f32[72,512]{1,0:T(8,128)S(1)}, f32[72,512]{1,0:T(8,128)S(1)}, u32[]{:S(2)}, u32[]{:S(2)}) collective-permute-start(f32[72,512]{1,0:T(8,128)S(1)} %collective-permute-done.2), channel_id=1, source_target_pairs={{0,64},{32,736},{64,128},{96,32},{128,192},{160,96},{192,256},{224... | collective-permute-start | bytes 442376 | tf_op jit(solution)/shard_map/ppermute | solution.py:322
  50.0 0.0 collective-permute-done.4.refs_1_
  50.0 0.0 collective-permute-done.3.refs_0_
  50.0 2.8 %collective-permute-done.5.refs_2_ = f32[72,512]{1,0:T(8,128)S(1)} collective-permute-done((f32[72,512]{1,0:T(8,128)S(1)}, f32[72,512]{1,0:T(8,128)S(1)}, u32[]{:S(2)}, u32[]{:S(2)}) %collective-permute-start.5) | collective-permute-done | bytes 147488 | tf_op jit(solution)/shard_map/ppermute | solution.py:322
  52.8 0.3 merge.5
  53.1 4.3 %collective-permute-start.9 = (f32[128,512]{1,0:T(8,128)S(1)}, f32[128,512]{1,0:T(8,128)S(1)}, u32[]{:S(2)}, u32[]{:S(2)}) collective-permute-start(f32[128,512]{1,0:T(8,128)S(1)} %get-tuple-element.57), channel_id=1, source_target_pairs={{0,64},{32,736},{64,128},{96,32},{128,192},{160,96},{192,256},{224... | collective-permute-start | bytes 786440 | tf_op jit(solution)/shard_map/ppermute | solution.py:322
  57.4 2.1 %stage.9 = (f32[256,512]{1,0:T(8,128)S(1)}, f32[72,512]{1,0:T(8,128)S(1)}) custom-call(s32[2,48]{1,0:T(2,128)S(1)} %get-tuple-element.71.table, bf16[8,16,512]{2,1,0:T(8,128)(2,1)S(1)} %vertical.1.v_ref, bf16[32,96,512]{2,1,0:T(8,128)(2,1)S(1)} %get-tuple-element.43.p_ref, s32[8,8,512]{2,1,0:T(8,128)S(1)} %get-tuple-element.44.q_ref), custom_call_target="tpu_custom_call" | custom-call | flops 3400000000 | bytes 500000 | tf_op jit(solution)/shard_map/stage/pallas_call | solution.py:194
  59.5 2.4 %collective-permute-start.7 = (f32[72,512]{1,0:T(8,128)S(1)}, f32[72,512]{1,0:T(8,128)S(1)}, u32[]{:S(2)}, u32[]{:S(2)}) collective-permute-start(f32[72,512]{1,0:T(8,128)S(1)} %get-tuple-element.55), channel_id=1, source_target_pairs={{0,32},{32,0},{64,96},{96,64},{128,160},{160,128},{192,224},{224,1... | collective-permute-start | bytes 442376 | tf_op jit(solution)/shard_map/ppermute | solution.py:332
  61.9 4.6 %collective-permute-start.6 = (f32[128,512]{1,0:T(8,128)S(1)}, f32[128,512]{1,0:T(8,128)S(1)}, u32[]{:S(2)}, u32[]{:S(2)}) collective-permute-start(f32[128,512]{1,0:T(8,128)S(1)} %get-tuple-element.51), channel_id=1, source_target_pairs={{0,64},{32,736},{64,128},{96,32},{128,192},{160,96},{192,256},{224... | collective-permute-start | bytes 786440 | tf_op jit(solution)/shard_map/ppermute | solution.py:322
  66.5 0.0 collective-permute-done.7.refs_0_
  66.5 0.1 merge.6
  66.6 0.0 collective-permute-done.9
  66.7 1.9 %collective-permute-start.12 = (f32[128,512]{1,0:T(8,128)S(1)}, f32[128,512]{1,0:T(8,128)S(1)}, u32[]{:S(2)}, u32[]{:S(2)}) collective-permute-start(f32[128,512]{1,0:T(8,128)S(1)} %add.28), channel_id=1, source_target_pairs={{0,64},{32,736},{64,128},{96,32},{128,192},{160,96},{192,256},{224... | collective-permute-start | bytes 786440 | tf_op jit(solution)/shard_map/ppermute | solution.py:322
  68.6 2.4 %stage.10 = (f32[256,512]{1,0:T(8,128)S(1)}, f32[72,512]{1,0:T(8,128)S(1)}) custom-call(s32[2,48]{1,0:T(2,128)S(1)} %get-tuple-element.71.table, bf16[8,16,512]{2,1,0:T(8,128)(2,1)S(1)} %vertical.1.v_ref, bf16[32,96,512]{2,1,0:T(8,128)(2,1)S(1)} %get-tuple-element.43.p_ref, s32[8,8,512]{2,1,0:T(8,128)S(1)} %get-tuple-element.44.q_ref), custom_call_target="tpu_custom_call" | custom-call | flops 3400000000 | bytes 500000 | tf_op jit(solution)/shard_map/stage/pallas_call | solution.py:194
  71.1 1.9 %collective-permute-start.10 = (f32[72,512]{1,0:T(8,128)S(1)}, f32[72,512]{1,0:T(8,128)S(1)}, u32[]{:S(2)}, u32[]{:S(2)}) collective-permute-start(f32[72,512]{1,0:T(8,128)S(1)} %get-tuple-element.61), channel_id=1, source_target_pairs={{0,32},{32,0},{64,96},{96,64},{128,160},{160,128},{192,224},{224,1... | collective-permute-start | bytes 442376 | tf_op jit(solution)/shard_map/ppermute | solution.py:332
  73.0 0.0 collective-permute-done.6
  73.0 3.3 %collective-permute-start.8 = (f32[128,512]{1,0:T(8,128)S(1)}, f32[128,512]{1,0:T(8,128)S(1)}, u32[]{:S(2)}, u32[]{:S(2)}) collective-permute-start(f32[128,512]{1,0:T(8,128)S(1)} %add.27), channel_id=1, source_target_pairs={{0,64},{32,736},{64,128},{96,32},{128,192},{160,96},{192,256},{224... | collective-permute-start | bytes 786440 | tf_op jit(solution)/shard_map/ppermute | solution.py:322
  76.4 0.0 collective-permute-done.10.refs_0_
  76.4 0.1 merge.7
  76.5 0.0 collective-permute-done.12
  76.5 2.2 %collective-permute-start.15 = (f32[128,512]{1,0:T(8,128)S(1)}, f32[128,512]{1,0:T(8,128)S(1)}, u32[]{:S(2)}, u32[]{:S(2)}) collective-permute-start(f32[128,512]{1,0:T(8,128)S(1)} %add.30), channel_id=1, source_target_pairs={{0,64},{32,736},{64,128},{96,32},{128,192},{160,96},{192,256},{224... | collective-permute-start | bytes 786440 | tf_op jit(solution)/shard_map/ppermute | solution.py:322
  78.8 2.1 %stage.11 = (f32[256,512]{1,0:T(8,128)S(1)}, f32[72,512]{1,0:T(8,128)S(1)}) custom-call(s32[2,48]{1,0:T(2,128)S(1)} %get-tuple-element.71.table, bf16[8,16,512]{2,1,0:T(8,128)(2,1)S(1)} %vertical.1.v_ref, bf16[32,96,512]{2,1,0:T(8,128)(2,1)S(1)} %get-tuple-element.43.p_ref, s32[8,8,512]{2,1,0:T(8,128)S(1)} %get-tuple-element.44.q_ref), custom_call_target="tpu_custom_call" | custom-call | flops 3400000000 | bytes 500000 | tf_op jit(solution)/shard_map/stage/pallas_call | solution.py:194
  80.9 2.1 %collective-permute-start.13 = (f32[72,512]{1,0:T(8,128)S(1)}, f32[72,512]{1,0:T(8,128)S(1)}, u32[]{:S(2)}, u32[]{:S(2)}) collective-permute-start(f32[72,512]{1,0:T(8,128)S(1)} %get-tuple-element.67), channel_id=1, source_target_pairs={{0,32},{32,0},{64,96},{96,64},{128,160},{160,128},{192,224},{224,1... | collective-permute-start | bytes 442376 | tf_op jit(solution)/shard_map/ppermute | solution.py:332
  83.0 0.0 collective-permute-done.8
  83.1 5.4 %collective-permute-start.11 = (f32[128,512]{1,0:T(8,128)S(1)}, f32[128,512]{1,0:T(8,128)S(1)}, u32[]{:S(2)}, u32[]{:S(2)}) collective-permute-start(f32[128,512]{1,0:T(8,128)S(1)} %add.29), channel_id=1, source_target_pairs={{0,64},{32,736},{64,128},{96,32},{128,192},{160,96},{192,256},{224... | collective-permute-start | bytes 786440 | tf_op jit(solution)/shard_map/ppermute | solution.py:322
  88.6 0.0 collective-permute-done.13.refs_0_
  88.6 0.1 merge.8
  88.7 0.0 collective-permute-done.15
  88.7 1.9 %collective-permute-start.17 = (f32[128,512]{1,0:T(8,128)S(1)}, f32[128,512]{1,0:T(8,128)S(1)}, u32[]{:S(2)}, u32[]{:S(2)}) collective-permute-start(f32[128,512]{1,0:T(8,128)S(1)} %add.32), channel_id=1, source_target_pairs={{0,64},{32,736},{64,128},{96,32},{128,192},{160,96},{192,256},{224... | collective-permute-start | bytes 786440 | tf_op jit(solution)/shard_map/ppermute | solution.py:322
  90.6 1.5 %stage.13 = f32[72,512]{1,0:T(8,128)S(1)} custom-call(s32[2,48]{1,0:T(2,128)S(1)} %get-tuple-element.71.table, bf16[8,16,512]{2,1,0:T(8,128)(2,1)S(1)} %vertical.1.v_ref, bf16[32,96,512]{2,1,0:T(8,128)(2,1)S(1)} %get-tuple-element.43.p_ref, s32[8,8,512]{2,1,0:T(8,128)S(1)} %get-tuple-element.44.q_ref), custom_call_target="tpu_custom_call" | custom-call | flops 1700000000 | bytes 500000 | tf_op jit(solution)/shard_map/stage/pallas_call | solution.py:194
  92.1 4.0 %collective-permute-start.16 = (f32[72,512]{1,0:T(8,128)S(1)}, f32[72,512]{1,0:T(8,128)S(1)}, u32[]{:S(2)}, u32[]{:S(2)}) collective-permute-start(f32[72,512]{1,0:T(8,128)S(1)} %stage.13), channel_id=1, source_target_pairs={{0,384},{32,416},{64,448},{96,480},{128,512},{160,544},{192,576},{... | collective-permute-start | bytes 442376 | tf_op jit(solution)/shard_map/ppermute | solution.py:340
  96.1 0.0 collective-permute-done.11
  96.2 4.3 %collective-permute-start.14 = (f32[128,512]{1,0:T(8,128)S(1)}, f32[128,512]{1,0:T(8,128)S(1)}, u32[]{:S(2)}, u32[]{:S(2)}) collective-permute-start(f32[128,512]{1,0:T(8,128)S(1)} %add.31), channel_id=1, source_target_pairs={{0,64},{32,736},{64,128},{96,32},{128,192},{160,96},{192,256},{224... | collective-permute-start | bytes 786440 | tf_op jit(solution)/shard_map/ppermute | solution.py:322
  100.5 1.5 %stage.12.dense_ref = f32[256,512]{1,0:T(8,128)S(1)} custom-call(s32[2,48]{1,0:T(2,128)S(1)} %get-tuple-element.71.table, bf16[8,16,512]{2,1,0:T(8,128)(2,1)S(1)} %vertical.1.v_ref, bf16[32,96,512]{2,1,0:T(8,128)(2,1)S(1)} %get-tuple-element.43.p_ref, s32[8,8,512]{2,1,0:T(8,128)S(1)} %get-tuple-element.44.q_ref), custom_call_target="tpu_custom_call" | custom-call | flops 1700000000 | bytes 500000 | tf_op jit(solution)/shard_map/stage/pallas_call | solution.py:194
  102.0 8.8 %collective-permute-done.16.refs_0_ = f32[72,512]{1,0:T(8,128)S(1)} collective-permute-done((f32[72,512]{1,0:T(8,128)S(1)}, f32[72,512]{1,0:T(8,128)S(1)}, u32[]{:S(2)}, u32[]{:S(2)}) %collective-permute-start.16) | collective-permute-done | bytes 147488 | tf_op jit(solution)/shard_map/ppermute | solution.py:340
  110.8 0.1 merge.9
  110.9 0.0 collective-permute-done.17
  111.0 2.2 %collective-permute-start.18 = (f32[128,512]{1,0:T(8,128)S(1)}, f32[128,512]{1,0:T(8,128)S(1)}, u32[]{:S(2)}, u32[]{:S(2)}) collective-permute-start(f32[128,512]{1,0:T(8,128)S(1)} %add.34), channel_id=1, source_target_pairs={{0,32},{32,0},{64,96},{96,64},{128,160},{160,128},{192,224},{224,1... | collective-permute-start | bytes 786440 | tf_op jit(solution)/shard_map/ppermute | solution.py:344
  113.2 0.0 collective-permute-done.14
  113.3 1.2 %collective-permute-done.18 = f32[128,512]{1,0:T(8,128)S(1)} collective-permute-done((f32[128,512]{1,0:T(8,128)S(1)}, f32[128,512]{1,0:T(8,128)S(1)}, u32[]{:S(2)}, u32[]{:S(2)}) %collective-permute-start.18) | collective-permute-done | bytes 262176 | tf_op jit(solution)/shard_map/ppermute | solution.py:344
  114.4 0.1 add_add_fusion
  114.5 0.9 copy.7
  (10 shorter events, 0.3 us)
Async XLA Ops:
  1.6 21.8 %collective-permute-start = (f32[1,4,8,512]{3,2,1,0:T(8,128)}, f32[1,4,8,512]{3,2,1,0:T(8,128)S(1)}, u32[]{:S(2)}, u32[]{:S(2)}) collective-permute-start(f32[1,4,8,512]{3,2,1,0:T(8,128)} %get-tuple-element.41), channel_id=1, source_target_pairs={{1,0},{2,1},{3,2},{4,3},{5,4},{6,5},{7,6},{8,7},{9,8},{10,9},{11,1... | collective-permute-start | bytes 196616 | tf_op jit(solution)/shard_map/ppermute | solution.py:298
  4.0 19.4 %collective-permute-start.1 = (f32[1,4,8,512]{3,2,1,0:T(8,128)}, f32[1,4,8,512]{3,2,1,0:T(8,128)S(1)}, u32[]{:S(2)}, u32[]{:S(2)}) collective-permute-start(f32[1,4,8,512]{3,2,1,0:T(8,128)} %get-tuple-element.42), channel_id=1, source_target_pairs={{0,1},{1,2},{2,3},{3,4},{4,5},{5,6},{6,7},{7,8},{8,9},{9,10},{10,1... | collective-permute-start | bytes 196616 | tf_op jit(solution)/shard_map/ppermute | solution.py:299
  10.2 1.2 %copy-start.2 = (s32[8,4,16,512]{3,2,1,0:T(8,128)S(1)}, s32[8,4,16,512]{3,2,1,0:T(8,128)}, u32[]{:S(2)}) copy-start(s32[8,4,16,512]{3,2,1,0:T(8,128)} %param.9) | copy-start | bytes 3145732
  11.4 1.0 copy-start.3
  12.4 0.7 copy-start.4
  13.1 0.7 copy-start.5
  13.8 9.6 %copy-start = (f32[4,4,8,512]{3,2,1,0:T(8,128)S(1)}, f32[4,4,8,512]{3,2,1,0:T(8,128)}, u32[]{:S(2)}) copy-start(f32[4,4,8,512]{3,2,1,0:T(8,128)} %adj_ref.1) | copy-start | bytes 786436
  13.8 9.6 %copy-start.1 = (f32[3,4,8,512]{3,2,1,0:T(8,128)S(1)}, f32[3,4,8,512]{3,2,1,0:T(8,128)}, u32[]{:S(2)}) copy-start(f32[3,4,8,512]{3,2,1,0:T(8,128)} %coef_ref.1) | copy-start | bytes 589828
  26.0 17.2 %collective-permute-start.2 = (f32[72,512]{1,0:T(8,128)S(1)}, f32[72,512]{1,0:T(8,128)S(1)}, u32[]{:S(2)}, u32[]{:S(2)}) collective-permute-start(f32[72,512]{1,0:T(8,128)S(1)} %get-tuple-element.45), channel_id=1, source_target_pairs={{0,32},{32,0},{64,96},{96,64},{128,160},{160,128},{192,224},{224,1... | collective-permute-start | bytes 442376 | tf_op jit(solution)/shard_map/ppermute | solution.py:325
  29.1 20.9 %collective-permute-start.4 = (f32[72,512]{1,0:T(8,128)S(1)}, f32[72,512]{1,0:T(8,128)S(1)}, u32[]{:S(2)}, u32[]{:S(2)}) collective-permute-start(f32[72,512]{1,0:T(8,128)S(1)} %get-tuple-element.49), channel_id=1, source_target_pairs={{0,64},{32,736},{64,128},{96,32},{128,192},{160,96},{192,256},{224... | collective-permute-start | bytes 442376 | tf_op jit(solution)/shard_map/ppermute | solution.py:322
  45.0 5.0 %collective-permute-start.3 = (f32[72,512]{1,0:T(8,128)S(1)}, f32[72,512]{1,0:T(8,128)S(1)}, u32[]{:S(2)}, u32[]{:S(2)}) collective-permute-start(f32[72,512]{1,0:T(8,128)S(1)} %get-tuple-element.48), channel_id=1, source_target_pairs={{0,32},{32,0},{64,96},{96,64},{128,160},{160,128},{192,224},{224,1... | collective-permute-start | bytes 442376 | tf_op jit(solution)/shard_map/ppermute | solution.py:332
  46.9 5.9 %collective-permute-start.5 = (f32[72,512]{1,0:T(8,128)S(1)}, f32[72,512]{1,0:T(8,128)S(1)}, u32[]{:S(2)}, u32[]{:S(2)}) collective-permute-start(f32[72,512]{1,0:T(8,128)S(1)} %collective-permute-done.2), channel_id=1, source_target_pairs={{0,64},{32,736},{64,128},{96,32},{128,192},{160,96},{192,256},{224... | collective-permute-start | bytes 442376 | tf_op jit(solution)/shard_map/ppermute | solution.py:322
  53.1 13.5 %collective-permute-start.9 = (f32[128,512]{1,0:T(8,128)S(1)}, f32[128,512]{1,0:T(8,128)S(1)}, u32[]{:S(2)}, u32[]{:S(2)}) collective-permute-start(f32[128,512]{1,0:T(8,128)S(1)} %get-tuple-element.57), channel_id=1, source_target_pairs={{0,64},{32,736},{64,128},{96,32},{128,192},{160,96},{192,256},{224... | collective-permute-start | bytes 786440 | tf_op jit(solution)/shard_map/ppermute | solution.py:322
  59.5 7.0 %collective-permute-start.7 = (f32[72,512]{1,0:T(8,128)S(1)}, f32[72,512]{1,0:T(8,128)S(1)}, u32[]{:S(2)}, u32[]{:S(2)}) collective-permute-start(f32[72,512]{1,0:T(8,128)S(1)} %get-tuple-element.55), channel_id=1, source_target_pairs={{0,32},{32,0},{64,96},{96,64},{128,160},{160,128},{192,224},{224,1... | collective-permute-start | bytes 442376 | tf_op jit(solution)/shard_map/ppermute | solution.py:332
  61.9 11.0 %collective-permute-start.6 = (f32[128,512]{1,0:T(8,128)S(1)}, f32[128,512]{1,0:T(8,128)S(1)}, u32[]{:S(2)}, u32[]{:S(2)}) collective-permute-start(f32[128,512]{1,0:T(8,128)S(1)} %get-tuple-element.51), channel_id=1, source_target_pairs={{0,64},{32,736},{64,128},{96,32},{128,192},{160,96},{192,256},{224... | collective-permute-start | bytes 786440 | tf_op jit(solution)/shard_map/ppermute | solution.py:322
  66.7 9.8 %collective-permute-start.12 = (f32[128,512]{1,0:T(8,128)S(1)}, f32[128,512]{1,0:T(8,128)S(1)}, u32[]{:S(2)}, u32[]{:S(2)}) collective-permute-start(f32[128,512]{1,0:T(8,128)S(1)} %add.28), channel_id=1, source_target_pairs={{0,64},{32,736},{64,128},{96,32},{128,192},{160,96},{192,256},{224... | collective-permute-start | bytes 786440 | tf_op jit(solution)/shard_map/ppermute | solution.py:322
  71.1 5.3 %collective-permute-start.10 = (f32[72,512]{1,0:T(8,128)S(1)}, f32[72,512]{1,0:T(8,128)S(1)}, u32[]{:S(2)}, u32[]{:S(2)}) collective-permute-start(f32[72,512]{1,0:T(8,128)S(1)} %get-tuple-element.61), channel_id=1, source_target_pairs={{0,32},{32,0},{64,96},{96,64},{128,160},{160,128},{192,224},{224,1... | collective-permute-start | bytes 442376 | tf_op jit(solution)/shard_map/ppermute | solution.py:332
  73.0 10.0 %collective-permute-start.8 = (f32[128,512]{1,0:T(8,128)S(1)}, f32[128,512]{1,0:T(8,128)S(1)}, u32[]{:S(2)}, u32[]{:S(2)}) collective-permute-start(f32[128,512]{1,0:T(8,128)S(1)} %add.27), channel_id=1, source_target_pairs={{0,64},{32,736},{64,128},{96,32},{128,192},{160,96},{192,256},{224... | collective-permute-start | bytes 786440 | tf_op jit(solution)/shard_map/ppermute | solution.py:322
  76.5 12.1 %collective-permute-start.15 = (f32[128,512]{1,0:T(8,128)S(1)}, f32[128,512]{1,0:T(8,128)S(1)}, u32[]{:S(2)}, u32[]{:S(2)}) collective-permute-start(f32[128,512]{1,0:T(8,128)S(1)} %add.30), channel_id=1, source_target_pairs={{0,64},{32,736},{64,128},{96,32},{128,192},{160,96},{192,256},{224... | collective-permute-start | bytes 786440 | tf_op jit(solution)/shard_map/ppermute | solution.py:322
  80.9 7.6 %collective-permute-start.13 = (f32[72,512]{1,0:T(8,128)S(1)}, f32[72,512]{1,0:T(8,128)S(1)}, u32[]{:S(2)}, u32[]{:S(2)}) collective-permute-start(f32[72,512]{1,0:T(8,128)S(1)} %get-tuple-element.67), channel_id=1, source_target_pairs={{0,32},{32,0},{64,96},{96,64},{128,160},{160,128},{192,224},{224,1... | collective-permute-start | bytes 442376 | tf_op jit(solution)/shard_map/ppermute | solution.py:332
  83.1 13.0 %collective-permute-start.11 = (f32[128,512]{1,0:T(8,128)S(1)}, f32[128,512]{1,0:T(8,128)S(1)}, u32[]{:S(2)}, u32[]{:S(2)}) collective-permute-start(f32[128,512]{1,0:T(8,128)S(1)} %add.29), channel_id=1, source_target_pairs={{0,64},{32,736},{64,128},{96,32},{128,192},{160,96},{192,256},{224... | collective-permute-start | bytes 786440 | tf_op jit(solution)/shard_map/ppermute | solution.py:322
  88.7 22.2 %collective-permute-start.17 = (f32[128,512]{1,0:T(8,128)S(1)}, f32[128,512]{1,0:T(8,128)S(1)}, u32[]{:S(2)}, u32[]{:S(2)}) collective-permute-start(f32[128,512]{1,0:T(8,128)S(1)} %add.32), channel_id=1, source_target_pairs={{0,64},{32,736},{64,128},{96,32},{128,192},{160,96},{192,256},{224... | collective-permute-start | bytes 786440 | tf_op jit(solution)/shard_map/ppermute | solution.py:322
  92.1 18.7 %collective-permute-start.16 = (f32[72,512]{1,0:T(8,128)S(1)}, f32[72,512]{1,0:T(8,128)S(1)}, u32[]{:S(2)}, u32[]{:S(2)}) collective-permute-start(f32[72,512]{1,0:T(8,128)S(1)} %stage.13), channel_id=1, source_target_pairs={{0,384},{32,416},{64,448},{96,480},{128,512},{160,544},{192,576},{... | collective-permute-start | bytes 442376 | tf_op jit(solution)/shard_map/ppermute | solution.py:340
  96.2 17.0 %collective-permute-start.14 = (f32[128,512]{1,0:T(8,128)S(1)}, f32[128,512]{1,0:T(8,128)S(1)}, u32[]{:S(2)}, u32[]{:S(2)}) collective-permute-start(f32[128,512]{1,0:T(8,128)S(1)} %add.31), channel_id=1, source_target_pairs={{0,64},{32,736},{64,128},{96,32},{128,192},{160,96},{192,256},{224... | collective-permute-start | bytes 786440 | tf_op jit(solution)/shard_map/ppermute | solution.py:322
  111.0 3.4 %collective-permute-start.18 = (f32[128,512]{1,0:T(8,128)S(1)}, f32[128,512]{1,0:T(8,128)S(1)}, u32[]{:S(2)}, u32[]{:S(2)}) collective-permute-start(f32[128,512]{1,0:T(8,128)S(1)} %add.34), channel_id=1, source_target_pairs={{0,32},{32,0},{64,96},{96,64},{128,160},{160,128},{192,224},{224,1... | collective-permute-start | bytes 786440 | tf_op jit(solution)/shard_map/ppermute | solution.py:344

commit v3 on v2

--- a/solution.py
+++ b/solution.py
@@ -10,6 +10,7 @@
 WIN = 32
 SPAN = 96
 LANES = 128
+TILE = 16
 CAP = 2
 MIB = 1024 * 1024
 
@@ -62,41 +63,32 @@
     lax.fori_loop(0, blk * deps, enter, 0)
 
 
-def place_kernel(chips, deps, owner_ref, slot_ref, w_hbm, cols_hbm, p_ref, q_ref, table, w_sc, cols_sc, x_sc, count, sems):
-    items, points, cols = cols_hbm.shape
-
-    def fetches(a):
-        part = pl.ds(a * deps, deps)
-        return (
-            pltpu.make_async_copy(w_hbm.at[part], w_sc.at[part], sems.at[0, a]),
-            pltpu.make_async_copy(cols_hbm.at[part], cols_sc.at[part], sems.at[1, a]),
-        )
-
-    for a in range(items // deps):
-        for fetch in fetches(a):
-            fetch.start()
+def place_kernel(chips, deps, owner_ref, slot_ref, w_ref, cols_ref, p_ref, q_ref, table, x_sc, w_sc, count):
+    items, points, cols = cols_ref.shape
     fill_table(chips, owner_ref, slot_ref, table, count)
     q_ref[...] = jnp.zeros_like(q_ref)
-    place = lax.broadcasted_iota(jnp.int32, (SPAN, LANES), 0).astype(jnp.float32).astype(jnp.bfloat16)
+    first = lax.broadcasted_iota(jnp.int32, (TILE, LANES), 0)
+    places = [(first + i).astype(jnp.float32).astype(jnp.bfloat16) for i in range(0, SPAN, TILE)]
 
     def block(a, _):
-        for fetch in fetches(a):
-            fetch.wait()
         for k in range(deps):
             item = a * deps + k
-            d = cols_sc[item]
+            d = cols_ref[item]
             rel = ((d - d[0:1] + cols // 2) & (cols - 1)) - cols // 2
             low = jnp.min(rel, axis=0, keepdims=True)
             base = (d[0:1] + low) & (cols - 1)
-            x_sc[k] = (rel - low + (base & (WIN - 1))).astype(jnp.float32).astype(jnp.bfloat16)
+            x_sc[k] = (rel - low + (base & (WIN - 1))).astype(jnp.float32)
+            w_sc[k] = w_ref[item].astype(jnp.float32)
             q_ref[a, k:k + 1, :] = base // WIN
             for t in range(cols // LANES):
                 part = slice(t * LANES, (t + 1) * LANES)
-                x, w = x_sc[k, :, part], w_sc[item, :, part]
-                acc = jnp.zeros((SPAN, LANES), jnp.bfloat16)
+                acc = [jnp.zeros((TILE, LANES), jnp.bfloat16)] * len(places)
                 for s in range(points):
-                    acc = jnp.where(place == x[s:s + 1], w[s:s + 1], acc)
-                p_ref[item, :, part] = acc
+                    x = jnp.broadcast_to(x_sc[k, s:s + 1, part], (TILE, LANES)).astype(jnp.bfloat16)
+                    w = jnp.broadcast_to(w_sc[k, s:s + 1, part], (TILE, LANES)).astype(jnp.bfloat16)
+                    acc = [jnp.where(place == x, w, total) for place, total in zip(places, acc)]
+                for i, total in enumerate(acc):
+                    p_ref[item, i * TILE:(i + 1) * TILE, part] = total
         return 0
 
     lax.fori_loop(0, items // deps, block, 0)
@@ -108,10 +100,9 @@
     entries = sum(stage_sizes(chips // 2))
     smem = pl.BlockSpec(memory_space=pltpu.SMEM)
     vmem = pl.BlockSpec(memory_space=pltpu.VMEM)
-    hbm = pl.BlockSpec(memory_space=pltpu.HBM)
     return pl.pallas_call(
         functools.partial(place_kernel, chips, deps),
-        in_specs=[smem, smem, hbm, hbm],
+        in_specs=[smem, smem, vmem, vmem],
         out_specs=[vmem, vmem, smem],
         out_shape=[
             jax.ShapeDtypeStruct((items, SPAN, cols), jnp.bfloat16),
@@ -119,11 +110,9 @@
             jax.ShapeDtypeStruct((2, entries), jnp.int32),
         ],
         scratch_shapes=[
-            pltpu.VMEM((items, points, cols), jnp.bfloat16),
-            pltpu.VMEM((items, points, cols), jnp.int32),
-            pltpu.VMEM((deps, points, cols), jnp.bfloat16),
+            pltpu.VMEM((deps, points, cols), jnp.float32),
+            pltpu.VMEM((deps, points, cols), jnp.float32),
             pltpu.SMEM((2 * chips,), jnp.int32),
-            pltpu.SemaphoreType.DMA((2, blk)),
         ],
         compiler_params=pltpu.CompilerParams(vmem_limit_bytes=8 * MIB),
         cost_estimate=pl.CostEstimate(flops=10000000000, bytes_accessed=5000000, transcendentals=0),
@@ -131,14 +120,15 @@
     )(dep_owner.T, dep_slot.T, weight, places)
 
 
-def item_contribution(v, q, p_ref, index, v_sc, p_sc):
+def item_contribution(v, q, p_ref, index, v_sc):
     rows, cols = v.shape
+    window = jnp.broadcast_to(q.astype(jnp.float32), (rows, cols)).astype(jnp.bfloat16)
     for i in range(cols // WIN):
-        v_sc[i * rows:(i + 1) * rows, :] = jnp.where(q == i, v, 0.0).astype(jnp.bfloat16)
-    p_sc[0:SPAN, :] = p_ref[index]
+        v_sc[i * rows:(i + 1) * rows, :] = jnp.where(window == jnp.bfloat16(i), v, jnp.bfloat16(0))
     u = lax.dot_general(
-        v_sc[...], p_sc[...], (((1,), (1,)), ((), ())), preferred_element_type=jnp.float32
+        v_sc[...], p_ref[index], (((1,), (1,)), ((), ())), preferred_element_type=jnp.float32
     )
+    u = jnp.concatenate([u, jnp.zeros((u.shape[0], LANES - SPAN), jnp.float32)], 1)
     lane = lax.broadcasted_iota(jnp.int32, (rows, LANES), 1)
     kept, passed = [], []
     for t in range(cols // LANES):
@@ -151,45 +141,44 @@
 
 
 def stage_kernel(groups, deps, rows, table, v_ref, p_ref, q_ref, *rest):
-    outs, (v_sc, p_sc) = rest[:-2], rest[-2:]
+    *outs, v_sc = rest
     cols = v_ref.shape[-1]
     blk = v_ref.shape[0]
-    p_sc[SPAN:, :] = jnp.zeros((LANES - SPAN, cols), jnp.bfloat16)
-    for (first, listed), out in zip(groups, outs):
+    for (firsts, listed), out in zip(groups, outs):
         out[...] = jnp.zeros_like(out)
-        if listed:
-            ids = lax.broadcasted_iota(jnp.int32, (8, cols), 0)
-            slots = jnp.zeros((8, cols), jnp.int32)
-            for n in range(2 * CAP):
-                slots = jnp.where(ids == n, table[1, first + n], slots)
-            out[2 * CAP * rows:, :] = slots.astype(jnp.float32)
-
-        def one(n, _):
-            index = table[0, first + n]
-
-            @pl.when(index >= 0)
-            def _():
-                row = lax.div(index, deps)
-                v = v_ref[row].astype(jnp.float32)
-                q = q_ref[row, pl.ds(lax.rem(index, deps), 1), :]
-                parts = item_contribution(v, q, p_ref, index, v_sc, p_sc)
-                if listed:
-                    at = n * rows
-                else:
-                    at = (lax.div(n, CAP) * blk + table[1, first + n]) * rows
-                at = pl.multiple_of(at, rows)
-                for t, part in enumerate(parts):
-                    where = (pl.ds(at, rows), slice(t * LANES, (t + 1) * LANES))
-                    out[where] = out[where] + part
-
-            return 0
-
-        lax.fori_loop(0, 2 * CAP, one, 0)
+        for number, first in enumerate(firsts):
+            top = number * (2 * CAP * rows + 8)
+            if listed:
+                ids = lax.broadcasted_iota(jnp.int32, (8, cols), 0)
+                slots = jnp.zeros((8, cols), jnp.int32)
+                for n in range(2 * CAP):
+                    slots = jnp.where(ids == n, table[1, first + n], slots)
+                out[top + 2 * CAP * rows:top + 2 * CAP * rows + 8, :] = slots.astype(jnp.float32)
+
+            def one(n, _):
+                index = table[0, first + n]
+
+                @pl.when(index >= 0)
+                def _():
+                    row = lax.div(index, deps)
+                    q = q_ref[row, pl.ds(lax.rem(index, deps), 1), :]
+                    parts = item_contribution(v_ref[row], q, p_ref, index, v_sc)
+                    if listed:
+                        at = pl.multiple_of(top + n * rows, 8)
+                    else:
+                        at = pl.multiple_of((lax.div(n, CAP) * blk + table[1, first + n]) * rows, rows)
+                    for t, part in enumerate(parts):
+                        where = (pl.ds(at, rows), slice(t * LANES, (t + 1) * LANES))
+                        out[where] = out[where] + part
+
+                return 0
+
+            lax.fori_loop(0, 2 * CAP, one, 0)
 
 
 def stage(groups, deps, table, v, p, q):
     blk, rows, cols = v.shape
-    heights = [2 * CAP * rows + 8 if listed else 2 * blk * rows for _, listed in groups]
+    heights = [len(firsts) * (2 * CAP * rows + 8) if listed else 2 * blk * rows for firsts, listed in groups]
     vmem = pl.BlockSpec(memory_space=pltpu.VMEM)
     return pl.pallas_call(
         functools.partial(stage_kernel, groups, deps, rows),
@@ -198,27 +187,27 @@
         out_shape=[jax.ShapeDtypeStruct((height, cols), jnp.float32) for height in heights],
         scratch_shapes=[
             pltpu.VMEM((cols // WIN * rows, cols), jnp.bfloat16),
-            pltpu.VMEM((LANES, cols), jnp.bfloat16),
         ],
         compiler_params=pltpu.CompilerParams(vmem_limit_bytes=10 * MIB),
         cost_estimate=pl.CostEstimate(
-            flops=len(groups) * 1700000000, bytes_accessed=500000, transcendentals=0
+            flops=len(groups) * 200000000, bytes_accessed=500000, transcendentals=0
         ),
         name="stage",
     )(table, v, p, q)
 
 
-def merge_kernel(blk, rows, dense_ref, *refs):
+def merge_kernel(blk, rows, picks, dense_ref, *refs):
     lists, outs = refs[:-2], refs[-2:]
     width = dense_ref.shape[1]
     for half, out in enumerate(outs):
         for c in range(0, width, LANES):
             part = slice(c, c + LANES)
             items = []
-            for ref in lists:
-                for n in range(half * CAP, half * CAP + CAP):
-                    at = 2 * CAP * rows + n
-                    items.append((ref[at:at + 1, part], ref[n * rows:(n + 1) * rows, part]))
+            for ref, numbers in zip(lists, picks):
+                for top in (number * (2 * CAP * rows + 8) for number in numbers):
+                    for n in range(half * CAP, half * CAP + CAP):
+                        at, slot = top + n * rows, top + 2 * CAP * rows + n
+                        items.append((ref[slot:slot + 1, part], ref[at:at + rows, part]))
             for b in range(blk):
                 at = (half * blk + b) * rows
                 total = dense_ref[at:at + rows, part]
@@ -230,12 +219,12 @@
 def merge(blk, rows, dense, *lists):
     width = dense.shape[1]
     return list(pl.pallas_call(
-        functools.partial(merge_kernel, blk, rows),
+        functools.partial(merge_kernel, blk, rows, [numbers for _, numbers in lists]),
         out_shape=[jax.ShapeDtypeStruct((blk * rows, width), jnp.float32)] * 2,
         compiler_params=pltpu.CompilerParams(vmem_limit_bytes=6 * MIB),
         cost_estimate=pl.CostEstimate(flops=1000000, bytes_accessed=1000000, transcendentals=0),
         name="merge",
-    )(dense, *lists))
+    )(dense, *(ref for ref, _ in lists)))
 
 
 def edges_kernel(adj0_ref, coef0_ref, adj1_ref, coef1_ref, first_ref, last_ref):
@@ -321,28 +310,45 @@
     def onward(values, pairs):
         return [lax.ppermute(value, "tile", pairs) for value in values]
 
-    own, others = made(table, (quad, True), (2 * quad, True))
-    given = lax.ppermute(others, "tile", sibling)
+    def own_at(h):
+        return quad + (far - 1 - h) * 2 * quad
+
+    def other_at(h):
+        return own_at(h) + quad
+
+    (listed,) = made(table, ((0,), True))
+    table, listed = behind(table, listed)
+    (farthest,) = onward([listed], ring)
+    own, others = made(table, ((own_at(far - 1),), True), ((other_at(far - 1),), True))
+    (given,) = onward([others], sibling)
     table, given = behind(table, given)
-    arrived = onward([own, given], ring)
-    opposite = None
-    for h in range(far - 2, 0, -1):
-        at = quad + (far - 1 - h) * 2 * quad
-        own, others = made(table, (at, False), (at + quad, True))
-        given = lax.ppermute(others, "tile", sibling)
-        if h == far - 2:
-            totals = merge(blk, rows, own, given, *arrived)
+    arrived = onward([jnp.concatenate([own, farthest], 0), given], ring)
+
+    totals, waiting = None, {}
+    near = far - 2
+
+    def exchanged(table, distances, *others):
+        (listed,) = made(table, (tuple(other_at(d) for d in distances), True))
+        table, listed, *others = lax.optimization_barrier((table, listed, *others))
+        (given,) = onward([listed], sibling)
+        waiting.update({d: (given, (number,)) for number, d in enumerate(distances)})
+        return table, *others
+
+    (table,) = exchanged(table, range(near, near // 2, -1))
+    for h in range(near, 0, -1):
+        (own,) = made(table, ((own_at(h),), False))
+        if totals is None:
+            table, own = behind(table, own)
+            table, own = exchanged(table, range(near // 2, 0, -1), own)
+            totals = merge(blk, rows, own, waiting[h], (arrived[0], (0, 1)), (arrived[1], (0,)))
         else:
-            totals = [total + mine for total, mine in zip(sums, lax.optimization_barrier(merge(blk, rows, own, given)))]
+            mine = lax.optimization_barrier(merge(blk, rows, own, waiting[h]))
+            totals = [total + here for total, here in zip(onward(totals, ring), mine)]
         table, totals[0] = behind(table, totals[0])
-        if h == far - 3:
-            (listed,) = made(table, (0, True))
-            opposite = lax.ppermute(listed, "tile", [(t, (t + tiles // 2) % tiles) for t in range(tiles)])
-        sums = onward(totals, ring)
-    (here,) = made(table, (quad + (far - 1) * 2 * quad, False))
-    here = lax.optimization_barrier(merge(blk, rows, here, opposite))
-    swapped = lax.ppermute(sums[0] + here[0], "tile", sibling)
-    result = sums[1] + here[1] + swapped
+    sums = onward(totals, ring)
+    (here,) = made(table, ((own_at(0),), False))
+    (swapped,) = onward([sums[0] + here[:blk * rows]], sibling)
+    result = sums[1] + here[blk * rows:] + swapped
     result = jnp.transpose(result.reshape(blk, rows, cols), (1, 0, 2))
     return result.reshape(lev_dev, fields, blk, cols)
 

time: 116 us -> 101 us (0.87)
  waiting for transfers between devices: 12.8 us -> 1.17 us
  starting transfers between devices: 71.4 us -> 69.6 us
  Pallas kernels: 25.9 us -> 24.2 us
    ppermute x7 -> x0, starting transfers between devices: 17.7 us -> none  [the longest x5 11.5 us: shards(): given = lax.ppermute(others, 'tile', sibling)]
    ppermute x10 -> x15, starting transfers between devices: 45.1 us -> 61 us  [onward(): return [lax.ppermute(value, 'tile', pairs) for value in values]]
    ppermute x7 -> x0, waiting for transfers between devices: 9.99 us -> none  [the longest x1 8.81 us: shards(): lax.ppermute(listed, 'tile', [(t, (t + tiles // 2) % tiles) for t in rang...]
    pallas_call x1, Pallas kernels: 9.59 us -> 7.28 us  [placed(): pl.pallas_call(functools.partial(place_kernel, chips, deps), in_specs=[sm...]
    ppermute x10 -> x15, waiting for transfers between devices: 2.81 us -> 1.17 us  [onward(): return [lax.ppermute(value, 'tile', pairs) for value in values]]
    pallas_call x7 -> x9, Pallas kernels: 14 us -> 14.7 us  [stage(): pl.pallas_call(functools.partial(stage_kernel, groups, deps, rows), in_sp...]
  transfers between devices with their start and end apart: 19 -> 17, of which waited for: 3 -> 1; matrix products, arithmetic and copies ran while one was open for 0% -> 0% of each run, Pallas kernels for 19% -> 19%
where the time goes in v3:
time: 101 us; the launch traced here: 100 us
  starting transfers between devices  69.6 us (69%)
  Pallas kernels  24.2 us (24%)
  local copies, waits for them, and re-layouts  4.49 us (4%)
  waiting for transfers between devices  1.17 us (1%)
    ppermute x15, starting transfers between devices, onward(): return [lax.ppermute(value, 'tile', pairs) for value in values]  61 us
    pallas_call x9, Pallas kernels, stage(): pl.pallas_call(functools.partial(stage_kernel, groups, deps, rows), in_sp...  14.7 us
    pallas_call x1, Pallas kernels, placed(): pl.pallas_call(functools.partial(place_kernel, chips, deps), in_specs=[sm...  7.28 us
    ppermute x1, starting transfers between devices, shards(): before = lax.ppermute(last, 'lev', [(i, i + 1) for i in range(levels - 1)])  6.15 us
    unnamed x12, local copies, waits for them, and re-layouts  3.63 us
    ppermute x1, starting transfers between devices, shards(): after = lax.ppermute(first, 'lev', [(i + 1, i) for i in range(levels - 1)])  2.44 us
  transfers between devices with their start and end apart: 17, of which 1 were waited for; matrix products, arithmetic and copies ran while one was open for 0% of the time, Pallas kernels for 19%

profile of v3, /device:TPU:31, one launch (start us, length us, event | category | flops | bytes accessed | tf_op | source)
XLA Modules:
  0.0 100.3 jit_solution(13537449790272924625)
XLA Ops:
  0.0 1.5 %edges.1 = (f32[1,4,8,512]{3,2,1,0:T(8,128)}, f32[1,4,8,512]{3,2,1,0:T(8,128)}) custom-call(f32[4,4,8,512]{3,2,1,0:T(8,128)} %adj_ref.1, f32[3,4,8,512]{3,2,1,0:T(8,128)} %coef_ref.1, f32[4,4,8,512]{3,2,1,0:T(8,128)} %adj_ref.1, f32[3,4,8,512]{3,2,1,0:T(8,128)} %coef_ref.1), custom_call_target="tpu_custom_call" | custom-call | tf_op jit(solution)/shard_map/edges/pallas_call | solution.py:238
  1.5 2.4 %collective-permute-start = (f32[1,4,8,512]{3,2,1,0:T(8,128)}, f32[1,4,8,512]{3,2,1,0:T(8,128)S(1)}, u32[]{:S(2)}, u32[]{:S(2)}) collective-permute-start(f32[1,4,8,512]{3,2,1,0:T(8,128)} %get-tuple-element.40), channel_id=1, source_target_pairs={{1,0},{2,1},{3,2},{4,3},{5,4},{6,5},{7,6},{8,7},{9,8},{10,9},{11,1... | collective-permute-start | bytes 196616 | tf_op jit(solution)/shard_map/ppermute | solution.py:287
  4.0 6.1 %collective-permute-start.1 = (f32[1,4,8,512]{3,2,1,0:T(8,128)}, f32[1,4,8,512]{3,2,1,0:T(8,128)S(1)}, u32[]{:S(2)}, u32[]{:S(2)}) collective-permute-start(f32[1,4,8,512]{3,2,1,0:T(8,128)} %get-tuple-element.41), channel_id=1, source_target_pairs={{0,1},{1,2},{2,3},{3,4},{4,5},{5,6},{6,7},{7,8},{8,9},{9,10},{10,1... | collective-permute-start | bytes 196616 | tf_op jit(solution)/shard_map/ppermute | solution.py:288
  10.1 0.0 copy-start.2
  10.2 1.2 %copy-done.2 = s32[8,4,16,512]{3,2,1,0:T(8,128)S(1)} copy-done((s32[8,4,16,512]{3,2,1,0:T(8,128)S(1)}, s32[8,4,16,512]{3,2,1,0:T(8,128)}, u32[]{:S(2)}) %copy-start.2) | copy-done | bytes 1048600
  11.4 0.0 copy-start.3
  11.4 1.0 %copy-done.3 = bf16[8,4,16,512]{3,2,1,0:T(8,128)(2,1)S(1)} copy-done((bf16[8,4,16,512]{3,2,1,0:T(8,128)(2,1)S(1)}, bf16[8,4,16,512]{3,2,1,0:T(8,128)(2,1)}, u32[]{:S(2)}) %copy-start.3) | copy-done | bytes 524312
  12.4 0.0 copy-start.4
  12.4 0.7 copy-done.4
  13.1 0.0 copy-start.5
  13.1 0.7 copy-done.5
  13.8 0.0 copy-start
  13.8 0.0 copy-start.1
  13.8 7.3 %place.1 = (bf16[32,96,512]{2,1,0:T(8,128)(2,1)S(1)}, s32[8,8,512]{2,1,0:T(8,128)S(1)}, s32[2,48]{1,0:T(2,128)S(1)}) custom-call(s32[4,8]{1,0:T(4,128)S(1)} %bitcast.10, s32[4,8]{1,0:T(4,128)S(1)} %bitcast.11, bf16[32,16,512]{2,1,0:T(8,128)(2,1)S(1)} %bitcast.9, s32[32,16,512]{2,1,0:T(8,128)S(1)} %bitcast.8), custom_call_target="tpu_custom_call" | custom-call | flops 10000000000 | bytes 5000000 | tf_op jit(solution)/shard_map/place/pallas_call | solution.py:103
  21.1 0.0 collective-permute-done.after_ref
  21.1 0.0 collective-permute-done.1.before_ref
  21.1 0.0 copy-done
  21.1 0.0 copy-done.1
  21.1 0.1 vertical.1.v_ref
  21.2 1.2 %stage.9 = f32[72,512]{1,0:T(8,128)S(1)} custom-call(s32[2,48]{1,0:T(2,128)S(1)} %get-tuple-element.71.table, bf16[8,16,512]{2,1,0:T(8,128)(2,1)S(1)} %vertical.1.v_ref, bf16[32,96,512]{2,1,0:T(8,128)(2,1)S(1)} %get-tuple-element.42.p_ref, s32[8,8,512]{2,1,0:T(8,128)S(1)} %get-tuple-element.43.q_ref), custom_call_target="tpu_custom_call" | custom-call | flops 200000000 | bytes 500000 | tf_op jit(solution)/shard_map/stage/pallas_call | solution.py:183
  22.4 1.8 %stage.10 = (f32[72,512]{1,0:T(8,128)S(1)}, f32[72,512]{1,0:T(8,128)S(1)}) custom-call(s32[2,48]{1,0:T(2,128)S(1)} %get-tuple-element.71.table, bf16[8,16,512]{2,1,0:T(8,128)(2,1)S(1)} %vertical.1.v_ref, bf16[32,96,512]{2,1,0:T(8,128)(2,1)S(1)} %get-tuple-element.42.p_ref, s32[8,8,512]{2,1,0:T(8,128)S(1)} %get-tuple-element.43.q_ref), custom_call_target="tpu_custom_call" | custom-call | flops 400000000 | bytes 500000 | tf_op jit(solution)/shard_map/stage/pallas_call | solution.py:183
  24.2 3.1 %collective-permute-start.2 = (f32[72,512]{1,0:T(8,128)S(1)}, f32[72,512]{1,0:T(8,128)S(1)}, u32[]{:S(2)}, u32[]{:S(2)}) collective-permute-start(f32[72,512]{1,0:T(8,128)S(1)} %get-tuple-element.45), channel_id=1, source_target_pairs={{0,32},{32,0},{64,96},{96,64},{128,160},{160,128},{192,224},{224,1... | collective-permute-start | bytes 442376 | tf_op jit(solution)/shard_map/ppermute | solution.py:311
  27.3 14.3 %collective-permute-start.4 = (f32[72,512]{1,0:T(8,128)S(1)}, f32[72,512]{1,0:T(8,128)S(1)}, u32[]{:S(2)}, u32[]{:S(2)}) collective-permute-start(f32[72,512]{1,0:T(8,128)S(1)} %stage.9), channel_id=1, source_target_pairs={{0,64},{32,736},{64,128},{96,32},{128,192},{160,96},{192,256},{224... | collective-permute-start | bytes 442376 | tf_op jit(solution)/shard_map/ppermute | solution.py:311
  41.6 0.0 collective-permute-done.2
  41.6 2.3 %stage.11 = f32[144,512]{1,0:T(8,128)S(1)} custom-call(s32[2,48]{1,0:T(2,128)S(1)} %get-tuple-element.71.table, bf16[8,16,512]{2,1,0:T(8,128)(2,1)S(1)} %vertical.1.v_ref, bf16[32,96,512]{2,1,0:T(8,128)(2,1)S(1)} %get-tuple-element.42.p_ref, s32[8,8,512]{2,1,0:T(8,128)S(1)} %get-tuple-element.43.q_ref), custom_call_target="tpu_custom_call" | custom-call | flops 200000000 | bytes 500000 | tf_op jit(solution)/shard_map/stage/pallas_call | solution.py:183
  44.0 1.9 %collective-permute-start.3 = (f32[144,512]{1,0:T(8,128)S(1)}, f32[144,512]{1,0:T(8,128)S(1)}, u32[]{:S(2)}, u32[]{:S(2)}) collective-permute-start(f32[144,512]{1,0:T(8,128)S(1)} %stage.11), channel_id=1, source_target_pairs={{0,32},{32,0},{64,96},{96,64},{128,160},{160,128},{192,224},{224,1... | collective-permute-start | bytes 884744 | tf_op jit(solution)/shard_map/ppermute | solution.py:311
  45.9 0.0 collective-permute-done.4
  46.0 3.3 %collective-permute-start.5 = (f32[144,512]{1,0:T(8,128)S(1)}, f32[144,512]{1,0:T(8,128)S(1)}, u32[]{:S(2)}, u32[]{:S(2)}) collective-permute-start(f32[144,512]{1,0:T(8,128)S(1)} %pad_maximum_fusion), channel_id=1, source_target_pairs={{0,64},{32,736},{64,128},{96,32},{128,192},{160,96},{192,256},{224... | collective-permute-start | bytes 884744 | tf_op jit(solution)/shard_map/ppermute | solution.py:311
  49.3 2.4 %collective-permute-start.6 = (f32[72,512]{1,0:T(8,128)S(1)}, f32[72,512]{1,0:T(8,128)S(1)}, u32[]{:S(2)}, u32[]{:S(2)}) collective-permute-start(f32[72,512]{1,0:T(8,128)S(1)} %collective-permute-done.2), channel_id=1, source_target_pairs={{0,64},{32,736},{64,128},{96,32},{128,192},{160,96},{192,256},{224... | collective-permute-start | bytes 442376 | tf_op jit(solution)/shard_map/ppermute | solution.py:311
  51.7 1.7 %stage.12.dense_ref = f32[256,512]{1,0:T(8,128)S(1)} custom-call(s32[2,48]{1,0:T(2,128)S(1)} %get-tuple-element.71.table, bf16[8,16,512]{2,1,0:T(8,128)(2,1)S(1)} %vertical.1.v_ref, bf16[32,96,512]{2,1,0:T(8,128)(2,1)S(1)} %get-tuple-element.42.p_ref, s32[8,8,512]{2,1,0:T(8,128)S(1)} %get-tuple-element.43.q_ref), custom_call_target="tpu_custom_call" | custom-call | flops 200000000 | bytes 500000 | tf_op jit(solution)/shard_map/stage/pallas_call | solution.py:183
  53.5 2.6 %stage.13 = f32[144,512]{1,0:T(8,128)S(1)} custom-call(s32[2,48]{1,0:T(2,128)S(1)} %get-tuple-element.71.table, bf16[8,16,512]{2,1,0:T(8,128)(2,1)S(1)} %vertical.1.v_ref, bf16[32,96,512]{2,1,0:T(8,128)(2,1)S(1)} %get-tuple-element.42.p_ref, s32[8,8,512]{2,1,0:T(8,128)S(1)} %get-tuple-element.43.q_ref), custom_call_target="tpu_custom_call" | custom-call | flops 200000000 | bytes 500000 | tf_op jit(solution)/shard_map/stage/pallas_call | solution.py:183
  56.1 0.0 collective-permute-done.6.refs_2_
  56.2 0.0 collective-permute-done.3.refs_0_
  56.2 0.0 collective-permute-done.5.refs_1_
  56.2 0.3 merge.4
  56.5 3.4 %collective-permute-start.9 = (f32[128,512]{1,0:T(8,128)S(1)}, f32[128,512]{1,0:T(8,128)S(1)}, u32[]{:S(2)}, u32[]{:S(2)}) collective-permute-start(f32[128,512]{1,0:T(8,128)S(1)} %get-tuple-element.60), channel_id=1, source_target_pairs={{0,64},{32,736},{64,128},{96,32},{128,192},{160,96},{192,256},{224... | collective-permute-start | bytes 786440 | tf_op jit(solution)/shard_map/ppermute | solution.py:311
  59.9 2.1 %collective-permute-start.10 = (f32[144,512]{1,0:T(8,128)S(1)}, f32[144,512]{1,0:T(8,128)S(1)}, u32[]{:S(2)}, u32[]{:S(2)}) collective-permute-start(f32[144,512]{1,0:T(8,128)S(1)} %stage.13), channel_id=1, source_target_pairs={{0,32},{32,0},{64,96},{96,64},{128,160},{160,128},{192,224},{224,1... | collective-permute-start | bytes 884744 | tf_op jit(solution)/shard_map/ppermute | solution.py:311
  62.1 4.9 %collective-permute-start.7 = (f32[128,512]{1,0:T(8,128)S(1)}, f32[128,512]{1,0:T(8,128)S(1)}, u32[]{:S(2)}, u32[]{:S(2)}) collective-permute-start(f32[128,512]{1,0:T(8,128)S(1)} %get-tuple-element.55), channel_id=1, source_target_pairs={{0,64},{32,736},{64,128},{96,32},{128,192},{160,96},{192,256},{224... | collective-permute-start | bytes 786440 | tf_op jit(solution)/shard_map/ppermute | solution.py:311
  66.9 1.2 %stage.14.dense_ref = f32[256,512]{1,0:T(8,128)S(1)} custom-call(s32[2,48]{1,0:T(2,128)S(1)} %get-tuple-element.71.table, bf16[8,16,512]{2,1,0:T(8,128)(2,1)S(1)} %vertical.1.v_ref, bf16[32,96,512]{2,1,0:T(8,128)(2,1)S(1)} %get-tuple-element.42.p_ref, s32[8,8,512]{2,1,0:T(8,128)S(1)} %get-tuple-element.43.q_ref), custom_call_target="tpu_custom_call" | custom-call | flops 200000000 | bytes 500000 | tf_op jit(solution)/shard_map/stage/pallas_call | solution.py:183
  68.1 0.1 merge.5
  68.2 0.0 collective-permute-done.9
  68.3 2.5 %collective-permute-start.12 = (f32[128,512]{1,0:T(8,128)S(1)}, f32[128,512]{1,0:T(8,128)S(1)}, u32[]{:S(2)}, u32[]{:S(2)}) collective-permute-start(f32[128,512]{1,0:T(8,128)S(1)} %add.28), channel_id=1, source_target_pairs={{0,64},{32,736},{64,128},{96,32},{128,192},{160,96},{192,256},{224... | collective-permute-start | bytes 786440 | tf_op jit(solution)/shard_map/ppermute | solution.py:311
  70.8 0.0 collective-permute-done.7
  70.8 4.5 %collective-permute-start.8 = (f32[128,512]{1,0:T(8,128)S(1)}, f32[128,512]{1,0:T(8,128)S(1)}, u32[]{:S(2)}, u32[]{:S(2)}) collective-permute-start(f32[128,512]{1,0:T(8,128)S(1)} %add.27), channel_id=1, source_target_pairs={{0,64},{32,736},{64,128},{96,32},{128,192},{160,96},{192,256},{224... | collective-permute-start | bytes 786440 | tf_op jit(solution)/shard_map/ppermute | solution.py:311
  75.3 1.2 %stage.15.dense_ref = f32[256,512]{1,0:T(8,128)S(1)} custom-call(s32[2,48]{1,0:T(2,128)S(1)} %get-tuple-element.71.table, bf16[8,16,512]{2,1,0:T(8,128)(2,1)S(1)} %vertical.1.v_ref, bf16[32,96,512]{2,1,0:T(8,128)(2,1)S(1)} %get-tuple-element.42.p_ref, s32[8,8,512]{2,1,0:T(8,128)S(1)} %get-tuple-element.43.q_ref), custom_call_target="tpu_custom_call" | custom-call | flops 200000000 | bytes 500000 | tf_op jit(solution)/shard_map/stage/pallas_call | solution.py:183
  76.5 0.0 collective-permute-done.10.refs_0_
  76.5 0.1 merge.6
  76.6 0.0 collective-permute-done.12
  76.6 2.5 %collective-permute-start.14 = (f32[128,512]{1,0:T(8,128)S(1)}, f32[128,512]{1,0:T(8,128)S(1)}, u32[]{:S(2)}, u32[]{:S(2)}) collective-permute-start(f32[128,512]{1,0:T(8,128)S(1)} %add.30), channel_id=1, source_target_pairs={{0,64},{32,736},{64,128},{96,32},{128,192},{160,96},{192,256},{224... | collective-permute-start | bytes 786440 | tf_op jit(solution)/shard_map/ppermute | solution.py:311
  79.1 0.0 collective-permute-done.8
  79.2 4.5 %collective-permute-start.11 = (f32[128,512]{1,0:T(8,128)S(1)}, f32[128,512]{1,0:T(8,128)S(1)}, u32[]{:S(2)}, u32[]{:S(2)}) collective-permute-start(f32[128,512]{1,0:T(8,128)S(1)} %add.29), channel_id=1, source_target_pairs={{0,64},{32,736},{64,128},{96,32},{128,192},{160,96},{192,256},{224... | collective-permute-start | bytes 786440 | tf_op jit(solution)/shard_map/ppermute | solution.py:311
  83.7 1.2 %stage.16.dense_ref = f32[256,512]{1,0:T(8,128)S(1)} custom-call(s32[2,48]{1,0:T(2,128)S(1)} %get-tuple-element.71.table, bf16[8,16,512]{2,1,0:T(8,128)(2,1)S(1)} %vertical.1.v_ref, bf16[32,96,512]{2,1,0:T(8,128)(2,1)S(1)} %get-tuple-element.42.p_ref, s32[8,8,512]{2,1,0:T(8,128)S(1)} %get-tuple-element.43.q_ref), custom_call_target="tpu_custom_call" | custom-call | flops 200000000 | bytes 500000 | tf_op jit(solution)/shard_map/stage/pallas_call | solution.py:183
  84.8 0.1 merge.7
  84.9 0.0 collective-permute-done.14
  85.0 2.5 %collective-permute-start.15 = (f32[128,512]{1,0:T(8,128)S(1)}, f32[128,512]{1,0:T(8,128)S(1)}, u32[]{:S(2)}, u32[]{:S(2)}) collective-permute-start(f32[128,512]{1,0:T(8,128)S(1)} %add.32), channel_id=1, source_target_pairs={{0,64},{32,736},{64,128},{96,32},{128,192},{160,96},{192,256},{224... | collective-permute-start | bytes 786440 | tf_op jit(solution)/shard_map/ppermute | solution.py:311
  87.5 0.0 collective-permute-done.11
  87.5 4.5 %collective-permute-start.13 = (f32[128,512]{1,0:T(8,128)S(1)}, f32[128,512]{1,0:T(8,128)S(1)}, u32[]{:S(2)}, u32[]{:S(2)}) collective-permute-start(f32[128,512]{1,0:T(8,128)S(1)} %add.31), channel_id=1, source_target_pairs={{0,64},{32,736},{64,128},{96,32},{128,192},{160,96},{192,256},{224... | collective-permute-start | bytes 786440 | tf_op jit(solution)/shard_map/ppermute | solution.py:311
  92.0 1.5 %stage.17 = f32[256,512]{1,0:T(8,128)S(1)} custom-call(s32[2,48]{1,0:T(2,128)S(1)} %get-tuple-element.71.table, bf16[8,16,512]{2,1,0:T(8,128)(2,1)S(1)} %vertical.1.v_ref, bf16[32,96,512]{2,1,0:T(8,128)(2,1)S(1)} %get-tuple-element.42.p_ref, s32[8,8,512]{2,1,0:T(8,128)S(1)} %get-tuple-element.43.q_ref), custom_call_target="tpu_custom_call" | custom-call | flops 200000000 | bytes 500000 | tf_op jit(solution)/shard_map/stage/pallas_call | solution.py:183
  93.5 0.0 collective-permute-done.15
  93.5 4.6 %collective-permute-start.16 = (f32[128,512]{1,0:T(8,128)S(1)}, f32[128,512]{1,0:T(8,128)S(1)}, u32[]{:S(2)}, u32[]{:S(2)}) collective-permute-start(f32[128,512]{1,0:T(8,128)S(1)} %slice_add_fusion), channel_id=1, source_target_pairs={{0,32},{32,0},{64,96},{96,64},{128,160},{160,128},{192,224},{224,1... | collective-permute-start | bytes 786440 | tf_op jit(solution)/shard_map/ppermute | solution.py:311
  98.2 0.0 collective-permute-done.13
  98.2 1.1 %collective-permute-done.16 = f32[128,512]{1,0:T(8,128)S(1)} collective-permute-done((f32[128,512]{1,0:T(8,128)S(1)}, f32[128,512]{1,0:T(8,128)S(1)}, u32[]{:S(2)}, u32[]{:S(2)}) %collective-permute-start.16) | collective-permute-done | bytes 262176 | tf_op jit(solution)/shard_map/ppermute | solution.py:311
  99.3 0.1 fusion
  99.4 0.9 copy.7
  (8 shorter events, 0.3 us)
Async XLA Ops:
  1.5 19.5 %collective-permute-start = (f32[1,4,8,512]{3,2,1,0:T(8,128)}, f32[1,4,8,512]{3,2,1,0:T(8,128)S(1)}, u32[]{:S(2)}, u32[]{:S(2)}) collective-permute-start(f32[1,4,8,512]{3,2,1,0:T(8,128)} %get-tuple-element.40), channel_id=1, source_target_pairs={{1,0},{2,1},{3,2},{4,3},{5,4},{6,5},{7,6},{8,7},{9,8},{10,9},{11,1... | collective-permute-start | bytes 196616 | tf_op jit(solution)/shard_map/ppermute | solution.py:287
  4.0 17.1 %collective-permute-start.1 = (f32[1,4,8,512]{3,2,1,0:T(8,128)}, f32[1,4,8,512]{3,2,1,0:T(8,128)S(1)}, u32[]{:S(2)}, u32[]{:S(2)}) collective-permute-start(f32[1,4,8,512]{3,2,1,0:T(8,128)} %get-tuple-element.41), channel_id=1, source_target_pairs={{0,1},{1,2},{2,3},{3,4},{4,5},{5,6},{6,7},{7,8},{8,9},{9,10},{10,1... | collective-permute-start | bytes 196616 | tf_op jit(solution)/shard_map/ppermute | solution.py:288
  10.1 1.2 %copy-start.2 = (s32[8,4,16,512]{3,2,1,0:T(8,128)S(1)}, s32[8,4,16,512]{3,2,1,0:T(8,128)}, u32[]{:S(2)}) copy-start(s32[8,4,16,512]{3,2,1,0:T(8,128)} %param.9) | copy-start | bytes 3145732
  11.4 1.0 %copy-start.3 = (bf16[8,4,16,512]{3,2,1,0:T(8,128)(2,1)S(1)}, bf16[8,4,16,512]{3,2,1,0:T(8,128)(2,1)}, u32[]{:S(2)}) copy-start(bf16[8,4,16,512]{3,2,1,0:T(8,128)(2,1)} %param.8) | copy-start | bytes 1572868
  12.4 0.7 copy-start.4
  13.1 0.7 copy-start.5
  13.8 7.3 %copy-start = (f32[4,4,8,512]{3,2,1,0:T(8,128)S(1)}, f32[4,4,8,512]{3,2,1,0:T(8,128)}, u32[]{:S(2)}) copy-start(f32[4,4,8,512]{3,2,1,0:T(8,128)} %adj_ref.1) | copy-start | bytes 786436
  13.8 7.3 %copy-start.1 = (f32[3,4,8,512]{3,2,1,0:T(8,128)S(1)}, f32[3,4,8,512]{3,2,1,0:T(8,128)}, u32[]{:S(2)}) copy-start(f32[3,4,8,512]{3,2,1,0:T(8,128)} %coef_ref.1) | copy-start | bytes 589828
  24.2 17.5 %collective-permute-start.2 = (f32[72,512]{1,0:T(8,128)S(1)}, f32[72,512]{1,0:T(8,128)S(1)}, u32[]{:S(2)}, u32[]{:S(2)}) collective-permute-start(f32[72,512]{1,0:T(8,128)S(1)} %get-tuple-element.45), channel_id=1, source_target_pairs={{0,32},{32,0},{64,96},{96,64},{128,160},{160,128},{192,224},{224,1... | collective-permute-start | bytes 442376 | tf_op jit(solution)/shard_map/ppermute | solution.py:311
  27.3 18.6 %collective-permute-start.4 = (f32[72,512]{1,0:T(8,128)S(1)}, f32[72,512]{1,0:T(8,128)S(1)}, u32[]{:S(2)}, u32[]{:S(2)}) collective-permute-start(f32[72,512]{1,0:T(8,128)S(1)} %stage.9), channel_id=1, source_target_pairs={{0,64},{32,736},{64,128},{96,32},{128,192},{160,96},{192,256},{224... | collective-permute-start | bytes 442376 | tf_op jit(solution)/shard_map/ppermute | solution.py:311
  44.0 12.2 %collective-permute-start.3 = (f32[144,512]{1,0:T(8,128)S(1)}, f32[144,512]{1,0:T(8,128)S(1)}, u32[]{:S(2)}, u32[]{:S(2)}) collective-permute-start(f32[144,512]{1,0:T(8,128)S(1)} %stage.11), channel_id=1, source_target_pairs={{0,32},{32,0},{64,96},{96,64},{128,160},{160,128},{192,224},{224,1... | collective-permute-start | bytes 884744 | tf_op jit(solution)/shard_map/ppermute | solution.py:311
  46.0 10.2 %collective-permute-start.5 = (f32[144,512]{1,0:T(8,128)S(1)}, f32[144,512]{1,0:T(8,128)S(1)}, u32[]{:S(2)}, u32[]{:S(2)}) collective-permute-start(f32[144,512]{1,0:T(8,128)S(1)} %pad_maximum_fusion), channel_id=1, source_target_pairs={{0,64},{32,736},{64,128},{96,32},{128,192},{160,96},{192,256},{224... | collective-permute-start | bytes 884744 | tf_op jit(solution)/shard_map/ppermute | solution.py:311
  49.3 6.9 %collective-permute-start.6 = (f32[72,512]{1,0:T(8,128)S(1)}, f32[72,512]{1,0:T(8,128)S(1)}, u32[]{:S(2)}, u32[]{:S(2)}) collective-permute-start(f32[72,512]{1,0:T(8,128)S(1)} %collective-permute-done.2), channel_id=1, source_target_pairs={{0,64},{32,736},{64,128},{96,32},{128,192},{160,96},{192,256},{224... | collective-permute-start | bytes 442376 | tf_op jit(solution)/shard_map/ppermute | solution.py:311
  56.5 11.7 %collective-permute-start.9 = (f32[128,512]{1,0:T(8,128)S(1)}, f32[128,512]{1,0:T(8,128)S(1)}, u32[]{:S(2)}, u32[]{:S(2)}) collective-permute-start(f32[128,512]{1,0:T(8,128)S(1)} %get-tuple-element.60), channel_id=1, source_target_pairs={{0,64},{32,736},{64,128},{96,32},{128,192},{160,96},{192,256},{224... | collective-permute-start | bytes 786440 | tf_op jit(solution)/shard_map/ppermute | solution.py:311
  59.9 16.6 %collective-permute-start.10 = (f32[144,512]{1,0:T(8,128)S(1)}, f32[144,512]{1,0:T(8,128)S(1)}, u32[]{:S(2)}, u32[]{:S(2)}) collective-permute-start(f32[144,512]{1,0:T(8,128)S(1)} %stage.13), channel_id=1, source_target_pairs={{0,32},{32,0},{64,96},{96,64},{128,160},{160,128},{192,224},{224,1... | collective-permute-start | bytes 884744 | tf_op jit(solution)/shard_map/ppermute | solution.py:311
  62.1 8.7 %collective-permute-start.7 = (f32[128,512]{1,0:T(8,128)S(1)}, f32[128,512]{1,0:T(8,128)S(1)}, u32[]{:S(2)}, u32[]{:S(2)}) collective-permute-start(f32[128,512]{1,0:T(8,128)S(1)} %get-tuple-element.55), channel_id=1, source_target_pairs={{0,64},{32,736},{64,128},{96,32},{128,192},{160,96},{192,256},{224... | collective-permute-start | bytes 786440 | tf_op jit(solution)/shard_map/ppermute | solution.py:311
  68.3 8.3 %collective-permute-start.12 = (f32[128,512]{1,0:T(8,128)S(1)}, f32[128,512]{1,0:T(8,128)S(1)}, u32[]{:S(2)}, u32[]{:S(2)}) collective-permute-start(f32[128,512]{1,0:T(8,128)S(1)} %add.28), channel_id=1, source_target_pairs={{0,64},{32,736},{64,128},{96,32},{128,192},{160,96},{192,256},{224... | collective-permute-start | bytes 786440 | tf_op jit(solution)/shard_map/ppermute | solution.py:311
  70.8 8.3 %collective-permute-start.8 = (f32[128,512]{1,0:T(8,128)S(1)}, f32[128,512]{1,0:T(8,128)S(1)}, u32[]{:S(2)}, u32[]{:S(2)}) collective-permute-start(f32[128,512]{1,0:T(8,128)S(1)} %add.27), channel_id=1, source_target_pairs={{0,64},{32,736},{64,128},{96,32},{128,192},{160,96},{192,256},{224... | collective-permute-start | bytes 786440 | tf_op jit(solution)/shard_map/ppermute | solution.py:311
  76.6 8.3 %collective-permute-start.14 = (f32[128,512]{1,0:T(8,128)S(1)}, f32[128,512]{1,0:T(8,128)S(1)}, u32[]{:S(2)}, u32[]{:S(2)}) collective-permute-start(f32[128,512]{1,0:T(8,128)S(1)} %add.30), channel_id=1, source_target_pairs={{0,64},{32,736},{64,128},{96,32},{128,192},{160,96},{192,256},{224... | collective-permute-start | bytes 786440 | tf_op jit(solution)/shard_map/ppermute | solution.py:311
  79.2 8.3 %collective-permute-start.11 = (f32[128,512]{1,0:T(8,128)S(1)}, f32[128,512]{1,0:T(8,128)S(1)}, u32[]{:S(2)}, u32[]{:S(2)}) collective-permute-start(f32[128,512]{1,0:T(8,128)S(1)} %add.29), channel_id=1, source_target_pairs={{0,64},{32,736},{64,128},{96,32},{128,192},{160,96},{192,256},{224... | collective-permute-start | bytes 786440 | tf_op jit(solution)/shard_map/ppermute | solution.py:311
  85.0 8.5 %collective-permute-start.15 = (f32[128,512]{1,0:T(8,128)S(1)}, f32[128,512]{1,0:T(8,128)S(1)}, u32[]{:S(2)}, u32[]{:S(2)}) collective-permute-start(f32[128,512]{1,0:T(8,128)S(1)} %add.32), channel_id=1, source_target_pairs={{0,64},{32,736},{64,128},{96,32},{128,192},{160,96},{192,256},{224... | collective-permute-start | bytes 786440 | tf_op jit(solution)/shard_map/ppermute | solution.py:311
  87.5 10.7 %collective-permute-start.13 = (f32[128,512]{1,0:T(8,128)S(1)}, f32[128,512]{1,0:T(8,128)S(1)}, u32[]{:S(2)}, u32[]{:S(2)}) collective-permute-start(f32[128,512]{1,0:T(8,128)S(1)} %add.31), channel_id=1, source_target_pairs={{0,64},{32,736},{64,128},{96,32},{128,192},{160,96},{192,256},{224... | collective-permute-start | bytes 786440 | tf_op jit(solution)/shard_map/ppermute | solution.py:311
  93.5 5.8 %collective-permute-start.16 = (f32[128,512]{1,0:T(8,128)S(1)}, f32[128,512]{1,0:T(8,128)S(1)}, u32[]{:S(2)}, u32[]{:S(2)}) collective-permute-start(f32[128,512]{1,0:T(8,128)S(1)} %slice_add_fusion), channel_id=1, source_target_pairs={{0,32},{32,0},{64,96},{96,64},{128,160},{160,128},{192,224},{224,1... | collective-permute-start | bytes 786440 | tf_op jit(solution)/shard_map/ppermute | solution.py:311

commit v4 on v3

--- a/solution.py
+++ b/solution.py
@@ -19,8 +19,8 @@
     return [2 * CAP] + [4 * CAP] * (far - 1) + [2 * CAP]
 
 
-def fill_table(chips, owner_ref, slot_ref, table, count):
-    deps, blk = owner_ref.shape
+def fill_table(chips, pair_ref, table, count):
+    deps, blk = pair_ref.shape[1:]
     far = chips // 2
     tile = lax.axis_index("tile")
     chip, core = lax.div(tile, 2), lax.rem(tile, 2)
@@ -42,7 +42,7 @@
 
     def enter(n, _):
         row, k = lax.div(n, deps), lax.rem(n, deps)
-        owner = owner_ref[k, row]
+        owner = pair_ref[0, k, row]
         turn = count[owner]
         count[owner] = turn + 1
         away = lax.rem(ahead * (lax.div(owner, 2) - chip) + chips, chips)
@@ -57,15 +57,15 @@
         )
         at = start + half * CAP + turn
         table[0, at] = n
-        table[1, at] = slot_ref[k, row]
+        table[1, at] = pair_ref[1, k, row]
         return 0
 
     lax.fori_loop(0, blk * deps, enter, 0)
 
 
-def place_kernel(chips, deps, owner_ref, slot_ref, w_ref, cols_ref, p_ref, q_ref, table, x_sc, w_sc, count):
+def place_kernel(chips, deps, pair_ref, w_ref, cols_ref, p_ref, q_ref, table, x_sc, w_sc, count):
     items, points, cols = cols_ref.shape
-    fill_table(chips, owner_ref, slot_ref, table, count)
+    fill_table(chips, pair_ref, table, count)
     q_ref[...] = jnp.zeros_like(q_ref)
     first = lax.broadcasted_iota(jnp.int32, (TILE, LANES), 0)
     places = [(first + i).astype(jnp.float32).astype(jnp.bfloat16) for i in range(0, SPAN, TILE)]
@@ -102,7 +102,7 @@
     vmem = pl.BlockSpec(memory_space=pltpu.VMEM)
     return pl.pallas_call(
         functools.partial(place_kernel, chips, deps),
-        in_specs=[smem, smem, vmem, vmem],
+        in_specs=[smem, vmem, vmem],
         out_specs=[vmem, vmem, smem],
         out_shape=[
             jax.ShapeDtypeStruct((items, SPAN, cols), jnp.bfloat16),
@@ -117,7 +117,7 @@
         compiler_params=pltpu.CompilerParams(vmem_limit_bytes=8 * MIB),
         cost_estimate=pl.CostEstimate(flops=10000000000, bytes_accessed=5000000, transcendentals=0),
         name="place",
-    )(dep_owner.T, dep_slot.T, weight, places)
+    )(jnp.stack([dep_owner.T, dep_slot.T]), weight, places)
 
 
 def item_contribution(v, q, p_ref, index, v_sc):
@@ -319,13 +319,14 @@
     (listed,) = made(table, ((0,), True))
     table, listed = behind(table, listed)
     (farthest,) = onward([listed], ring)
-    own, others = made(table, ((own_at(far - 1),), True), ((other_at(far - 1),), True))
+    near = far - 2
+    own, others = made(table, ((own_at(far - 1),), True), ((other_at(far - 1), other_at(near)), True))
+    others, farthest = lax.optimization_barrier((others, farthest))
     (given,) = onward([others], sibling)
     table, given = behind(table, given)
-    arrived = onward([jnp.concatenate([own, farthest], 0), given], ring)
-
-    totals, waiting = None, {}
-    near = far - 2
+    (arrived,) = onward([jnp.concatenate([own, farthest, given[:own.shape[0]]], 0)], ring)
+
+    totals, waiting = None, {near: (given, (1,))}
 
     def exchanged(table, distances, *others):
         (listed,) = made(table, (tuple(other_at(d) for d in distances), True))
@@ -334,13 +335,12 @@
         waiting.update({d: (given, (number,)) for number, d in enumerate(distances)})
         return table, *others
 
-    (table,) = exchanged(table, range(near, near // 2, -1))
     for h in range(near, 0, -1):
         (own,) = made(table, ((own_at(h),), False))
         if totals is None:
             table, own = behind(table, own)
-            table, own = exchanged(table, range(near // 2, 0, -1), own)
-            totals = merge(blk, rows, own, waiting[h], (arrived[0], (0, 1)), (arrived[1], (0,)))
+            table, own = exchanged(table, range(near - 1, 0, -1), own)
+            totals = merge(blk, rows, own, waiting[h], (arrived, (0, 1, 2)))
         else:
             mine = lax.optimization_barrier(merge(blk, rows, own, waiting[h]))
             totals = [total + here for total, here in zip(onward(totals, ring), mine)]

time: 101 us -> 98.6 us (0.976)
  starting transfers between devices: 69.6 us -> 67.4 us
  local copies, waits for them, and re-layouts: 4.49 us -> 3.14 us
  waiting for transfers between devices: 1.17 us -> 2.35 us
    ppermute x15 -> x13, starting transfers between devices: 61 us -> 58.8 us  [onward(): return [lax.ppermute(value, 'tile', pairs) for value in values]]
    unnamed x12 -> x8, local copies, waits for them, and re-layouts: 3.63 us -> 2.27 us
    ppermute x15 -> x13, waiting for transfers between devices: 1.17 us -> 2.35 us  [onward(): return [lax.ppermute(value, 'tile', pairs) for value in values]]
    pallas_call x9 -> x8, Pallas kernels: 14.7 us -> 14.1 us  [stage(): pl.pallas_call(functools.partial(stage_kernel, groups, deps, rows), in_sp...]
  transfers between devices with their start and end apart: 17 -> 15, of which waited for: 1 -> 2; matrix products, arithmetic and copies ran while one was open for 0% -> 1% of each run, Pallas kernels for 19% -> 21%
where the time goes in v4:
time: 98.6 us; the launch traced here: 98 us
  starting transfers between devices  67.4 us (68%)
  Pallas kernels  23.7 us (24%)
  local copies, waits for them, and re-layouts  3.14 us (3%)
  waiting for transfers between devices  2.35 us (2%)
  other arithmetic  1.07 us (1%)
    ppermute x13, starting transfers between devices, onward(): return [lax.ppermute(value, 'tile', pairs) for value in values]  58.8 us
    pallas_call x8, Pallas kernels, stage(): pl.pallas_call(functools.partial(stage_kernel, groups, deps, rows), in_sp...  14.1 us
    pallas_call x1, Pallas kernels, placed(): pl.pallas_call(functools.partial(place_kernel, chips, deps), in_specs=[sm...  7.28 us
    ppermute x1, starting transfers between devices, shards(): before = lax.ppermute(last, 'lev', [(i, i + 1) for i in range(levels - 1)])  6.15 us
    ppermute x1, starting transfers between devices, shards(): after = lax.ppermute(first, 'lev', [(i + 1, i) for i in range(levels - 1)])  2.44 us
    ppermute x13, waiting for transfers between devices, onward(): return [lax.ppermute(value, 'tile', pairs) for value in values]  2.35 us
    unnamed x8, local copies, waits for them, and re-layouts  2.27 us
  transfers between devices with their start and end apart: 15, of which 2 were waited for; matrix products, arithmetic and copies ran while one was open for 1% of the time, Pallas kernels for 21%

profile of v4, /device:TPU:31, one launch (start us, length us, event | category | flops | bytes accessed | tf_op | source)
XLA Modules:
  0.0 98.0 jit_solution(5590496036151070928)
XLA Ops:
  0.0 1.5 %edges.1 = (f32[1,4,8,512]{3,2,1,0:T(8,128)}, f32[1,4,8,512]{3,2,1,0:T(8,128)}) custom-call(f32[4,4,8,512]{3,2,1,0:T(8,128)} %adj_ref.1, f32[3,4,8,512]{3,2,1,0:T(8,128)} %coef_ref.1, f32[4,4,8,512]{3,2,1,0:T(8,128)} %adj_ref.1, f32[3,4,8,512]{3,2,1,0:T(8,128)} %coef_ref.1), custom_call_target="tpu_custom_call" | custom-call | tf_op jit(solution)/shard_map/edges/pallas_call | solution.py:238
  1.5 2.4 %collective-permute-start = (f32[1,4,8,512]{3,2,1,0:T(8,128)}, f32[1,4,8,512]{3,2,1,0:T(8,128)S(1)}, u32[]{:S(2)}, u32[]{:S(2)}) collective-permute-start(f32[1,4,8,512]{3,2,1,0:T(8,128)} %get-tuple-element.40), channel_id=1, source_target_pairs={{1,0},{2,1},{3,2},{4,3},{5,4},{6,5},{7,6},{8,7},{9,8},{10,9},{11,1... | collective-permute-start | bytes 196616 | tf_op jit(solution)/shard_map/ppermute | solution.py:287
  4.0 6.1 %collective-permute-start.1 = (f32[1,4,8,512]{3,2,1,0:T(8,128)}, f32[1,4,8,512]{3,2,1,0:T(8,128)S(1)}, u32[]{:S(2)}, u32[]{:S(2)}) collective-permute-start(f32[1,4,8,512]{3,2,1,0:T(8,128)} %get-tuple-element.41), channel_id=1, source_target_pairs={{0,1},{1,2},{2,3},{3,4},{4,5},{5,6},{6,7},{7,8},{8,9},{9,10},{10,1... | collective-permute-start | bytes 196616 | tf_op jit(solution)/shard_map/ppermute | solution.py:288
  10.1 0.7 pad_add_fusion.pair_ref
  10.8 0.0 copy-start.2
  10.8 1.2 %copy-done.2 = s32[8,4,16,512]{3,2,1,0:T(8,128)S(1)} copy-done((s32[8,4,16,512]{3,2,1,0:T(8,128)S(1)}, s32[8,4,16,512]{3,2,1,0:T(8,128)}, u32[]{:S(2)}) %copy-start.2) | copy-done | bytes 1048600
  12.1 0.0 copy-start.3
  12.1 1.0 %copy-done.3 = bf16[8,4,16,512]{3,2,1,0:T(8,128)(2,1)S(1)} copy-done((bf16[8,4,16,512]{3,2,1,0:T(8,128)(2,1)S(1)}, bf16[8,4,16,512]{3,2,1,0:T(8,128)(2,1)}, u32[]{:S(2)}) %copy-start.3) | copy-done | bytes 524312
  13.1 0.0 copy-start
  13.1 0.0 copy-start.1
  13.1 7.3 %place.1 = (bf16[32,96,512]{2,1,0:T(8,128)(2,1)S(1)}, s32[8,8,512]{2,1,0:T(8,128)S(1)}, s32[2,48]{1,0:T(2,128)S(1)}) custom-call(s32[2,4,8]{2,1,0:T(4,128)S(1)} %pad_add_fusion.pair_ref, bf16[32,16,512]{2,1,0:T(8,128)(2,1)S(1)} %bitcast.13, s32[32,16,512]{2,1,0:T(8,128)S(1)} %bitcast.12), custom_call_target="tpu_custom_call" | custom-call | flops 10000000000 | bytes 5000000 | tf_op jit(solution)/shard_map/place/pallas_call | solution.py:103
  20.4 0.0 collective-permute-done.after_ref
  20.4 0.0 collective-permute-done.1.before_ref
  20.4 0.0 copy-done
  20.4 0.0 copy-done.1
  20.4 0.1 vertical.1.v_ref
  20.6 1.2 %stage.8 = f32[72,512]{1,0:T(8,128)S(1)} custom-call(s32[2,48]{1,0:T(2,128)S(1)} %get-tuple-element.71.table, bf16[8,16,512]{2,1,0:T(8,128)(2,1)S(1)} %vertical.1.v_ref, bf16[32,96,512]{2,1,0:T(8,128)(2,1)S(1)} %get-tuple-element.42.p_ref, s32[8,8,512]{2,1,0:T(8,128)S(1)} %get-tuple-element.43.q_ref), custom_call_target="tpu_custom_call" | custom-call | flops 200000000 | bytes 500000 | tf_op jit(solution)/shard_map/stage/pallas_call | solution.py:183
  21.7 14.3 %collective-permute-start.2 = (f32[72,512]{1,0:T(8,128)S(1)}, f32[72,512]{1,0:T(8,128)S(1)}, u32[]{:S(2)}, u32[]{:S(2)}) collective-permute-start(f32[72,512]{1,0:T(8,128)S(1)} %stage.8), channel_id=1, source_target_pairs={{0,64},{32,736},{64,128},{96,32},{128,192},{160,96},{192,256},{224... | collective-permute-start | bytes 442376 | tf_op jit(solution)/shard_map/ppermute | solution.py:311
  36.0 2.7 %stage.9 = (f32[72,512]{1,0:T(8,128)S(1)}, f32[144,512]{1,0:T(8,128)S(1)}) custom-call(s32[2,48]{1,0:T(2,128)S(1)} %get-tuple-element.71.table, bf16[8,16,512]{2,1,0:T(8,128)(2,1)S(1)} %vertical.1.v_ref, bf16[32,96,512]{2,1,0:T(8,128)(2,1)S(1)} %get-tuple-element.42.p_ref, s32[8,8,512]{2,1,0:T(8,128)S(1)} %get-tuple-element.43.q_ref), custom_call_target="tpu_custom_call" | custom-call | flops 400000000 | bytes 500000 | tf_op jit(solution)/shard_map/stage/pallas_call | solution.py:183
  38.7 0.0 collective-permute-done.2
  38.7 3.8 %collective-permute-start.3 = (f32[144,512]{1,0:T(8,128)S(1)}, f32[144,512]{1,0:T(8,128)S(1)}, u32[]{:S(2)}, u32[]{:S(2)}) collective-permute-start(f32[144,512]{1,0:T(8,128)S(1)} %get-tuple-element.47), channel_id=1, source_target_pairs={{0,32},{32,0},{64,96},{96,64},{128,160},{160,128},{192,224},{224,1... | collective-permute-start | bytes 884744 | tf_op jit(solution)/shard_map/ppermute | solution.py:311
  42.6 1.2 %collective-permute-done.3.refs_0_ = f32[144,512]{1,0:T(8,128)S(1)} collective-permute-done((f32[144,512]{1,0:T(8,128)S(1)}, f32[144,512]{1,0:T(8,128)S(1)}, u32[]{:S(2)}, u32[]{:S(2)}) %collective-permute-start.3) | collective-permute-done | bytes 294944 | tf_op jit(solution)/shard_map/ppermute | solution.py:311
  43.8 3.6 %collective-permute-start.4 = (f32[216,512]{1,0:T(8,128)S(1)}, f32[216,512]{1,0:T(8,128)S(1)}, u32[]{:S(2)}, u32[]{:S(2)}) collective-permute-start(f32[216,512]{1,0:T(8,128)S(1)} %pad_maximum_fusion), channel_id=1, source_target_pairs={{0,64},{32,736},{64,128},{96,32},{128,192},{160,96},{192,256},{224... | collective-permute-start | bytes 1327112 | tf_op jit(solution)/shard_map/ppermute | solution.py:311
  47.5 1.2 %stage.10.dense_ref = f32[256,512]{1,0:T(8,128)S(1)} custom-call(s32[2,48]{1,0:T(2,128)S(1)} %get-tuple-element.71.table, bf16[8,16,512]{2,1,0:T(8,128)(2,1)S(1)} %vertical.1.v_ref, bf16[32,96,512]{2,1,0:T(8,128)(2,1)S(1)} %get-tuple-element.42.p_ref, s32[8,8,512]{2,1,0:T(8,128)S(1)} %get-tuple-element.43.q_ref), custom_call_target="tpu_custom_call" | custom-call | flops 200000000 | bytes 500000 | tf_op jit(solution)/shard_map/stage/pallas_call | solution.py:183
  48.7 3.2 %stage.11 = f32[216,512]{1,0:T(8,128)S(1)} custom-call(s32[2,48]{1,0:T(2,128)S(1)} %get-tuple-element.71.table, bf16[8,16,512]{2,1,0:T(8,128)(2,1)S(1)} %vertical.1.v_ref, bf16[32,96,512]{2,1,0:T(8,128)(2,1)S(1)} %get-tuple-element.42.p_ref, s32[8,8,512]{2,1,0:T(8,128)S(1)} %get-tuple-element.43.q_ref), custom_call_target="tpu_custom_call" | custom-call | flops 200000000 | bytes 500000 | tf_op jit(solution)/shard_map/stage/pallas_call | solution.py:183
  51.9 1.9 %collective-permute-start.6 = (f32[216,512]{1,0:T(8,128)S(1)}, f32[216,512]{1,0:T(8,128)S(1)}, u32[]{:S(2)}, u32[]{:S(2)}) collective-permute-start(f32[216,512]{1,0:T(8,128)S(1)} %stage.11), channel_id=1, source_target_pairs={{0,32},{32,0},{64,96},{96,64},{128,160},{160,128},{192,224},{224,1... | collective-permute-start | bytes 1327112 | tf_op jit(solution)/shard_map/ppermute | solution.py:311
  53.8 0.0 collective-permute-done.4.refs_1_
  53.8 0.3 merge.4
  54.2 3.9 %collective-permute-start.8 = (f32[128,512]{1,0:T(8,128)S(1)}, f32[128,512]{1,0:T(8,128)S(1)}, u32[]{:S(2)}, u32[]{:S(2)}) collective-permute-start(f32[128,512]{1,0:T(8,128)S(1)} %get-tuple-element.61), channel_id=1, source_target_pairs={{0,64},{32,736},{64,128},{96,32},{128,192},{160,96},{192,256},{224... | collective-permute-start | bytes 786440 | tf_op jit(solution)/shard_map/ppermute | solution.py:311
  58.1 2.3 %collective-permute-start.5 = (f32[128,512]{1,0:T(8,128)S(1)}, f32[128,512]{1,0:T(8,128)S(1)}, u32[]{:S(2)}, u32[]{:S(2)}) collective-permute-start(f32[128,512]{1,0:T(8,128)S(1)} %get-tuple-element.55), channel_id=1, source_target_pairs={{0,64},{32,736},{64,128},{96,32},{128,192},{160,96},{192,256},{224... | collective-permute-start | bytes 786440 | tf_op jit(solution)/shard_map/ppermute | solution.py:311
  60.4 1.5 %stage.12.dense_ref = f32[256,512]{1,0:T(8,128)S(1)} custom-call(s32[2,48]{1,0:T(2,128)S(1)} %get-tuple-element.71.table, bf16[8,16,512]{2,1,0:T(8,128)(2,1)S(1)} %vertical.1.v_ref, bf16[32,96,512]{2,1,0:T(8,128)(2,1)S(1)} %get-tuple-element.42.p_ref, s32[8,8,512]{2,1,0:T(8,128)S(1)} %get-tuple-element.43.q_ref), custom_call_target="tpu_custom_call" | custom-call | flops 200000000 | bytes 500000 | tf_op jit(solution)/shard_map/stage/pallas_call | solution.py:183
  61.9 0.0 collective-permute-done.6.refs_0_
  61.9 0.1 merge.5
  62.0 0.0 collective-permute-done.8
  62.1 4.4 %collective-permute-start.10 = (f32[128,512]{1,0:T(8,128)S(1)}, f32[128,512]{1,0:T(8,128)S(1)}, u32[]{:S(2)}, u32[]{:S(2)}) collective-permute-start(f32[128,512]{1,0:T(8,128)S(1)} %add.28), channel_id=1, source_target_pairs={{0,64},{32,736},{64,128},{96,32},{128,192},{160,96},{192,256},{224... | collective-permute-start | bytes 786440 | tf_op jit(solution)/shard_map/ppermute | solution.py:311
  66.4 0.0 collective-permute-done.5
  66.5 2.8 %collective-permute-start.7 = (f32[128,512]{1,0:T(8,128)S(1)}, f32[128,512]{1,0:T(8,128)S(1)}, u32[]{:S(2)}, u32[]{:S(2)}) collective-permute-start(f32[128,512]{1,0:T(8,128)S(1)} %add.27), channel_id=1, source_target_pairs={{0,64},{32,736},{64,128},{96,32},{128,192},{160,96},{192,256},{224... | collective-permute-start | bytes 786440 | tf_op jit(solution)/shard_map/ppermute | solution.py:311
  69.3 1.5 %stage.13.dense_ref = f32[256,512]{1,0:T(8,128)S(1)} custom-call(s32[2,48]{1,0:T(2,128)S(1)} %get-tuple-element.71.table, bf16[8,16,512]{2,1,0:T(8,128)(2,1)S(1)} %vertical.1.v_ref, bf16[32,96,512]{2,1,0:T(8,128)(2,1)S(1)} %get-tuple-element.42.p_ref, s32[8,8,512]{2,1,0:T(8,128)S(1)} %get-tuple-element.43.q_ref), custom_call_target="tpu_custom_call" | custom-call | flops 200000000 | bytes 500000 | tf_op jit(solution)/shard_map/stage/pallas_call | solution.py:183
  70.7 0.1 merge.6
  70.8 0.0 collective-permute-done.10
  70.9 3.9 %collective-permute-start.12 = (f32[128,512]{1,0:T(8,128)S(1)}, f32[128,512]{1,0:T(8,128)S(1)}, u32[]{:S(2)}, u32[]{:S(2)}) collective-permute-start(f32[128,512]{1,0:T(8,128)S(1)} %add.30), channel_id=1, source_target_pairs={{0,64},{32,736},{64,128},{96,32},{128,192},{160,96},{192,256},{224... | collective-permute-start | bytes 786440 | tf_op jit(solution)/shard_map/ppermute | solution.py:311
  74.8 0.0 collective-permute-done.7
  74.9 2.8 %collective-permute-start.9 = (f32[128,512]{1,0:T(8,128)S(1)}, f32[128,512]{1,0:T(8,128)S(1)}, u32[]{:S(2)}, u32[]{:S(2)}) collective-permute-start(f32[128,512]{1,0:T(8,128)S(1)} %add.29), channel_id=1, source_target_pairs={{0,64},{32,736},{64,128},{96,32},{128,192},{160,96},{192,256},{224... | collective-permute-start | bytes 786440 | tf_op jit(solution)/shard_map/ppermute | solution.py:311
  77.6 1.5 %stage.14.dense_ref = f32[256,512]{1,0:T(8,128)S(1)} custom-call(s32[2,48]{1,0:T(2,128)S(1)} %get-tuple-element.71.table, bf16[8,16,512]{2,1,0:T(8,128)(2,1)S(1)} %vertical.1.v_ref, bf16[32,96,512]{2,1,0:T(8,128)(2,1)S(1)} %get-tuple-element.42.p_ref, s32[8,8,512]{2,1,0:T(8,128)S(1)} %get-tuple-element.43.q_ref), custom_call_target="tpu_custom_call" | custom-call | flops 200000000 | bytes 500000 | tf_op jit(solution)/shard_map/stage/pallas_call | solution.py:183
  79.1 0.1 merge.7
  79.2 0.0 collective-permute-done.12
  79.3 3.9 %collective-permute-start.13 = (f32[128,512]{1,0:T(8,128)S(1)}, f32[128,512]{1,0:T(8,128)S(1)}, u32[]{:S(2)}, u32[]{:S(2)}) collective-permute-start(f32[128,512]{1,0:T(8,128)S(1)} %add.32), channel_id=1, source_target_pairs={{0,64},{32,736},{64,128},{96,32},{128,192},{160,96},{192,256},{224... | collective-permute-start | bytes 786440 | tf_op jit(solution)/shard_map/ppermute | solution.py:311
  83.2 0.0 collective-permute-done.9
  83.2 2.8 %collective-permute-start.11 = (f32[128,512]{1,0:T(8,128)S(1)}, f32[128,512]{1,0:T(8,128)S(1)}, u32[]{:S(2)}, u32[]{:S(2)}) collective-permute-start(f32[128,512]{1,0:T(8,128)S(1)} %add.31), channel_id=1, source_target_pairs={{0,64},{32,736},{64,128},{96,32},{128,192},{160,96},{192,256},{224... | collective-permute-start | bytes 786440 | tf_op jit(solution)/shard_map/ppermute | solution.py:311
  86.0 1.5 %stage.15 = f32[256,512]{1,0:T(8,128)S(1)} custom-call(s32[2,48]{1,0:T(2,128)S(1)} %get-tuple-element.71.table, bf16[8,16,512]{2,1,0:T(8,128)(2,1)S(1)} %vertical.1.v_ref, bf16[32,96,512]{2,1,0:T(8,128)(2,1)S(1)} %get-tuple-element.42.p_ref, s32[8,8,512]{2,1,0:T(8,128)S(1)} %get-tuple-element.43.q_ref), custom_call_target="tpu_custom_call" | custom-call | flops 200000000 | bytes 500000 | tf_op jit(solution)/shard_map/stage/pallas_call | solution.py:183
  87.5 0.0 collective-permute-done.13
  87.5 8.4 %collective-permute-start.14 = (f32[128,512]{1,0:T(8,128)S(1)}, f32[128,512]{1,0:T(8,128)S(1)}, u32[]{:S(2)}, u32[]{:S(2)}) collective-permute-start(f32[128,512]{1,0:T(8,128)S(1)} %slice_add_fusion), channel_id=1, source_target_pairs={{0,32},{32,0},{64,96},{96,64},{128,160},{160,128},{192,224},{224,1... | collective-permute-start | bytes 786440 | tf_op jit(solution)/shard_map/ppermute | solution.py:311
  95.9 0.0 collective-permute-done.11
  95.9 1.1 %collective-permute-done.14 = f32[128,512]{1,0:T(8,128)S(1)} collective-permute-done((f32[128,512]{1,0:T(8,128)S(1)}, f32[128,512]{1,0:T(8,128)S(1)}, u32[]{:S(2)}, u32[]{:S(2)}) %collective-permute-start.14) | collective-permute-done | bytes 262176 | tf_op jit(solution)/shard_map/ppermute | solution.py:311
  97.1 0.1 fusion
  97.1 0.9 copy.7
  (9 shorter events, 0.3 us)
Async XLA Ops:
  1.5 18.9 %collective-permute-start = (f32[1,4,8,512]{3,2,1,0:T(8,128)}, f32[1,4,8,512]{3,2,1,0:T(8,128)S(1)}, u32[]{:S(2)}, u32[]{:S(2)}) collective-permute-start(f32[1,4,8,512]{3,2,1,0:T(8,128)} %get-tuple-element.40), channel_id=1, source_target_pairs={{1,0},{2,1},{3,2},{4,3},{5,4},{6,5},{7,6},{8,7},{9,8},{10,9},{11,1... | collective-permute-start | bytes 196616 | tf_op jit(solution)/shard_map/ppermute | solution.py:287
  4.0 16.4 %collective-permute-start.1 = (f32[1,4,8,512]{3,2,1,0:T(8,128)}, f32[1,4,8,512]{3,2,1,0:T(8,128)S(1)}, u32[]{:S(2)}, u32[]{:S(2)}) collective-permute-start(f32[1,4,8,512]{3,2,1,0:T(8,128)} %get-tuple-element.41), channel_id=1, source_target_pairs={{0,1},{1,2},{2,3},{3,4},{4,5},{5,6},{6,7},{7,8},{8,9},{9,10},{10,1... | collective-permute-start | bytes 196616 | tf_op jit(solution)/shard_map/ppermute | solution.py:288
  10.8 1.2 %copy-start.2 = (s32[8,4,16,512]{3,2,1,0:T(8,128)S(1)}, s32[8,4,16,512]{3,2,1,0:T(8,128)}, u32[]{:S(2)}) copy-start(s32[8,4,16,512]{3,2,1,0:T(8,128)} %param.9) | copy-start | bytes 3145732
  12.1 1.0 %copy-start.3 = (bf16[8,4,16,512]{3,2,1,0:T(8,128)(2,1)S(1)}, bf16[8,4,16,512]{3,2,1,0:T(8,128)(2,1)}, u32[]{:S(2)}) copy-start(bf16[8,4,16,512]{3,2,1,0:T(8,128)(2,1)} %param.8) | copy-start | bytes 1572868
  13.1 7.3 %copy-start = (f32[4,4,8,512]{3,2,1,0:T(8,128)S(1)}, f32[4,4,8,512]{3,2,1,0:T(8,128)}, u32[]{:S(2)}) copy-start(f32[4,4,8,512]{3,2,1,0:T(8,128)} %adj_ref.1) | copy-start | bytes 786436
  13.1 7.3 %copy-start.1 = (f32[3,4,8,512]{3,2,1,0:T(8,128)S(1)}, f32[3,4,8,512]{3,2,1,0:T(8,128)}, u32[]{:S(2)}) copy-start(f32[3,4,8,512]{3,2,1,0:T(8,128)} %coef_ref.1) | copy-start | bytes 589828
  21.7 17.0 %collective-permute-start.2 = (f32[72,512]{1,0:T(8,128)S(1)}, f32[72,512]{1,0:T(8,128)S(1)}, u32[]{:S(2)}, u32[]{:S(2)}) collective-permute-start(f32[72,512]{1,0:T(8,128)S(1)} %stage.8), channel_id=1, source_target_pairs={{0,64},{32,736},{64,128},{96,32},{128,192},{160,96},{192,256},{224... | collective-permute-start | bytes 442376 | tf_op jit(solution)/shard_map/ppermute | solution.py:311
  38.7 5.0 %collective-permute-start.3 = (f32[144,512]{1,0:T(8,128)S(1)}, f32[144,512]{1,0:T(8,128)S(1)}, u32[]{:S(2)}, u32[]{:S(2)}) collective-permute-start(f32[144,512]{1,0:T(8,128)S(1)} %get-tuple-element.47), channel_id=1, source_target_pairs={{0,32},{32,0},{64,96},{96,64},{128,160},{160,128},{192,224},{224,1... | collective-permute-start | bytes 884744 | tf_op jit(solution)/shard_map/ppermute | solution.py:311
  43.8 10.0 %collective-permute-start.4 = (f32[216,512]{1,0:T(8,128)S(1)}, f32[216,512]{1,0:T(8,128)S(1)}, u32[]{:S(2)}, u32[]{:S(2)}) collective-permute-start(f32[216,512]{1,0:T(8,128)S(1)} %pad_maximum_fusion), channel_id=1, source_target_pairs={{0,64},{32,736},{64,128},{96,32},{128,192},{160,96},{192,256},{224... | collective-permute-start | bytes 1327112 | tf_op jit(solution)/shard_map/ppermute | solution.py:311
  51.9 10.0 %collective-permute-start.6 = (f32[216,512]{1,0:T(8,128)S(1)}, f32[216,512]{1,0:T(8,128)S(1)}, u32[]{:S(2)}, u32[]{:S(2)}) collective-permute-start(f32[216,512]{1,0:T(8,128)S(1)} %stage.11), channel_id=1, source_target_pairs={{0,32},{32,0},{64,96},{96,64},{128,160},{160,128},{192,224},{224,1... | collective-permute-start | bytes 1327112 | tf_op jit(solution)/shard_map/ppermute | solution.py:311
  54.2 7.8 %collective-permute-start.8 = (f32[128,512]{1,0:T(8,128)S(1)}, f32[128,512]{1,0:T(8,128)S(1)}, u32[]{:S(2)}, u32[]{:S(2)}) collective-permute-start(f32[128,512]{1,0:T(8,128)S(1)} %get-tuple-element.61), channel_id=1, source_target_pairs={{0,64},{32,736},{64,128},{96,32},{128,192},{160,96},{192,256},{224... | collective-permute-start | bytes 786440 | tf_op jit(solution)/shard_map/ppermute | solution.py:311
  58.1 8.4 %collective-permute-start.5 = (f32[128,512]{1,0:T(8,128)S(1)}, f32[128,512]{1,0:T(8,128)S(1)}, u32[]{:S(2)}, u32[]{:S(2)}) collective-permute-start(f32[128,512]{1,0:T(8,128)S(1)} %get-tuple-element.55), channel_id=1, source_target_pairs={{0,64},{32,736},{64,128},{96,32},{128,192},{160,96},{192,256},{224... | collective-permute-start | bytes 786440 | tf_op jit(solution)/shard_map/ppermute | solution.py:311
  62.1 8.8 %collective-permute-start.10 = (f32[128,512]{1,0:T(8,128)S(1)}, f32[128,512]{1,0:T(8,128)S(1)}, u32[]{:S(2)}, u32[]{:S(2)}) collective-permute-start(f32[128,512]{1,0:T(8,128)S(1)} %add.28), channel_id=1, source_target_pairs={{0,64},{32,736},{64,128},{96,32},{128,192},{160,96},{192,256},{224... | collective-permute-start | bytes 786440 | tf_op jit(solution)/shard_map/ppermute | solution.py:311
  66.5 8.3 %collective-permute-start.7 = (f32[128,512]{1,0:T(8,128)S(1)}, f32[128,512]{1,0:T(8,128)S(1)}, u32[]{:S(2)}, u32[]{:S(2)}) collective-permute-start(f32[128,512]{1,0:T(8,128)S(1)} %add.27), channel_id=1, source_target_pairs={{0,64},{32,736},{64,128},{96,32},{128,192},{160,96},{192,256},{224... | collective-permute-start | bytes 786440 | tf_op jit(solution)/shard_map/ppermute | solution.py:311
  70.9 8.3 %collective-permute-start.12 = (f32[128,512]{1,0:T(8,128)S(1)}, f32[128,512]{1,0:T(8,128)S(1)}, u32[]{:S(2)}, u32[]{:S(2)}) collective-permute-start(f32[128,512]{1,0:T(8,128)S(1)} %add.30), channel_id=1, source_target_pairs={{0,64},{32,736},{64,128},{96,32},{128,192},{160,96},{192,256},{224... | collective-permute-start | bytes 786440 | tf_op jit(solution)/shard_map/ppermute | solution.py:311
  74.9 8.3 %collective-permute-start.9 = (f32[128,512]{1,0:T(8,128)S(1)}, f32[128,512]{1,0:T(8,128)S(1)}, u32[]{:S(2)}, u32[]{:S(2)}) collective-permute-start(f32[128,512]{1,0:T(8,128)S(1)} %add.29), channel_id=1, source_target_pairs={{0,64},{32,736},{64,128},{96,32},{128,192},{160,96},{192,256},{224... | collective-permute-start | bytes 786440 | tf_op jit(solution)/shard_map/ppermute | solution.py:311
  79.3 8.2 %collective-permute-start.13 = (f32[128,512]{1,0:T(8,128)S(1)}, f32[128,512]{1,0:T(8,128)S(1)}, u32[]{:S(2)}, u32[]{:S(2)}) collective-permute-start(f32[128,512]{1,0:T(8,128)S(1)} %add.32), channel_id=1, source_target_pairs={{0,64},{32,736},{64,128},{96,32},{128,192},{160,96},{192,256},{224... | collective-permute-start | bytes 786440 | tf_op jit(solution)/shard_map/ppermute | solution.py:311
  83.2 12.7 %collective-permute-start.11 = (f32[128,512]{1,0:T(8,128)S(1)}, f32[128,512]{1,0:T(8,128)S(1)}, u32[]{:S(2)}, u32[]{:S(2)}) collective-permute-start(f32[128,512]{1,0:T(8,128)S(1)} %add.31), channel_id=1, source_target_pairs={{0,64},{32,736},{64,128},{96,32},{128,192},{160,96},{192,256},{224... | collective-permute-start | bytes 786440 | tf_op jit(solution)/shard_map/ppermute | solution.py:311
  87.5 9.5 %collective-permute-start.14 = (f32[128,512]{1,0:T(8,128)S(1)}, f32[128,512]{1,0:T(8,128)S(1)}, u32[]{:S(2)}, u32[]{:S(2)}) collective-permute-start(f32[128,512]{1,0:T(8,128)S(1)} %slice_add_fusion), channel_id=1, source_target_pairs={{0,32},{32,0},{64,96},{96,64},{128,160},{160,128},{192,224},{224,1... | collective-permute-start | bytes 786440 | tf_op jit(solution)/shard_map/ppermute | solution.py:311

commit v5 on v4

--- a/solution.py
+++ b/solution.py
@@ -63,70 +63,53 @@
     lax.fori_loop(0, blk * deps, enter, 0)
 
 
-def place_kernel(chips, deps, pair_ref, w_ref, cols_ref, p_ref, q_ref, table, x_sc, w_sc, count):
-    items, points, cols = cols_ref.shape
+def table_kernel(chips, pair_ref, table, count):
     fill_table(chips, pair_ref, table, count)
-    q_ref[...] = jnp.zeros_like(q_ref)
+
+
+def item_table(chips, dep_owner, dep_slot):
+    entries = sum(stage_sizes(chips // 2))
+    smem = pl.BlockSpec(memory_space=pltpu.SMEM)
+    return pl.pallas_call(
+        functools.partial(table_kernel, chips),
+        in_specs=[smem],
+        out_specs=smem,
+        out_shape=jax.ShapeDtypeStruct((2, entries), jnp.int32),
+        scratch_shapes=[pltpu.SMEM((2 * chips,), jnp.int32)],
+        compiler_params=pltpu.CompilerParams(vmem_limit_bytes=MIB),
+        cost_estimate=pl.CostEstimate(flops=1000000000, bytes_accessed=1000, transcendentals=0),
+        name="table",
+    )(jnp.stack([dep_owner.T, dep_slot.T]))
+
+
+def place_item(w, d, x_sc, w_sc, p_sc):
+    points, cols = d.shape
+    rel = ((d - d[0:1] + cols // 2) & (cols - 1)) - cols // 2
+    low = jnp.min(rel, axis=0, keepdims=True)
+    base = (d[0:1] + low) & (cols - 1)
+    x_sc[...] = (rel - low + (base & (WIN - 1))).astype(jnp.float32)
+    w_sc[...] = w.astype(jnp.float32)
     first = lax.broadcasted_iota(jnp.int32, (TILE, LANES), 0)
     places = [(first + i).astype(jnp.float32).astype(jnp.bfloat16) for i in range(0, SPAN, TILE)]
-
-    def block(a, _):
-        for k in range(deps):
-            item = a * deps + k
-            d = cols_ref[item]
-            rel = ((d - d[0:1] + cols // 2) & (cols - 1)) - cols // 2
-            low = jnp.min(rel, axis=0, keepdims=True)
-            base = (d[0:1] + low) & (cols - 1)
-            x_sc[k] = (rel - low + (base & (WIN - 1))).astype(jnp.float32)
-            w_sc[k] = w_ref[item].astype(jnp.float32)
-            q_ref[a, k:k + 1, :] = base // WIN
-            for t in range(cols // LANES):
-                part = slice(t * LANES, (t + 1) * LANES)
-                acc = [jnp.zeros((TILE, LANES), jnp.bfloat16)] * len(places)
-                for s in range(points):
-                    x = jnp.broadcast_to(x_sc[k, s:s + 1, part], (TILE, LANES)).astype(jnp.bfloat16)
-                    w = jnp.broadcast_to(w_sc[k, s:s + 1, part], (TILE, LANES)).astype(jnp.bfloat16)
-                    acc = [jnp.where(place == x, w, total) for place, total in zip(places, acc)]
-                for i, total in enumerate(acc):
-                    p_ref[item, i * TILE:(i + 1) * TILE, part] = total
-        return 0
-
-    lax.fori_loop(0, items // deps, block, 0)
-
-
-def placed(chips, dep_owner, dep_slot, weight, places):
-    blk, deps = dep_owner.shape
-    items, points, cols = weight.shape
-    entries = sum(stage_sizes(chips // 2))
-    smem = pl.BlockSpec(memory_space=pltpu.SMEM)
-    vmem = pl.BlockSpec(memory_space=pltpu.VMEM)
-    return pl.pallas_call(
-        functools.partial(place_kernel, chips, deps),
-        in_specs=[smem, vmem, vmem],
-        out_specs=[vmem, vmem, smem],
-        out_shape=[
-            jax.ShapeDtypeStruct((items, SPAN, cols), jnp.bfloat16),
-            jax.ShapeDtypeStruct((blk, 8, cols), jnp.int32),
-            jax.ShapeDtypeStruct((2, entries), jnp.int32),
-        ],
-        scratch_shapes=[
-            pltpu.VMEM((deps, points, cols), jnp.float32),
-            pltpu.VMEM((deps, points, cols), jnp.float32),
-            pltpu.SMEM((2 * chips,), jnp.int32),
-        ],
-        compiler_params=pltpu.CompilerParams(vmem_limit_bytes=8 * MIB),
-        cost_estimate=pl.CostEstimate(flops=10000000000, bytes_accessed=5000000, transcendentals=0),
-        name="place",
-    )(jnp.stack([dep_owner.T, dep_slot.T]), weight, places)
-
-
-def item_contribution(v, q, p_ref, index, v_sc):
+    for t in range(cols // LANES):
+        part = slice(t * LANES, (t + 1) * LANES)
+        acc = [jnp.zeros((TILE, LANES), jnp.bfloat16)] * len(places)
+        for s in range(points):
+            x = jnp.broadcast_to(x_sc[s:s + 1, part], (TILE, LANES)).astype(jnp.bfloat16)
+            value = jnp.broadcast_to(w_sc[s:s + 1, part], (TILE, LANES)).astype(jnp.bfloat16)
+            acc = [jnp.where(place == x, value, total) for place, total in zip(places, acc)]
+        for i, total in enumerate(acc):
+            p_sc[i * TILE:(i + 1) * TILE, part] = total
+    return base // WIN
+
+
+def item_contribution(v, q, p_sc, v_sc):
     rows, cols = v.shape
     window = jnp.broadcast_to(q.astype(jnp.float32), (rows, cols)).astype(jnp.bfloat16)
     for i in range(cols // WIN):
         v_sc[i * rows:(i + 1) * rows, :] = jnp.where(window == jnp.bfloat16(i), v, jnp.bfloat16(0))
     u = lax.dot_general(
-        v_sc[...], p_ref[index], (((1,), (1,)), ((), ())), preferred_element_type=jnp.float32
+        v_sc[...], p_sc[...], (((1,), (1,)), ((), ())), preferred_element_type=jnp.float32
     )
     u = jnp.concatenate([u, jnp.zeros((u.shape[0], LANES - SPAN), jnp.float32)], 1)
     lane = lax.broadcasted_iota(jnp.int32, (rows, LANES), 1)
@@ -140,8 +123,8 @@
     ]
 
 
-def stage_kernel(groups, deps, rows, table, v_ref, p_ref, q_ref, *rest):
-    *outs, v_sc = rest
+def stage_kernel(groups, deps, rows, table, v_ref, w_ref, cols_ref, *rest):
+    *outs, v_sc, x_sc, w_sc, p_sc = rest
     cols = v_ref.shape[-1]
     blk = v_ref.shape[0]
     for (firsts, listed), out in zip(groups, outs):
@@ -160,9 +143,8 @@
 
                 @pl.when(index >= 0)
                 def _():
-                    row = lax.div(index, deps)
-                    q = q_ref[row, pl.ds(lax.rem(index, deps), 1), :]
-                    parts = item_contribution(v_ref[row], q, p_ref, index, v_sc)
+                    q = place_item(w_ref[index], cols_ref[index], x_sc, w_sc, p_sc)
+                    parts = item_contribution(v_ref[lax.div(index, deps)], q, p_sc, v_sc)
                     if listed:
                         at = pl.multiple_of(top + n * rows, 8)
                     else:
@@ -176,7 +158,7 @@
             lax.fori_loop(0, 2 * CAP, one, 0)
 
 
-def stage(groups, deps, table, v, p, q):
+def stage(groups, deps, table, v, weight, places):
     blk, rows, cols = v.shape
     heights = [len(firsts) * (2 * CAP * rows + 8) if listed else 2 * blk * rows for firsts, listed in groups]
     vmem = pl.BlockSpec(memory_space=pltpu.VMEM)
@@ -187,13 +169,16 @@
         out_shape=[jax.ShapeDtypeStruct((height, cols), jnp.float32) for height in heights],
         scratch_shapes=[
             pltpu.VMEM((cols // WIN * rows, cols), jnp.bfloat16),
+            pltpu.VMEM(weight.shape[1:], jnp.float32),
+            pltpu.VMEM(weight.shape[1:], jnp.float32),
+            pltpu.VMEM((SPAN, cols), jnp.bfloat16),
         ],
         compiler_params=pltpu.CompilerParams(vmem_limit_bytes=10 * MIB),
         cost_estimate=pl.CostEstimate(
             flops=len(groups) * 200000000, bytes_accessed=500000, transcendentals=0
         ),
         name="stage",
-    )(table, v, p, q)
+    )(table, v, weight, places)
 
 
 def merge_kernel(blk, rows, picks, dense_ref, *refs):
@@ -287,14 +272,9 @@
     after = lax.ppermute(first, "lev", [(i + 1, i) for i in range(levels - 1)])
     before = lax.ppermute(last, "lev", [(i, i + 1) for i in range(levels - 1)])
 
-    p, q, table = placed(
-        chips,
-        dep_owner,
-        dep_slot,
-        stencil_weight.reshape(items, points, cols),
-        stencil_cols.reshape(items, points, cols),
-    )
-
+    table = item_table(chips, dep_owner, dep_slot)
+    weight = stencil_weight.reshape(items, points, cols)
+    places = stencil_cols.reshape(items, points, cols)
     v = vertical(adj_arrival, vert_coef, after, before)
 
     sibling = [(t, t ^ 1) for t in range(tiles)]
@@ -302,7 +282,7 @@
     quad = 2 * CAP
 
     def made(table, *groups):
-        return stage(groups, deps, table, v, p, q)
+        return stage(groups, deps, table, v, weight, places)
 
     def behind(table, value):
         return lax.optimization_barrier((table, value))

time: 98.6 us -> 95.4 us (0.968)
  the two profiles are of different devices: /device:TPU:31 before, /device:TPU:33 now
where the time goes in v5:
time: 95.4 us; the launch traced here: 94.8 us
  starting transfers between devices  61.8 us (65%)
  Pallas kernels  25 us (26%)
  waiting for transfers between devices  6.32 us (7%)
    ppermute x13, starting transfers between devices, onward(): return [lax.ppermute(value, 'tile', pairs) for value in values]  55.6 us
    pallas_call x8, Pallas kernels, stage(): pl.pallas_call(functools.partial(stage_kernel, groups, deps, rows), in_sp...  19.9 us
    ppermute x1, starting transfers between devices, shards(): after = lax.ppermute(first, 'lev', [(i + 1, i) for i in range(levels - 1)])  4.26 us
    ppermute x1, waiting for transfers between devices, shards(): before = lax.ppermute(last, 'lev', [(i, i + 1) for i in range(levels - 1)])  3.69 us
    pallas_call x1, Pallas kernels, item_table(): pl.pallas_call(functools.partial(table_kernel, chips), in_specs=[smem], o...  2.82 us
    ppermute x13, waiting for transfers between devices, onward(): return [lax.ppermute(value, 'tile', pairs) for value in values]  2.62 us
    ppermute x1, starting transfers between devices, shards(): before = lax.ppermute(last, 'lev', [(i, i + 1) for i in range(levels - 1)])  1.92 us
  transfers between devices with their start and end apart: 15, of which 4 were waited for; matrix products, arithmetic and copies ran while one was open for 0% of the time, Pallas kernels for 23%

profile of v5, /device:TPU:33, one launch (start us, length us, event | category | flops | bytes accessed | tf_op | source)
XLA Modules:
  0.0 94.8 jit_solution(9965651640399597193)
XLA Ops:
  0.0 1.5 %edges.1 = (f32[1,4,8,512]{3,2,1,0:T(8,128)}, f32[1,4,8,512]{3,2,1,0:T(8,128)}) custom-call(f32[4,4,8,512]{3,2,1,0:T(8,128)} %adj_ref.1, f32[3,4,8,512]{3,2,1,0:T(8,128)} %coef_ref.1, f32[4,4,8,512]{3,2,1,0:T(8,128)} %adj_ref.1, f32[3,4,8,512]{3,2,1,0:T(8,128)} %coef_ref.1), custom_call_target="tpu_custom_call" | custom-call | tf_op jit(solution)/shard_map/edges/pallas_call | solution.py:223
  1.5 4.3 %collective-permute-start = (f32[1,4,8,512]{3,2,1,0:T(8,128)}, f32[1,4,8,512]{3,2,1,0:T(8,128)S(1)}, u32[]{:S(2)}, u32[]{:S(2)}) collective-permute-start(f32[1,4,8,512]{3,2,1,0:T(8,128)} %get-tuple-element.36), channel_id=1, source_target_pairs={{1,0},{2,1},{3,2},{4,3},{5,4},{6,5},{7,6},{8,7},{9,8},{10,9},{11,1... | collective-permute-start | bytes 196616 | tf_op jit(solution)/shard_map/ppermute | solution.py:272
  5.8 0.0 copy-start.5
  5.8 0.0 copy-start.4
  5.8 1.9 %collective-permute-start.1 = (f32[1,4,8,512]{3,2,1,0:T(8,128)}, f32[1,4,8,512]{3,2,1,0:T(8,128)S(1)}, u32[]{:S(2)}, u32[]{:S(2)}) collective-permute-start(f32[1,4,8,512]{3,2,1,0:T(8,128)} %get-tuple-element.37), channel_id=1, source_target_pairs={{0,1},{1,2},{2,3},{3,4},{4,5},{5,6},{6,7},{7,8},{8,9},{9,10},{10,1... | collective-permute-start | bytes 196616 | tf_op jit(solution)/shard_map/ppermute | solution.py:273
  7.8 0.0 copy-done.5
  7.8 0.0 copy-done.4
  7.8 0.0 copy-start.2
  7.8 0.0 copy-start.3
  7.8 0.0 copy-start
  7.8 2.8 %table.1 = s32[2,48]{1,0:T(2,128)S(1)} custom-call(s32[2,4,8]{2,1,0:T(4,128)S(1)} %pad_add_fusion.pair_ref), custom_call_target="tpu_custom_call" | custom-call | flops 1000000000 | bytes 1000 | tf_op jit(solution)/shard_map/table/pallas_call | solution.py:73
  10.7 0.0 copy-start.1
  10.7 0.0 collective-permute-done.after_ref
  10.7 3.7 %collective-permute-done.1.before_ref = f32[1,4,8,512]{3,2,1,0:T(8,128)S(1)} collective-permute-done((f32[1,4,8,512]{3,2,1,0:T(8,128)}, f32[1,4,8,512]{3,2,1,0:T(8,128)S(1)}, u32[]{:S(2)}, u32[]{:S(2)}) %collective-permute-start.1) | collective-permute-done | bytes 65568 | tf_op jit(solution)/shard_map/ppermute | solution.py:273
  14.4 0.0 copy-done.2
  14.4 0.0 copy-done.3
  14.4 0.1 vertical.1.v_ref
  14.5 0.0 copy-done
  14.5 0.0 copy-done.1
  14.5 1.5 %stage.8 = f32[72,512]{1,0:T(8,128)S(1)} custom-call(s32[2,48]{1,0:T(2,128)S(1)} %table.1, bf16[8,16,512]{2,1,0:T(8,128)(2,1)S(1)} %vertical.1.v_ref, bf16[32,16,512]{2,1,0:T(8,128)(2,1)S(1)} %bitcast.20, s32[32,16,512]{2,1,0:T(8,128)S(1)} %bitcast.12), custom_call_target="tpu_custom_call" | custom-call | flops 200000000 | bytes 500000 | tf_op jit(solution)/shard_map/stage/pallas_call | solution.py:165
  16.0 15.2 %collective-permute-start.2 = (f32[72,512]{1,0:T(8,128)S(1)}, f32[72,512]{1,0:T(8,128)S(1)}, u32[]{:S(2)}, u32[]{:S(2)}) collective-permute-start(f32[72,512]{1,0:T(8,128)S(1)} %stage.8), channel_id=1, source_target_pairs={{0,64},{32,736},{64,128},{96,32},{128,192},{160,96},{192,256},{224... | collective-permute-start | bytes 442376 | tf_op jit(solution)/shard_map/ppermute | solution.py:291
  31.3 4.9 %stage.9 = (f32[72,512]{1,0:T(8,128)S(1)}, f32[144,512]{1,0:T(8,128)S(1)}) custom-call(s32[2,48]{1,0:T(2,128)S(1)} %table.1, bf16[8,16,512]{2,1,0:T(8,128)(2,1)S(1)} %vertical.1.v_ref, bf16[32,16,512]{2,1,0:T(8,128)(2,1)S(1)} %bitcast.21, s32[32,16,512]{2,1,0:T(8,128)S(1)} %bitcast.13), custom_call_target="tpu_custom_call" | custom-call | flops 400000000 | bytes 500000 | tf_op jit(solution)/shard_map/stage/pallas_call | solution.py:165
  36.1 0.0 collective-permute-done.2
  36.2 2.5 %collective-permute-start.3 = (f32[144,512]{1,0:T(8,128)S(1)}, f32[144,512]{1,0:T(8,128)S(1)}, u32[]{:S(2)}, u32[]{:S(2)}) collective-permute-start(f32[144,512]{1,0:T(8,128)S(1)} %get-tuple-element.41), channel_id=1, source_target_pairs={{0,32},{32,0},{64,96},{96,64},{128,160},{160,128},{192,224},{224,1... | collective-permute-start | bytes 884744 | tf_op jit(solution)/shard_map/ppermute | solution.py:291
  38.7 1.2 %collective-permute-done.3.refs_0_ = f32[144,512]{1,0:T(8,128)S(1)} collective-permute-done((f32[144,512]{1,0:T(8,128)S(1)}, f32[144,512]{1,0:T(8,128)S(1)}, u32[]{:S(2)}, u32[]{:S(2)}) %collective-permute-start.3) | collective-permute-done | bytes 294944 | tf_op jit(solution)/shard_map/ppermute | solution.py:291
  39.9 3.6 %collective-permute-start.4 = (f32[216,512]{1,0:T(8,128)S(1)}, f32[216,512]{1,0:T(8,128)S(1)}, u32[]{:S(2)}, u32[]{:S(2)}) collective-permute-start(f32[216,512]{1,0:T(8,128)S(1)} %pad_maximum_fusion), channel_id=1, source_target_pairs={{0,64},{32,736},{64,128},{96,32},{128,192},{160,96},{192,256},{224... | collective-permute-start | bytes 1327112 | tf_op jit(solution)/shard_map/ppermute | solution.py:291
  43.6 2.0 %stage.10.dense_ref = f32[256,512]{1,0:T(8,128)S(1)} custom-call(s32[2,48]{1,0:T(2,128)S(1)} %table.1, bf16[8,16,512]{2,1,0:T(8,128)(2,1)S(1)} %vertical.1.v_ref, bf16[32,16,512]{2,1,0:T(8,128)(2,1)S(1)} %bitcast.22, s32[32,16,512]{2,1,0:T(8,128)S(1)} %bitcast.14), custom_call_target="tpu_custom_call" | custom-call | flops 200000000 | bytes 500000 | tf_op jit(solution)/shard_map/stage/pallas_call | solution.py:165
  45.6 4.4 %stage.11 = f32[216,512]{1,0:T(8,128)S(1)} custom-call(s32[2,48]{1,0:T(2,128)S(1)} %table.1, bf16[8,16,512]{2,1,0:T(8,128)(2,1)S(1)} %vertical.1.v_ref, bf16[32,16,512]{2,1,0:T(8,128)(2,1)S(1)} %bitcast.23, s32[32,16,512]{2,1,0:T(8,128)S(1)} %bitcast.15), custom_call_target="tpu_custom_call" | custom-call | flops 200000000 | bytes 500000 | tf_op jit(solution)/shard_map/stage/pallas_call | solution.py:165
  50.0 1.9 %collective-permute-start.6 = (f32[216,512]{1,0:T(8,128)S(1)}, f32[216,512]{1,0:T(8,128)S(1)}, u32[]{:S(2)}, u32[]{:S(2)}) collective-permute-start(f32[216,512]{1,0:T(8,128)S(1)} %stage.11), channel_id=1, source_target_pairs={{0,32},{32,0},{64,96},{96,64},{128,160},{160,128},{192,224},{224,1... | collective-permute-start | bytes 1327112 | tf_op jit(solution)/shard_map/ppermute | solution.py:291
  51.9 0.0 collective-permute-done.4.refs_1_
  51.9 0.3 merge.4
  52.3 3.0 %collective-permute-start.8 = (f32[128,512]{1,0:T(8,128)S(1)}, f32[128,512]{1,0:T(8,128)S(1)}, u32[]{:S(2)}, u32[]{:S(2)}) collective-permute-start(f32[128,512]{1,0:T(8,128)S(1)} %get-tuple-element.55), channel_id=1, source_target_pairs={{0,64},{32,736},{64,128},{96,32},{128,192},{160,96},{192,256},{224... | collective-permute-start | bytes 786440 | tf_op jit(solution)/shard_map/ppermute | solution.py:291
  55.3 2.4 %collective-permute-start.5 = (f32[128,512]{1,0:T(8,128)S(1)}, f32[128,512]{1,0:T(8,128)S(1)}, u32[]{:S(2)}, u32[]{:S(2)}) collective-permute-start(f32[128,512]{1,0:T(8,128)S(1)} %get-tuple-element.49), channel_id=1, source_target_pairs={{0,64},{32,736},{64,128},{96,32},{128,192},{160,96},{192,256},{224... | collective-permute-start | bytes 786440 | tf_op jit(solution)/shard_map/ppermute | solution.py:291
  57.8 1.5 %stage.12.dense_ref = f32[256,512]{1,0:T(8,128)S(1)} custom-call(s32[2,48]{1,0:T(2,128)S(1)} %table.1, bf16[8,16,512]{2,1,0:T(8,128)(2,1)S(1)} %vertical.1.v_ref, bf16[32,16,512]{2,1,0:T(8,128)(2,1)S(1)} %bitcast.24, s32[32,16,512]{2,1,0:T(8,128)S(1)} %bitcast.16), custom_call_target="tpu_custom_call" | custom-call | flops 200000000 | bytes 500000 | tf_op jit(solution)/shard_map/stage/pallas_call | solution.py:165
  59.3 0.0 collective-permute-done.6.refs_0_
  59.3 0.1 merge.5
  59.4 0.3 collective-permute-done.8
  59.7 3.9 %collective-permute-start.10 = (f32[128,512]{1,0:T(8,128)S(1)}, f32[128,512]{1,0:T(8,128)S(1)}, u32[]{:S(2)}, u32[]{:S(2)}) collective-permute-start(f32[128,512]{1,0:T(8,128)S(1)} %add.28), channel_id=1, source_target_pairs={{0,64},{32,736},{64,128},{96,32},{128,192},{160,96},{192,256},{224... | collective-permute-start | bytes 786440 | tf_op jit(solution)/shard_map/ppermute | solution.py:291
  63.7 0.0 collective-permute-done.5
  63.7 2.7 %collective-permute-start.7 = (f32[128,512]{1,0:T(8,128)S(1)}, f32[128,512]{1,0:T(8,128)S(1)}, u32[]{:S(2)}, u32[]{:S(2)}) collective-permute-start(f32[128,512]{1,0:T(8,128)S(1)} %add.27), channel_id=1, source_target_pairs={{0,64},{32,736},{64,128},{96,32},{128,192},{160,96},{192,256},{224... | collective-permute-start | bytes 786440 | tf_op jit(solution)/shard_map/ppermute | solution.py:291
  66.5 1.5 %stage.13.dense_ref = f32[256,512]{1,0:T(8,128)S(1)} custom-call(s32[2,48]{1,0:T(2,128)S(1)} %table.1, bf16[8,16,512]{2,1,0:T(8,128)(2,1)S(1)} %vertical.1.v_ref, bf16[32,16,512]{2,1,0:T(8,128)(2,1)S(1)} %bitcast.25, s32[32,16,512]{2,1,0:T(8,128)S(1)} %bitcast.17), custom_call_target="tpu_custom_call" | custom-call | flops 200000000 | bytes 500000 | tf_op jit(solution)/shard_map/stage/pallas_call | solution.py:165
  68.0 0.1 merge.6
  68.1 0.0 collective-permute-done.10
  68.2 3.8 %collective-permute-start.12 = (f32[128,512]{1,0:T(8,128)S(1)}, f32[128,512]{1,0:T(8,128)S(1)}, u32[]{:S(2)}, u32[]{:S(2)}) collective-permute-start(f32[128,512]{1,0:T(8,128)S(1)} %add.30), channel_id=1, source_target_pairs={{0,64},{32,736},{64,128},{96,32},{128,192},{160,96},{192,256},{224... | collective-permute-start | bytes 786440 | tf_op jit(solution)/shard_map/ppermute | solution.py:291
  72.0 0.0 collective-permute-done.7
  72.1 2.7 %collective-permute-start.9 = (f32[128,512]{1,0:T(8,128)S(1)}, f32[128,512]{1,0:T(8,128)S(1)}, u32[]{:S(2)}, u32[]{:S(2)}) collective-permute-start(f32[128,512]{1,0:T(8,128)S(1)} %add.29), channel_id=1, source_target_pairs={{0,64},{32,736},{64,128},{96,32},{128,192},{160,96},{192,256},{224... | collective-permute-start | bytes 786440 | tf_op jit(solution)/shard_map/ppermute | solution.py:291
  74.9 2.0 %stage.14.dense_ref = f32[256,512]{1,0:T(8,128)S(1)} custom-call(s32[2,48]{1,0:T(2,128)S(1)} %table.1, bf16[8,16,512]{2,1,0:T(8,128)(2,1)S(1)} %vertical.1.v_ref, bf16[32,16,512]{2,1,0:T(8,128)(2,1)S(1)} %bitcast.26, s32[32,16,512]{2,1,0:T(8,128)S(1)} %bitcast.18), custom_call_target="tpu_custom_call" | custom-call | flops 200000000 | bytes 500000 | tf_op jit(solution)/shard_map/stage/pallas_call | solution.py:165
  76.9 0.1 merge.7
  77.0 0.0 collective-permute-done.12
  77.0 3.4 %collective-permute-start.13 = (f32[128,512]{1,0:T(8,128)S(1)}, f32[128,512]{1,0:T(8,128)S(1)}, u32[]{:S(2)}, u32[]{:S(2)}) collective-permute-start(f32[128,512]{1,0:T(8,128)S(1)} %add.32), channel_id=1, source_target_pairs={{0,64},{32,736},{64,128},{96,32},{128,192},{160,96},{192,256},{224... | collective-permute-start | bytes 786440 | tf_op jit(solution)/shard_map/ppermute | solution.py:291
  80.4 0.0 collective-permute-done.9
  80.5 2.7 %collective-permute-start.11 = (f32[128,512]{1,0:T(8,128)S(1)}, f32[128,512]{1,0:T(8,128)S(1)}, u32[]{:S(2)}, u32[]{:S(2)}) collective-permute-start(f32[128,512]{1,0:T(8,128)S(1)} %add.31), channel_id=1, source_target_pairs={{0,64},{32,736},{64,128},{96,32},{128,192},{160,96},{192,256},{224... | collective-permute-start | bytes 786440 | tf_op jit(solution)/shard_map/ppermute | solution.py:291
  83.2 2.0 %stage.15 = f32[256,512]{1,0:T(8,128)S(1)} custom-call(s32[2,48]{1,0:T(2,128)S(1)} %table.1, bf16[8,16,512]{2,1,0:T(8,128)(2,1)S(1)} %vertical.1.v_ref, bf16[32,16,512]{2,1,0:T(8,128)(2,1)S(1)} %bitcast.27, s32[32,16,512]{2,1,0:T(8,128)S(1)} %bitcast.19), custom_call_target="tpu_custom_call" | custom-call | flops 200000000 | bytes 500000 | tf_op jit(solution)/shard_map/stage/pallas_call | solution.py:165
  85.2 0.0 collective-permute-done.13
  85.3 7.5 %collective-permute-start.14 = (f32[128,512]{1,0:T(8,128)S(1)}, f32[128,512]{1,0:T(8,128)S(1)}, u32[]{:S(2)}, u32[]{:S(2)}) collective-permute-start(f32[128,512]{1,0:T(8,128)S(1)} %slice_add_fusion), channel_id=1, source_target_pairs={{0,32},{32,0},{64,96},{96,64},{128,160},{160,128},{192,224},{224,1... | collective-permute-start | bytes 786440 | tf_op jit(solution)/shard_map/ppermute | solution.py:291
  92.8 0.0 collective-permute-done.11
  92.8 1.1 %collective-permute-done.14 = f32[128,512]{1,0:T(8,128)S(1)} collective-permute-done((f32[128,512]{1,0:T(8,128)S(1)}, f32[128,512]{1,0:T(8,128)S(1)}, u32[]{:S(2)}, u32[]{:S(2)}) %collective-permute-start.14) | collective-permute-done | bytes 262176 | tf_op jit(solution)/shard_map/ppermute | solution.py:291
  93.9 0.1 fusion
  94.0 0.9 copy.7
  (10 shorter events, 0.3 us)
Async XLA Ops:
  1.5 9.1 %collective-permute-start = (f32[1,4,8,512]{3,2,1,0:T(8,128)}, f32[1,4,8,512]{3,2,1,0:T(8,128)S(1)}, u32[]{:S(2)}, u32[]{:S(2)}) collective-permute-start(f32[1,4,8,512]{3,2,1,0:T(8,128)} %get-tuple-element.36), channel_id=1, source_target_pairs={{1,0},{2,1},{3,2},{4,3},{5,4},{6,5},{7,6},{8,7},{9,8},{10,9},{11,1... | collective-permute-start | bytes 196616 | tf_op jit(solution)/shard_map/ppermute | solution.py:272
  5.8 2.0 %copy-start.5 = (s32[8,4]{0,1:T(4,128)S(1)}, s32[8,4]{0,1:T(4,128)}, u32[]{:S(2)}) copy-start(s32[8,4]{0,1:T(4,128)} %param.10) | copy-start | bytes 388
  5.8 2.0 %copy-start.4 = (s32[8,4]{0,1:T(4,128)S(1)}, s32[8,4]{0,1:T(4,128)}, u32[]{:S(2)}) copy-start(s32[8,4]{0,1:T(4,128)} %param.11) | copy-start | bytes 388
  5.8 8.5 %collective-permute-start.1 = (f32[1,4,8,512]{3,2,1,0:T(8,128)}, f32[1,4,8,512]{3,2,1,0:T(8,128)S(1)}, u32[]{:S(2)}, u32[]{:S(2)}) collective-permute-start(f32[1,4,8,512]{3,2,1,0:T(8,128)} %get-tuple-element.37), channel_id=1, source_target_pairs={{0,1},{1,2},{2,3},{3,4},{4,5},{5,6},{6,7},{7,8},{8,9},{9,10},{10,1... | collective-permute-start | bytes 196616 | tf_op jit(solution)/shard_map/ppermute | solution.py:273
  7.8 6.6 %copy-start.2 = (f32[4,4,8,512]{3,2,1,0:T(8,128)S(1)}, f32[4,4,8,512]{3,2,1,0:T(8,128)}, u32[]{:S(2)}) copy-start(f32[4,4,8,512]{3,2,1,0:T(8,128)} %adj_ref.1) | copy-start | bytes 786436
  7.8 6.6 %copy-start.3 = (f32[3,4,8,512]{3,2,1,0:T(8,128)S(1)}, f32[3,4,8,512]{3,2,1,0:T(8,128)}, u32[]{:S(2)}) copy-start(f32[3,4,8,512]{3,2,1,0:T(8,128)} %coef_ref.1) | copy-start | bytes 589828
  7.8 6.7 %copy-start = (s32[8,4,16,512]{3,2,1,0:T(8,128)S(1)}, s32[8,4,16,512]{3,2,1,0:T(8,128)}, u32[]{:S(2)}) copy-start(s32[8,4,16,512]{3,2,1,0:T(8,128)} %param.9) | copy-start | bytes 3145732
  10.7 3.8 %copy-start.1 = (bf16[8,4,16,512]{3,2,1,0:T(8,128)(2,1)S(1)}, bf16[8,4,16,512]{3,2,1,0:T(8,128)(2,1)}, u32[]{:S(2)}) copy-start(bf16[8,4,16,512]{3,2,1,0:T(8,128)(2,1)} %param.8) | copy-start | bytes 1572868
  16.0 20.1 %collective-permute-start.2 = (f32[72,512]{1,0:T(8,128)S(1)}, f32[72,512]{1,0:T(8,128)S(1)}, u32[]{:S(2)}, u32[]{:S(2)}) collective-permute-start(f32[72,512]{1,0:T(8,128)S(1)} %stage.8), channel_id=1, source_target_pairs={{0,64},{32,736},{64,128},{96,32},{128,192},{160,96},{192,256},{224... | collective-permute-start | bytes 442376 | tf_op jit(solution)/shard_map/ppermute | solution.py:291
  36.2 3.7 %collective-permute-start.3 = (f32[144,512]{1,0:T(8,128)S(1)}, f32[144,512]{1,0:T(8,128)S(1)}, u32[]{:S(2)}, u32[]{:S(2)}) collective-permute-start(f32[144,512]{1,0:T(8,128)S(1)} %get-tuple-element.41), channel_id=1, source_target_pairs={{0,32},{32,0},{64,96},{96,64},{128,160},{160,128},{192,224},{224,1... | collective-permute-start | bytes 884744 | tf_op jit(solution)/shard_map/ppermute | solution.py:291
  39.9 12.0 %collective-permute-start.4 = (f32[216,512]{1,0:T(8,128)S(1)}, f32[216,512]{1,0:T(8,128)S(1)}, u32[]{:S(2)}, u32[]{:S(2)}) collective-permute-start(f32[216,512]{1,0:T(8,128)S(1)} %pad_maximum_fusion), channel_id=1, source_target_pairs={{0,64},{32,736},{64,128},{96,32},{128,192},{160,96},{192,256},{224... | collective-permute-start | bytes 1327112 | tf_op jit(solution)/shard_map/ppermute | solution.py:291
  50.0 9.3 %collective-permute-start.6 = (f32[216,512]{1,0:T(8,128)S(1)}, f32[216,512]{1,0:T(8,128)S(1)}, u32[]{:S(2)}, u32[]{:S(2)}) collective-permute-start(f32[216,512]{1,0:T(8,128)S(1)} %stage.11), channel_id=1, source_target_pairs={{0,32},{32,0},{64,96},{96,64},{128,160},{160,128},{192,224},{224,1... | collective-permute-start | bytes 1327112 | tf_op jit(solution)/shard_map/ppermute | solution.py:291
  52.3 7.4 %collective-permute-start.8 = (f32[128,512]{1,0:T(8,128)S(1)}, f32[128,512]{1,0:T(8,128)S(1)}, u32[]{:S(2)}, u32[]{:S(2)}) collective-permute-start(f32[128,512]{1,0:T(8,128)S(1)} %get-tuple-element.55), channel_id=1, source_target_pairs={{0,64},{32,736},{64,128},{96,32},{128,192},{160,96},{192,256},{224... | collective-permute-start | bytes 786440 | tf_op jit(solution)/shard_map/ppermute | solution.py:291
  55.3 8.4 %collective-permute-start.5 = (f32[128,512]{1,0:T(8,128)S(1)}, f32[128,512]{1,0:T(8,128)S(1)}, u32[]{:S(2)}, u32[]{:S(2)}) collective-permute-start(f32[128,512]{1,0:T(8,128)S(1)} %get-tuple-element.49), channel_id=1, source_target_pairs={{0,64},{32,736},{64,128},{96,32},{128,192},{160,96},{192,256},{224... | collective-permute-start | bytes 786440 | tf_op jit(solution)/shard_map/ppermute | solution.py:291
  59.7 8.4 %collective-permute-start.10 = (f32[128,512]{1,0:T(8,128)S(1)}, f32[128,512]{1,0:T(8,128)S(1)}, u32[]{:S(2)}, u32[]{:S(2)}) collective-permute-start(f32[128,512]{1,0:T(8,128)S(1)} %add.28), channel_id=1, source_target_pairs={{0,64},{32,736},{64,128},{96,32},{128,192},{160,96},{192,256},{224... | collective-permute-start | bytes 786440 | tf_op jit(solution)/shard_map/ppermute | solution.py:291
  63.7 8.3 %collective-permute-start.7 = (f32[128,512]{1,0:T(8,128)S(1)}, f32[128,512]{1,0:T(8,128)S(1)}, u32[]{:S(2)}, u32[]{:S(2)}) collective-permute-start(f32[128,512]{1,0:T(8,128)S(1)} %add.27), channel_id=1, source_target_pairs={{0,64},{32,736},{64,128},{96,32},{128,192},{160,96},{192,256},{224... | collective-permute-start | bytes 786440 | tf_op jit(solution)/shard_map/ppermute | solution.py:291
  68.2 8.8 %collective-permute-start.12 = (f32[128,512]{1,0:T(8,128)S(1)}, f32[128,512]{1,0:T(8,128)S(1)}, u32[]{:S(2)}, u32[]{:S(2)}) collective-permute-start(f32[128,512]{1,0:T(8,128)S(1)} %add.30), channel_id=1, source_target_pairs={{0,64},{32,736},{64,128},{96,32},{128,192},{160,96},{192,256},{224... | collective-permute-start | bytes 786440 | tf_op jit(solution)/shard_map/ppermute | solution.py:291
  72.1 8.3 %collective-permute-start.9 = (f32[128,512]{1,0:T(8,128)S(1)}, f32[128,512]{1,0:T(8,128)S(1)}, u32[]{:S(2)}, u32[]{:S(2)}) collective-permute-start(f32[128,512]{1,0:T(8,128)S(1)} %add.29), channel_id=1, source_target_pairs={{0,64},{32,736},{64,128},{96,32},{128,192},{160,96},{192,256},{224... | collective-permute-start | bytes 786440 | tf_op jit(solution)/shard_map/ppermute | solution.py:291
  77.0 8.2 %collective-permute-start.13 = (f32[128,512]{1,0:T(8,128)S(1)}, f32[128,512]{1,0:T(8,128)S(1)}, u32[]{:S(2)}, u32[]{:S(2)}) collective-permute-start(f32[128,512]{1,0:T(8,128)S(1)} %add.32), channel_id=1, source_target_pairs={{0,64},{32,736},{64,128},{96,32},{128,192},{160,96},{192,256},{224... | collective-permute-start | bytes 786440 | tf_op jit(solution)/shard_map/ppermute | solution.py:291
  80.5 12.3 %collective-permute-start.11 = (f32[128,512]{1,0:T(8,128)S(1)}, f32[128,512]{1,0:T(8,128)S(1)}, u32[]{:S(2)}, u32[]{:S(2)}) collective-permute-start(f32[128,512]{1,0:T(8,128)S(1)} %add.31), channel_id=1, source_target_pairs={{0,64},{32,736},{64,128},{96,32},{128,192},{160,96},{192,256},{224... | collective-permute-start | bytes 786440 | tf_op jit(solution)/shard_map/ppermute | solution.py:291
  85.3 8.6 %collective-permute-start.14 = (f32[128,512]{1,0:T(8,128)S(1)}, f32[128,512]{1,0:T(8,128)S(1)}, u32[]{:S(2)}, u32[]{:S(2)}) collective-permute-start(f32[128,512]{1,0:T(8,128)S(1)} %slice_add_fusion), channel_id=1, source_target_pairs={{0,32},{32,0},{64,96},{96,64},{128,160},{160,128},{192,224},{224,1... | collective-permute-start | bytes 786440 | tf_op jit(solution)/shard_map/ppermute | solution.py:291

commit v6 on v5

--- a/solution.py
+++ b/solution.py
@@ -27,18 +27,11 @@
     ahead = 1 - 2 * core
     entries = sum(stage_sizes(far))
 
-    def clear(n, _):
+    for n in range(entries):
         table[0, n] = jnp.int32(-1)
         table[1, n] = jnp.int32(0)
-        return 0
-
-    lax.fori_loop(0, entries, clear, 0)
-
-    def reset(n, _):
+    for n in range(2 * chips):
         count[n] = jnp.int32(0)
-        return 0
-
-    lax.fori_loop(0, 2 * chips, reset, 0)
 
     def enter(n, _):
         row, k = lax.div(n, deps), lax.rem(n, deps)
@@ -103,13 +96,47 @@
     return base // WIN
 
 
-def item_contribution(v, q, p_sc, v_sc):
+def place_kernel(slots, table, w_ref, cols_ref, p_ref, q_ref, x_sc, w_sc):
+    def one(n, _):
+        index = table[0, n]
+
+        @pl.when(index >= 0)
+        def _():
+            q_ref[n, 0:1, :] = place_item(w_ref[index], cols_ref[index], x_sc, w_sc, p_ref.at[n])
+
+        return 0
+
+    lax.fori_loop(0, slots, one, 0)
+
+
+def placed(slots, table, weight, places):
+    points, cols = weight.shape[1:]
+    vmem = pl.BlockSpec(memory_space=pltpu.VMEM)
+    return pl.pallas_call(
+        functools.partial(place_kernel, slots),
+        in_specs=[pl.BlockSpec(memory_space=pltpu.SMEM), vmem, vmem],
+        out_specs=[vmem, vmem],
+        out_shape=[
+            jax.ShapeDtypeStruct((slots, SPAN, cols), jnp.bfloat16),
+            jax.ShapeDtypeStruct((slots, 8, cols), jnp.int32),
+        ],
+        scratch_shapes=[
+            pltpu.VMEM((points, cols), jnp.float32),
+            pltpu.VMEM((points, cols), jnp.float32),
+        ],
+        compiler_params=pltpu.CompilerParams(vmem_limit_bytes=8 * MIB),
+        cost_estimate=pl.CostEstimate(flops=3000000000, bytes_accessed=1000, transcendentals=0),
+        name="place",
+    )(table, weight, places)
+
+
+def item_contribution(v, q, p_ref, v_sc):
     rows, cols = v.shape
     window = jnp.broadcast_to(q.astype(jnp.float32), (rows, cols)).astype(jnp.bfloat16)
     for i in range(cols // WIN):
         v_sc[i * rows:(i + 1) * rows, :] = jnp.where(window == jnp.bfloat16(i), v, jnp.bfloat16(0))
     u = lax.dot_general(
-        v_sc[...], p_sc[...], (((1,), (1,)), ((), ())), preferred_element_type=jnp.float32
+        v_sc[...], p_ref[...], (((1,), (1,)), ((), ())), preferred_element_type=jnp.float32
     )
     u = jnp.concatenate([u, jnp.zeros((u.shape[0], LANES - SPAN), jnp.float32)], 1)
     lane = lax.broadcasted_iota(jnp.int32, (rows, LANES), 1)
@@ -123,8 +150,8 @@
     ]
 
 
-def stage_kernel(groups, deps, rows, table, v_ref, w_ref, cols_ref, *rest):
-    *outs, v_sc, x_sc, w_sc, p_sc = rest
+def stage_kernel(groups, deps, rows, ready, table, v_ref, w_ref, cols_ref, *rest):
+    outs, v_sc, places = rest[:len(groups)], rest[len(groups)], rest[len(groups) + 1:]
     cols = v_ref.shape[-1]
     blk = v_ref.shape[0]
     for (firsts, listed), out in zip(groups, outs):
@@ -143,8 +170,12 @@
 
                 @pl.when(index >= 0)
                 def _():
-                    q = place_item(w_ref[index], cols_ref[index], x_sc, w_sc, p_sc)
-                    parts = item_contribution(v_ref[lax.div(index, deps)], q, p_sc, v_sc)
+                    if ready:
+                        p, q = w_ref.at[first + n], cols_ref[first + n, 0:1, :]
+                    else:
+                        x_sc, w_sc, p = places
+                        q = place_item(w_ref[index], cols_ref[index], x_sc, w_sc, p)
+                    parts = item_contribution(v_ref[lax.div(index, deps)], q, p, v_sc)
                     if listed:
                         at = pl.multiple_of(top + n * rows, 8)
                     else:
@@ -158,21 +189,22 @@
             lax.fori_loop(0, 2 * CAP, one, 0)
 
 
-def stage(groups, deps, table, v, weight, places):
+def stage(groups, deps, ready, table, v, weight, places):
     blk, rows, cols = v.shape
     heights = [len(firsts) * (2 * CAP * rows + 8) if listed else 2 * blk * rows for firsts, listed in groups]
     vmem = pl.BlockSpec(memory_space=pltpu.VMEM)
     return pl.pallas_call(
-        functools.partial(stage_kernel, groups, deps, rows),
+        functools.partial(stage_kernel, groups, deps, rows, ready),
         in_specs=[pl.BlockSpec(memory_space=pltpu.SMEM), vmem, vmem, vmem],
         out_specs=[vmem] * len(groups),
         out_shape=[jax.ShapeDtypeStruct((height, cols), jnp.float32) for height in heights],
         scratch_shapes=[
             pltpu.VMEM((cols // WIN * rows, cols), jnp.bfloat16),
+        ] + ([] if ready else [
             pltpu.VMEM(weight.shape[1:], jnp.float32),
             pltpu.VMEM(weight.shape[1:], jnp.float32),
             pltpu.VMEM((SPAN, cols), jnp.bfloat16),
-        ],
+        ]),
         compiler_params=pltpu.CompilerParams(vmem_limit_bytes=10 * MIB),
         cost_estimate=pl.CostEstimate(
             flops=len(groups) * 200000000, bytes_accessed=500000, transcendentals=0
@@ -275,6 +307,8 @@
     table = item_table(chips, dep_owner, dep_slot)
     weight = stencil_weight.reshape(items, points, cols)
     places = stencil_cols.reshape(items, points, cols)
+    early = 5 * 2 * CAP
+    p, q = placed(early, table, weight, places)
     v = vertical(adj_arrival, vert_coef, after, before)
 
     sibling = [(t, t ^ 1) for t in range(tiles)]
@@ -282,7 +316,8 @@
     quad = 2 * CAP
 
     def made(table, *groups):
-        return stage(groups, deps, table, v, weight, places)
+        ready = max(first for firsts, _ in groups for first in firsts) < early
+        return stage(groups, deps, ready, table, v, *((p, q) if ready else (weight, places)))
 
     def behind(table, value):
         return lax.optimization_barrier((table, value))
@@ -300,7 +335,9 @@
     table, listed = behind(table, listed)
     (farthest,) = onward([listed], ring)
     near = far - 2
-    own, others = made(table, ((own_at(far - 1),), True), ((other_at(far - 1), other_at(near)), True))
+    (others,) = made(table, ((other_at(far - 1), other_at(near)), True))
+    table, others = behind(table, others)
+    (own,) = made(table, ((own_at(far - 1),), True))
     others, farthest = lax.optimization_barrier((others, farthest))
     (given,) = onward([others], sibling)
     table, given = behind(table, given)

time: 95.4 us -> 94.8 us (level)
  the two profiles are of different devices: /device:TPU:33 before, /device:TPU:31 now
where the time goes in v6:
time: 94.8 us; the launch traced here: 94.2 us
  starting transfers between devices  64.7 us (68%)
  Pallas kernels  25.6 us (27%)
  waiting for transfers between devices  1.47 us (2%)
  other arithmetic  1.06 us (1%)
    ppermute x13, starting transfers between devices, onward(): return [lax.ppermute(value, 'tile', pairs) for value in values]  56 us
    pallas_call x9, Pallas kernels, stage(): pl.pallas_call(functools.partial(stage_kernel, groups, deps, rows, ready)...  18.4 us
    ppermute x1, starting transfers between devices, shards(): before = lax.ppermute(last, 'lev', [(i, i + 1) for i in range(levels - 1)])  6.15 us
    ppermute x1, starting transfers between devices, shards(): after = lax.ppermute(first, 'lev', [(i + 1, i) for i in range(levels - 1)])  2.58 us
    pallas_call x1, Pallas kernels, placed(): pl.pallas_call(functools.partial(place_kernel, slots), in_specs=[pl.Block...  2.57 us
    pallas_call x1, Pallas kernels, item_table(): pl.pallas_call(functools.partial(table_kernel, chips), in_specs=[smem], o...  2.34 us
  transfers between devices with their start and end apart: 15, of which 2 were waited for; matrix products, arithmetic and copies ran while one was open for 1% of the time, Pallas kernels for 24%

profile of v6, /device:TPU:31, one launch (start us, length us, event | category | flops | bytes accessed | tf_op | source)
XLA Modules:
  0.0 94.2 jit_solution(3023992637193318480)
XLA Ops:
  0.0 1.5 %edges.1 = (f32[1,4,8,512]{3,2,1,0:T(8,128)}, f32[1,4,8,512]{3,2,1,0:T(8,128)}) custom-call(f32[4,4,8,512]{3,2,1,0:T(8,128)} %adj_ref.1, f32[3,4,8,512]{3,2,1,0:T(8,128)} %coef_ref.1, f32[4,4,8,512]{3,2,1,0:T(8,128)} %adj_ref.1, f32[3,4,8,512]{3,2,1,0:T(8,128)} %coef_ref.1), custom_call_target="tpu_custom_call" | custom-call | tf_op jit(solution)/shard_map/edges/pallas_call | solution.py:255
  1.5 0.0 copy-start
  1.5 0.0 copy-start.1
  1.5 2.6 %collective-permute-start = (f32[1,4,8,512]{3,2,1,0:T(8,128)}, f32[1,4,8,512]{3,2,1,0:T(8,128)S(1)}, u32[]{:S(2)}, u32[]{:S(2)}) collective-permute-start(f32[1,4,8,512]{3,2,1,0:T(8,128)} %get-tuple-element.38), channel_id=1, source_target_pairs={{1,0},{2,1},{3,2},{4,3},{5,4},{6,5},{7,6},{8,7},{9,8},{10,9},{11,1... | collective-permute-start | bytes 196616 | tf_op jit(solution)/shard_map/ppermute | solution.py:304
  4.1 6.1 %collective-permute-start.1 = (f32[1,4,8,512]{3,2,1,0:T(8,128)}, f32[1,4,8,512]{3,2,1,0:T(8,128)S(1)}, u32[]{:S(2)}, u32[]{:S(2)}) collective-permute-start(f32[1,4,8,512]{3,2,1,0:T(8,128)} %get-tuple-element.39), channel_id=1, source_target_pairs={{0,1},{1,2},{2,3},{3,4},{4,5},{5,6},{6,7},{7,8},{8,9},{9,10},{10,1... | collective-permute-start | bytes 196616 | tf_op jit(solution)/shard_map/ppermute | solution.py:305
  10.3 0.7 pad_add_fusion.pair_ref
  11.0 2.3 %table.1 = s32[2,48]{1,0:T(2,128)S(1)} custom-call(s32[2,4,8]{2,1,0:T(4,128)S(1)} %pad_add_fusion.pair_ref), custom_call_target="tpu_custom_call" | custom-call | flops 1000000000 | bytes 1000 | tf_op jit(solution)/shard_map/table/pallas_call | solution.py:66
  13.3 0.0 copy-done
  13.3 0.0 copy-done.1
  13.4 0.0 copy-start.2
  13.4 0.0 copy-start.3
  13.4 2.6 %place.1 = (bf16[20,96,512]{2,1,0:T(8,128)(2,1)S(1)}, s32[20,8,512]{2,1,0:T(8,128)S(1)}) custom-call(s32[2,48]{1,0:T(2,128)S(1)} %table.1, bf16[32,16,512]{2,1,0:T(8,128)(2,1)S(1)} %bitcast.18, s32[32,16,512]{2,1,0:T(8,128)S(1)} %bitcast.12), custom_call_target="tpu_custom_call" | custom-call | flops 3000000000 | bytes 1000 | tf_op jit(solution)/shard_map/place/pallas_call | solution.py:115
  16.0 0.0 collective-permute-done.after_ref
  16.0 0.0 collective-permute-done.1.before_ref
  16.0 0.0 copy-done.2
  16.0 0.0 copy-done.3
  16.0 0.1 vertical.1.v_ref
  16.1 1.2 %stage.9 = f32[72,512]{1,0:T(8,128)S(1)} custom-call(s32[2,48]{1,0:T(2,128)S(1)} %table.1, bf16[8,16,512]{2,1,0:T(8,128)(2,1)S(1)} %vertical.1.v_ref, bf16[20,96,512]{2,1,0:T(8,128)(2,1)S(1)} %get-tuple-element.40.w_ref, s32[20,8,512]{2,1,0:T(8,128)S(1)} %get-tuple-element.41.cols_ref), custom_call_target="tpu_custom_call" | custom-call | flops 200000000 | bytes 500000 | tf_op jit(solution)/shard_map/stage/pallas_call | solution.py:196
  17.3 14.3 %collective-permute-start.2 = (f32[72,512]{1,0:T(8,128)S(1)}, f32[72,512]{1,0:T(8,128)S(1)}, u32[]{:S(2)}, u32[]{:S(2)}) collective-permute-start(f32[72,512]{1,0:T(8,128)S(1)} %stage.9), channel_id=1, source_target_pairs={{0,64},{32,736},{64,128},{96,32},{128,192},{160,96},{192,256},{224... | collective-permute-start | bytes 442376 | tf_op jit(solution)/shard_map/ppermute | solution.py:326
  31.6 1.8 %stage.10 = f32[144,512]{1,0:T(8,128)S(1)} custom-call(s32[2,48]{1,0:T(2,128)S(1)} %table.1, bf16[8,16,512]{2,1,0:T(8,128)(2,1)S(1)} %vertical.1.v_ref, bf16[20,96,512]{2,1,0:T(8,128)(2,1)S(1)} %get-tuple-element.40.w_ref, s32[20,8,512]{2,1,0:T(8,128)S(1)} %get-tuple-element.41.cols_ref), custom_call_target="tpu_custom_call" | custom-call | flops 200000000 | bytes 500000 | tf_op jit(solution)/shard_map/stage/pallas_call | solution.py:196
  33.4 0.3 collective-permute-done.2
  33.7 4.4 %collective-permute-start.3 = (f32[144,512]{1,0:T(8,128)S(1)}, f32[144,512]{1,0:T(8,128)S(1)}, u32[]{:S(2)}, u32[]{:S(2)}) collective-permute-start(f32[144,512]{1,0:T(8,128)S(1)} %stage.10), channel_id=1, source_target_pairs={{0,32},{32,0},{64,96},{96,64},{128,160},{160,128},{192,224},{224,1... | collective-permute-start | bytes 884744 | tf_op jit(solution)/shard_map/ppermute | solution.py:326
  38.1 1.2 %stage.13 = f32[72,512]{1,0:T(8,128)S(1)} custom-call(s32[2,48]{1,0:T(2,128)S(1)} %table.1, bf16[8,16,512]{2,1,0:T(8,128)(2,1)S(1)} %vertical.1.v_ref, bf16[20,96,512]{2,1,0:T(8,128)(2,1)S(1)} %get-tuple-element.40.w_ref, s32[20,8,512]{2,1,0:T(8,128)S(1)} %get-tuple-element.41.cols_ref), custom_call_target="tpu_custom_call" | custom-call | flops 200000000 | bytes 500000 | tf_op jit(solution)/shard_map/stage/pallas_call | solution.py:196
  39.3 0.0 collective-permute-done.3.refs_0_
  39.4 3.6 %collective-permute-start.4 = (f32[216,512]{1,0:T(8,128)S(1)}, f32[216,512]{1,0:T(8,128)S(1)}, u32[]{:S(2)}, u32[]{:S(2)}) collective-permute-start(f32[216,512]{1,0:T(8,128)S(1)} %pad_maximum_fusion), channel_id=1, source_target_pairs={{0,64},{32,736},{64,128},{96,32},{128,192},{160,96},{192,256},{224... | collective-permute-start | bytes 1327112 | tf_op jit(solution)/shard_map/ppermute | solution.py:326
  43.0 1.5 %stage.11.dense_ref = f32[256,512]{1,0:T(8,128)S(1)} custom-call(s32[2,48]{1,0:T(2,128)S(1)} %table.1, bf16[8,16,512]{2,1,0:T(8,128)(2,1)S(1)} %vertical.1.v_ref, bf16[20,96,512]{2,1,0:T(8,128)(2,1)S(1)} %get-tuple-element.40.w_ref, s32[20,8,512]{2,1,0:T(8,128)S(1)} %get-tuple-element.41.cols_ref), custom_call_target="tpu_custom_call" | custom-call | flops 200000000 | bytes 500000 | tf_op jit(solution)/shard_map/stage/pallas_call | solution.py:196
  44.5 4.9 %stage.12 = f32[216,512]{1,0:T(8,128)S(1)} custom-call(s32[2,48]{1,0:T(2,128)S(1)} %table.1, bf16[8,16,512]{2,1,0:T(8,128)(2,1)S(1)} %vertical.1.v_ref, bf16[32,16,512]{2,1,0:T(8,128)(2,1)S(1)} %bitcast.19, s32[32,16,512]{2,1,0:T(8,128)S(1)} %bitcast.13), custom_call_target="tpu_custom_call" | custom-call | flops 200000000 | bytes 500000 | tf_op jit(solution)/shard_map/stage/pallas_call | solution.py:196
  49.4 1.9 %collective-permute-start.6 = (f32[216,512]{1,0:T(8,128)S(1)}, f32[216,512]{1,0:T(8,128)S(1)}, u32[]{:S(2)}, u32[]{:S(2)}) collective-permute-start(f32[216,512]{1,0:T(8,128)S(1)} %stage.12), channel_id=1, source_target_pairs={{0,32},{32,0},{64,96},{96,64},{128,160},{160,128},{192,224},{224,1... | collective-permute-start | bytes 1327112 | tf_op jit(solution)/shard_map/ppermute | solution.py:326
  51.3 0.0 collective-permute-done.4.refs_1_
  51.3 0.3 merge.4
  51.7 3.5 %collective-permute-start.8 = (f32[128,512]{1,0:T(8,128)S(1)}, f32[128,512]{1,0:T(8,128)S(1)}, u32[]{:S(2)}, u32[]{:S(2)}) collective-permute-start(f32[128,512]{1,0:T(8,128)S(1)} %get-tuple-element.59), channel_id=1, source_target_pairs={{0,64},{32,736},{64,128},{96,32},{128,192},{160,96},{192,256},{224... | collective-permute-start | bytes 786440 | tf_op jit(solution)/shard_map/ppermute | solution.py:326
  55.1 2.0 %collective-permute-start.5 = (f32[128,512]{1,0:T(8,128)S(1)}, f32[128,512]{1,0:T(8,128)S(1)}, u32[]{:S(2)}, u32[]{:S(2)}) collective-permute-start(f32[128,512]{1,0:T(8,128)S(1)} %get-tuple-element.53), channel_id=1, source_target_pairs={{0,64},{32,736},{64,128},{96,32},{128,192},{160,96},{192,256},{224... | collective-permute-start | bytes 786440 | tf_op jit(solution)/shard_map/ppermute | solution.py:326
  57.1 2.0 %stage.14.dense_ref = f32[256,512]{1,0:T(8,128)S(1)} custom-call(s32[2,48]{1,0:T(2,128)S(1)} %table.1, bf16[8,16,512]{2,1,0:T(8,128)(2,1)S(1)} %vertical.1.v_ref, bf16[32,16,512]{2,1,0:T(8,128)(2,1)S(1)} %bitcast.20, s32[32,16,512]{2,1,0:T(8,128)S(1)} %bitcast.14), custom_call_target="tpu_custom_call" | custom-call | flops 200000000 | bytes 500000 | tf_op jit(solution)/shard_map/stage/pallas_call | solution.py:196
  59.1 0.0 collective-permute-done.6.refs_0_
  59.1 0.1 merge.5
  59.2 0.0 collective-permute-done.8
  59.3 4.2 %collective-permute-start.10 = (f32[128,512]{1,0:T(8,128)S(1)}, f32[128,512]{1,0:T(8,128)S(1)}, u32[]{:S(2)}, u32[]{:S(2)}) collective-permute-start(f32[128,512]{1,0:T(8,128)S(1)} %add.28), channel_id=1, source_target_pairs={{0,64},{32,736},{64,128},{96,32},{128,192},{160,96},{192,256},{224... | collective-permute-start | bytes 786440 | tf_op jit(solution)/shard_map/ppermute | solution.py:326
  63.5 0.0 collective-permute-done.5
  63.6 2.7 %collective-permute-start.7 = (f32[128,512]{1,0:T(8,128)S(1)}, f32[128,512]{1,0:T(8,128)S(1)}, u32[]{:S(2)}, u32[]{:S(2)}) collective-permute-start(f32[128,512]{1,0:T(8,128)S(1)} %add.27), channel_id=1, source_target_pairs={{0,64},{32,736},{64,128},{96,32},{128,192},{160,96},{192,256},{224... | collective-permute-start | bytes 786440 | tf_op jit(solution)/shard_map/ppermute | solution.py:326
  66.3 2.0 %stage.15.dense_ref = f32[256,512]{1,0:T(8,128)S(1)} custom-call(s32[2,48]{1,0:T(2,128)S(1)} %table.1, bf16[8,16,512]{2,1,0:T(8,128)(2,1)S(1)} %vertical.1.v_ref, bf16[32,16,512]{2,1,0:T(8,128)(2,1)S(1)} %bitcast.21, s32[32,16,512]{2,1,0:T(8,128)S(1)} %bitcast.15), custom_call_target="tpu_custom_call" | custom-call | flops 200000000 | bytes 500000 | tf_op jit(solution)/shard_map/stage/pallas_call | solution.py:196
  68.3 0.1 merge.6
  68.4 0.0 collective-permute-done.10
  68.5 3.4 %collective-permute-start.12 = (f32[128,512]{1,0:T(8,128)S(1)}, f32[128,512]{1,0:T(8,128)S(1)}, u32[]{:S(2)}, u32[]{:S(2)}) collective-permute-start(f32[128,512]{1,0:T(8,128)S(1)} %add.30), channel_id=1, source_target_pairs={{0,64},{32,736},{64,128},{96,32},{128,192},{160,96},{192,256},{224... | collective-permute-start | bytes 786440 | tf_op jit(solution)/shard_map/ppermute | solution.py:326
  71.9 0.0 collective-permute-done.7
  71.9 2.7 %collective-permute-start.9 = (f32[128,512]{1,0:T(8,128)S(1)}, f32[128,512]{1,0:T(8,128)S(1)}, u32[]{:S(2)}, u32[]{:S(2)}) collective-permute-start(f32[128,512]{1,0:T(8,128)S(1)} %add.29), channel_id=1, source_target_pairs={{0,64},{32,736},{64,128},{96,32},{128,192},{160,96},{192,256},{224... | collective-permute-start | bytes 786440 | tf_op jit(solution)/shard_map/ppermute | solution.py:326
  74.7 2.0 %stage.16.dense_ref = f32[256,512]{1,0:T(8,128)S(1)} custom-call(s32[2,48]{1,0:T(2,128)S(1)} %table.1, bf16[8,16,512]{2,1,0:T(8,128)(2,1)S(1)} %vertical.1.v_ref, bf16[32,16,512]{2,1,0:T(8,128)(2,1)S(1)} %bitcast.22, s32[32,16,512]{2,1,0:T(8,128)S(1)} %bitcast.16), custom_call_target="tpu_custom_call" | custom-call | flops 200000000 | bytes 500000 | tf_op jit(solution)/shard_map/stage/pallas_call | solution.py:196
  76.7 0.1 merge.7
  76.8 0.0 collective-permute-done.12
  76.8 3.4 %collective-permute-start.13 = (f32[128,512]{1,0:T(8,128)S(1)}, f32[128,512]{1,0:T(8,128)S(1)}, u32[]{:S(2)}, u32[]{:S(2)}) collective-permute-start(f32[128,512]{1,0:T(8,128)S(1)} %add.32), channel_id=1, source_target_pairs={{0,64},{32,736},{64,128},{96,32},{128,192},{160,96},{192,256},{224... | collective-permute-start | bytes 786440 | tf_op jit(solution)/shard_map/ppermute | solution.py:326
  80.2 0.0 collective-permute-done.9
  80.3 2.7 %collective-permute-start.11 = (f32[128,512]{1,0:T(8,128)S(1)}, f32[128,512]{1,0:T(8,128)S(1)}, u32[]{:S(2)}, u32[]{:S(2)}) collective-permute-start(f32[128,512]{1,0:T(8,128)S(1)} %add.31), channel_id=1, source_target_pairs={{0,64},{32,736},{64,128},{96,32},{128,192},{160,96},{192,256},{224... | collective-permute-start | bytes 786440 | tf_op jit(solution)/shard_map/ppermute | solution.py:326
  83.1 2.0 %stage.17 = f32[256,512]{1,0:T(8,128)S(1)} custom-call(s32[2,48]{1,0:T(2,128)S(1)} %table.1, bf16[8,16,512]{2,1,0:T(8,128)(2,1)S(1)} %vertical.1.v_ref, bf16[32,16,512]{2,1,0:T(8,128)(2,1)S(1)} %bitcast.23, s32[32,16,512]{2,1,0:T(8,128)S(1)} %bitcast.17), custom_call_target="tpu_custom_call" | custom-call | flops 200000000 | bytes 500000 | tf_op jit(solution)/shard_map/stage/pallas_call | solution.py:196
  85.1 0.0 collective-permute-done.13
  85.1 7.0 %collective-permute-start.14 = (f32[128,512]{1,0:T(8,128)S(1)}, f32[128,512]{1,0:T(8,128)S(1)}, u32[]{:S(2)}, u32[]{:S(2)}) collective-permute-start(f32[128,512]{1,0:T(8,128)S(1)} %slice_add_fusion), channel_id=1, source_target_pairs={{0,32},{32,0},{64,96},{96,64},{128,160},{160,128},{192,224},{224,1... | collective-permute-start | bytes 786440 | tf_op jit(solution)/shard_map/ppermute | solution.py:326
  92.1 0.0 collective-permute-done.11
  92.1 1.1 %collective-permute-done.14 = f32[128,512]{1,0:T(8,128)S(1)} collective-permute-done((f32[128,512]{1,0:T(8,128)S(1)}, f32[128,512]{1,0:T(8,128)S(1)}, u32[]{:S(2)}, u32[]{:S(2)}) %collective-permute-start.14) | collective-permute-done | bytes 262176 | tf_op jit(solution)/shard_map/ppermute | solution.py:326
  93.3 0.1 fusion
  93.3 0.9 copy.7
  (9 shorter events, 0.3 us)
Async XLA Ops:
  1.5 11.8 %copy-start = (s32[8,4,16,512]{3,2,1,0:T(8,128)S(1)}, s32[8,4,16,512]{3,2,1,0:T(8,128)}, u32[]{:S(2)}) copy-start(s32[8,4,16,512]{3,2,1,0:T(8,128)} %param.9) | copy-start | bytes 3145732
  1.5 11.8 %copy-start.1 = (bf16[8,4,16,512]{3,2,1,0:T(8,128)(2,1)S(1)}, bf16[8,4,16,512]{3,2,1,0:T(8,128)(2,1)}, u32[]{:S(2)}) copy-start(bf16[8,4,16,512]{3,2,1,0:T(8,128)(2,1)} %param.8) | copy-start | bytes 1572868
  1.5 14.4 %collective-permute-start = (f32[1,4,8,512]{3,2,1,0:T(8,128)}, f32[1,4,8,512]{3,2,1,0:T(8,128)S(1)}, u32[]{:S(2)}, u32[]{:S(2)}) collective-permute-start(f32[1,4,8,512]{3,2,1,0:T(8,128)} %get-tuple-element.38), channel_id=1, source_target_pairs={{1,0},{2,1},{3,2},{4,3},{5,4},{6,5},{7,6},{8,7},{9,8},{10,9},{11,1... | collective-permute-start | bytes 196616 | tf_op jit(solution)/shard_map/ppermute | solution.py:304
  4.1 11.8 %collective-permute-start.1 = (f32[1,4,8,512]{3,2,1,0:T(8,128)}, f32[1,4,8,512]{3,2,1,0:T(8,128)S(1)}, u32[]{:S(2)}, u32[]{:S(2)}) collective-permute-start(f32[1,4,8,512]{3,2,1,0:T(8,128)} %get-tuple-element.39), channel_id=1, source_target_pairs={{0,1},{1,2},{2,3},{3,4},{4,5},{5,6},{6,7},{7,8},{8,9},{9,10},{10,1... | collective-permute-start | bytes 196616 | tf_op jit(solution)/shard_map/ppermute | solution.py:305
  13.4 2.6 %copy-start.2 = (f32[4,4,8,512]{3,2,1,0:T(8,128)S(1)}, f32[4,4,8,512]{3,2,1,0:T(8,128)}, u32[]{:S(2)}) copy-start(f32[4,4,8,512]{3,2,1,0:T(8,128)} %adj_ref.1) | copy-start | bytes 786436
  13.4 2.6 %copy-start.3 = (f32[3,4,8,512]{3,2,1,0:T(8,128)S(1)}, f32[3,4,8,512]{3,2,1,0:T(8,128)}, u32[]{:S(2)}) copy-start(f32[3,4,8,512]{3,2,1,0:T(8,128)} %coef_ref.1) | copy-start | bytes 589828
  17.3 16.4 %collective-permute-start.2 = (f32[72,512]{1,0:T(8,128)S(1)}, f32[72,512]{1,0:T(8,128)S(1)}, u32[]{:S(2)}, u32[]{:S(2)}) collective-permute-start(f32[72,512]{1,0:T(8,128)S(1)} %stage.9), channel_id=1, source_target_pairs={{0,64},{32,736},{64,128},{96,32},{128,192},{160,96},{192,256},{224... | collective-permute-start | bytes 442376 | tf_op jit(solution)/shard_map/ppermute | solution.py:326
  33.7 5.6 %collective-permute-start.3 = (f32[144,512]{1,0:T(8,128)S(1)}, f32[144,512]{1,0:T(8,128)S(1)}, u32[]{:S(2)}, u32[]{:S(2)}) collective-permute-start(f32[144,512]{1,0:T(8,128)S(1)} %stage.10), channel_id=1, source_target_pairs={{0,32},{32,0},{64,96},{96,64},{128,160},{160,128},{192,224},{224,1... | collective-permute-start | bytes 884744 | tf_op jit(solution)/shard_map/ppermute | solution.py:326
  39.4 11.9 %collective-permute-start.4 = (f32[216,512]{1,0:T(8,128)S(1)}, f32[216,512]{1,0:T(8,128)S(1)}, u32[]{:S(2)}, u32[]{:S(2)}) collective-permute-start(f32[216,512]{1,0:T(8,128)S(1)} %pad_maximum_fusion), channel_id=1, source_target_pairs={{0,64},{32,736},{64,128},{96,32},{128,192},{160,96},{192,256},{224... | collective-permute-start | bytes 1327112 | tf_op jit(solution)/shard_map/ppermute | solution.py:326
  49.4 9.8 %collective-permute-start.6 = (f32[216,512]{1,0:T(8,128)S(1)}, f32[216,512]{1,0:T(8,128)S(1)}, u32[]{:S(2)}, u32[]{:S(2)}) collective-permute-start(f32[216,512]{1,0:T(8,128)S(1)} %stage.12), channel_id=1, source_target_pairs={{0,32},{32,0},{64,96},{96,64},{128,160},{160,128},{192,224},{224,1... | collective-permute-start | bytes 1327112 | tf_op jit(solution)/shard_map/ppermute | solution.py:326
  51.7 7.6 %collective-permute-start.8 = (f32[128,512]{1,0:T(8,128)S(1)}, f32[128,512]{1,0:T(8,128)S(1)}, u32[]{:S(2)}, u32[]{:S(2)}) collective-permute-start(f32[128,512]{1,0:T(8,128)S(1)} %get-tuple-element.59), channel_id=1, source_target_pairs={{0,64},{32,736},{64,128},{96,32},{128,192},{160,96},{192,256},{224... | collective-permute-start | bytes 786440 | tf_op jit(solution)/shard_map/ppermute | solution.py:326
  55.1 8.4 %collective-permute-start.5 = (f32[128,512]{1,0:T(8,128)S(1)}, f32[128,512]{1,0:T(8,128)S(1)}, u32[]{:S(2)}, u32[]{:S(2)}) collective-permute-start(f32[128,512]{1,0:T(8,128)S(1)} %get-tuple-element.53), channel_id=1, source_target_pairs={{0,64},{32,736},{64,128},{96,32},{128,192},{160,96},{192,256},{224... | collective-permute-start | bytes 786440 | tf_op jit(solution)/shard_map/ppermute | solution.py:326
  59.3 9.1 %collective-permute-start.10 = (f32[128,512]{1,0:T(8,128)S(1)}, f32[128,512]{1,0:T(8,128)S(1)}, u32[]{:S(2)}, u32[]{:S(2)}) collective-permute-start(f32[128,512]{1,0:T(8,128)S(1)} %add.28), channel_id=1, source_target_pairs={{0,64},{32,736},{64,128},{96,32},{128,192},{160,96},{192,256},{224... | collective-permute-start | bytes 786440 | tf_op jit(solution)/shard_map/ppermute | solution.py:326
  63.6 8.3 %collective-permute-start.7 = (f32[128,512]{1,0:T(8,128)S(1)}, f32[128,512]{1,0:T(8,128)S(1)}, u32[]{:S(2)}, u32[]{:S(2)}) collective-permute-start(f32[128,512]{1,0:T(8,128)S(1)} %add.27), channel_id=1, source_target_pairs={{0,64},{32,736},{64,128},{96,32},{128,192},{160,96},{192,256},{224... | collective-permute-start | bytes 786440 | tf_op jit(solution)/shard_map/ppermute | solution.py:326
  68.5 8.3 %collective-permute-start.12 = (f32[128,512]{1,0:T(8,128)S(1)}, f32[128,512]{1,0:T(8,128)S(1)}, u32[]{:S(2)}, u32[]{:S(2)}) collective-permute-start(f32[128,512]{1,0:T(8,128)S(1)} %add.30), channel_id=1, source_target_pairs={{0,64},{32,736},{64,128},{96,32},{128,192},{160,96},{192,256},{224... | collective-permute-start | bytes 786440 | tf_op jit(solution)/shard_map/ppermute | solution.py:326
  71.9 8.3 %collective-permute-start.9 = (f32[128,512]{1,0:T(8,128)S(1)}, f32[128,512]{1,0:T(8,128)S(1)}, u32[]{:S(2)}, u32[]{:S(2)}) collective-permute-start(f32[128,512]{1,0:T(8,128)S(1)} %add.29), channel_id=1, source_target_pairs={{0,64},{32,736},{64,128},{96,32},{128,192},{160,96},{192,256},{224... | collective-permute-start | bytes 786440 | tf_op jit(solution)/shard_map/ppermute | solution.py:326
  76.8 8.2 %collective-permute-start.13 = (f32[128,512]{1,0:T(8,128)S(1)}, f32[128,512]{1,0:T(8,128)S(1)}, u32[]{:S(2)}, u32[]{:S(2)}) collective-permute-start(f32[128,512]{1,0:T(8,128)S(1)} %add.32), channel_id=1, source_target_pairs={{0,64},{32,736},{64,128},{96,32},{128,192},{160,96},{192,256},{224... | collective-permute-start | bytes 786440 | tf_op jit(solution)/shard_map/ppermute | solution.py:326
  80.3 11.8 %collective-permute-start.11 = (f32[128,512]{1,0:T(8,128)S(1)}, f32[128,512]{1,0:T(8,128)S(1)}, u32[]{:S(2)}, u32[]{:S(2)}) collective-permute-start(f32[128,512]{1,0:T(8,128)S(1)} %add.31), channel_id=1, source_target_pairs={{0,64},{32,736},{64,128},{96,32},{128,192},{160,96},{192,256},{224... | collective-permute-start | bytes 786440 | tf_op jit(solution)/shard_map/ppermute | solution.py:326
  85.1 8.2 %collective-permute-start.14 = (f32[128,512]{1,0:T(8,128)S(1)}, f32[128,512]{1,0:T(8,128)S(1)}, u32[]{:S(2)}, u32[]{:S(2)}) collective-permute-start(f32[128,512]{1,0:T(8,128)S(1)} %slice_add_fusion), channel_id=1, source_target_pairs={{0,32},{32,0},{64,96},{96,64},{128,160},{160,128},{192,224},{224,1... | collective-permute-start | bytes 786440 | tf_op jit(solution)/shard_map/ppermute | solution.py:326

commit v7 on v6

--- a/solution.py
+++ b/solution.py
@@ -23,7 +23,7 @@
     deps, blk = pair_ref.shape[1:]
     far = chips // 2
     tile = lax.axis_index("tile")
-    chip, core = lax.div(tile, 2), lax.rem(tile, 2)
+    chip, core = tile >> 1, tile & 1
     ahead = 1 - 2 * core
     entries = sum(stage_sizes(far))
 
@@ -33,27 +33,25 @@
     for n in range(2 * chips):
         count[n] = jnp.int32(0)
 
-    def enter(n, _):
-        row, k = lax.div(n, deps), lax.rem(n, deps)
-        owner = pair_ref[0, k, row]
-        turn = count[owner]
-        count[owner] = turn + 1
-        away = lax.rem(ahead * (lax.div(owner, 2) - chip) + chips, chips)
-        back = away > far
-        distance = jnp.where(back, chips - away, away)
-        own = (lax.rem(owner, 2) == core).astype(jnp.int32)
-        half = jnp.where(back, 1 - own, own)
-        start = jnp.where(
-            away == 0,
-            entries - 2 * CAP,
-            jnp.where(away == far, 0, 2 * CAP + (far - 1 - distance) * 4 * CAP + jnp.where(back, 2 * CAP, 0)),
-        )
-        at = start + half * CAP + turn
-        table[0, at] = n
-        table[1, at] = pair_ref[1, k, row]
-        return 0
-
-    lax.fori_loop(0, blk * deps, enter, 0)
+    for row in range(blk):
+        for k in range(deps):
+            owner = pair_ref[0, k, row]
+            turn = count[owner]
+            count[owner] = turn + 1
+            away = ahead * ((owner >> 1) - chip)
+            away = jnp.where(away < 0, away + chips, away)
+            back = away > far
+            distance = jnp.where(back, chips - away, away)
+            own = jnp.where((owner & 1) == core, 1, 0)
+            half = jnp.where(back, 1 - own, own)
+            start = jnp.where(
+                away == 0,
+                entries - 2 * CAP,
+                jnp.where(away == far, 0, 2 * CAP + (far - 1 - distance) * 4 * CAP + jnp.where(back, 2 * CAP, 0)),
+            )
+            at = start + half * CAP + turn
+            table[0, at] = jnp.int32(row * deps + k)
+            table[1, at] = pair_ref[1, k, row]
 
 
 def table_kernel(chips, pair_ref, table, count):

time: 94.8 us -> 94.4 us (level)
  the two profiles are of different devices: /device:TPU:31 before, /device:TPU:33 now
where the time goes in v7:
time: 94.4 us; the launch traced here: 93.8 us
  starting transfers between devices  63.9 us (68%)
  Pallas kernels  24.9 us (26%)
  waiting for transfers between devices  2.67 us (3%)
  other arithmetic  1.06 us (1%)
    ppermute x13, starting transfers between devices, onward(): return [lax.ppermute(value, 'tile', pairs) for value in values]  57.6 us
    pallas_call x9, Pallas kernels, stage(): pl.pallas_call(functools.partial(stage_kernel, groups, deps, rows, ready)...  18.3 us
    ppermute x1, starting transfers between devices, shards(): after = lax.ppermute(first, 'lev', [(i + 1, i) for i in range(levels - 1)])  4.39 us
    pallas_call x1, Pallas kernels, placed(): pl.pallas_call(functools.partial(place_kernel, slots), in_specs=[pl.Block...  2.73 us
    ppermute x1, starting transfers between devices, shards(): before = lax.ppermute(last, 'lev', [(i, i + 1) for i in range(levels - 1)])  1.92 us
  transfers between devices with their start and end apart: 15, of which 2 were waited for; matrix products, arithmetic and copies ran while one was open for 1% of the time, Pallas kernels for 24%

profile of v7, /device:TPU:33, one launch (start us, length us, event | category | flops | bytes accessed | tf_op | source)
XLA Modules:
  0.0 93.8 jit_solution(16485355282851872240)
XLA Ops:
  0.0 1.5 %edges.1 = (f32[1,4,8,512]{3,2,1,0:T(8,128)}, f32[1,4,8,512]{3,2,1,0:T(8,128)}) custom-call(f32[4,4,8,512]{3,2,1,0:T(8,128)} %adj_ref.1, f32[3,4,8,512]{3,2,1,0:T(8,128)} %coef_ref.1, f32[4,4,8,512]{3,2,1,0:T(8,128)} %adj_ref.1, f32[3,4,8,512]{3,2,1,0:T(8,128)} %coef_ref.1), custom_call_target="tpu_custom_call" | custom-call | tf_op jit(solution)/shard_map/edges/pallas_call | solution.py:253
  1.5 0.0 copy-start
  1.5 0.0 copy-start.1
  1.5 4.4 %collective-permute-start = (f32[1,4,8,512]{3,2,1,0:T(8,128)}, f32[1,4,8,512]{3,2,1,0:T(8,128)S(1)}, u32[]{:S(2)}, u32[]{:S(2)}) collective-permute-start(f32[1,4,8,512]{3,2,1,0:T(8,128)} %get-tuple-element.38), channel_id=1, source_target_pairs={{1,0},{2,1},{3,2},{4,3},{5,4},{6,5},{7,6},{8,7},{9,8},{10,9},{11,1... | collective-permute-start | bytes 196616 | tf_op jit(solution)/shard_map/ppermute | solution.py:302
  5.9 1.9 %collective-permute-start.1 = (f32[1,4,8,512]{3,2,1,0:T(8,128)}, f32[1,4,8,512]{3,2,1,0:T(8,128)S(1)}, u32[]{:S(2)}, u32[]{:S(2)}) collective-permute-start(f32[1,4,8,512]{3,2,1,0:T(8,128)} %get-tuple-element.39), channel_id=1, source_target_pairs={{0,1},{1,2},{2,3},{3,4},{4,5},{5,6},{6,7},{7,8},{8,9},{9,10},{10,1... | collective-permute-start | bytes 196616 | tf_op jit(solution)/shard_map/ppermute | solution.py:303
  7.9 0.7 pad_add_fusion.pair_ref
  8.6 1.6 %table.1 = s32[2,48]{1,0:T(2,128)S(1)} custom-call(s32[2,4,8]{2,1,0:T(4,128)S(1)} %pad_add_fusion.pair_ref), custom_call_target="tpu_custom_call" | custom-call | flops 1000000000 | bytes 1000 | tf_op jit(solution)/shard_map/table/pallas_call | solution.py:64
  10.2 0.0 copy-done
  10.2 0.0 copy-done.1
  10.2 0.0 copy-start.2
  10.2 0.0 copy-start.3
  10.3 2.7 %place.1 = (bf16[20,96,512]{2,1,0:T(8,128)(2,1)S(1)}, s32[20,8,512]{2,1,0:T(8,128)S(1)}) custom-call(s32[2,48]{1,0:T(2,128)S(1)} %table.1, bf16[32,16,512]{2,1,0:T(8,128)(2,1)S(1)} %bitcast.18, s32[32,16,512]{2,1,0:T(8,128)S(1)} %bitcast.12), custom_call_target="tpu_custom_call" | custom-call | flops 3000000000 | bytes 1000 | tf_op jit(solution)/shard_map/place/pallas_call | solution.py:113
  13.0 0.0 collective-permute-done.after_ref
  13.0 1.5 %collective-permute-done.1.before_ref = f32[1,4,8,512]{3,2,1,0:T(8,128)S(1)} collective-permute-done((f32[1,4,8,512]{3,2,1,0:T(8,128)}, f32[1,4,8,512]{3,2,1,0:T(8,128)S(1)}, u32[]{:S(2)}, u32[]{:S(2)}) %collective-permute-start.1) | collective-permute-done | bytes 65568 | tf_op jit(solution)/shard_map/ppermute | solution.py:303
  14.5 0.0 copy-done.2
  14.5 0.0 copy-done.3
  14.5 0.1 vertical.1.v_ref
  14.6 1.2 %stage.9 = f32[72,512]{1,0:T(8,128)S(1)} custom-call(s32[2,48]{1,0:T(2,128)S(1)} %table.1, bf16[8,16,512]{2,1,0:T(8,128)(2,1)S(1)} %vertical.1.v_ref, bf16[20,96,512]{2,1,0:T(8,128)(2,1)S(1)} %get-tuple-element.40.w_ref, s32[20,8,512]{2,1,0:T(8,128)S(1)} %get-tuple-element.41.cols_ref), custom_call_target="tpu_custom_call" | custom-call | flops 200000000 | bytes 500000 | tf_op jit(solution)/shard_map/stage/pallas_call | solution.py:194
  15.8 14.6 %collective-permute-start.2 = (f32[72,512]{1,0:T(8,128)S(1)}, f32[72,512]{1,0:T(8,128)S(1)}, u32[]{:S(2)}, u32[]{:S(2)}) collective-permute-start(f32[72,512]{1,0:T(8,128)S(1)} %stage.9), channel_id=1, source_target_pairs={{0,64},{32,736},{64,128},{96,32},{128,192},{160,96},{192,256},{224... | collective-permute-start | bytes 442376 | tf_op jit(solution)/shard_map/ppermute | solution.py:324
  30.4 2.1 %stage.10 = f32[144,512]{1,0:T(8,128)S(1)} custom-call(s32[2,48]{1,0:T(2,128)S(1)} %table.1, bf16[8,16,512]{2,1,0:T(8,128)(2,1)S(1)} %vertical.1.v_ref, bf16[20,96,512]{2,1,0:T(8,128)(2,1)S(1)} %get-tuple-element.40.w_ref, s32[20,8,512]{2,1,0:T(8,128)S(1)} %get-tuple-element.41.cols_ref), custom_call_target="tpu_custom_call" | custom-call | flops 200000000 | bytes 500000 | tf_op jit(solution)/shard_map/stage/pallas_call | solution.py:194
  32.4 0.0 collective-permute-done.2
  32.4 5.3 %collective-permute-start.3 = (f32[144,512]{1,0:T(8,128)S(1)}, f32[144,512]{1,0:T(8,128)S(1)}, u32[]{:S(2)}, u32[]{:S(2)}) collective-permute-start(f32[144,512]{1,0:T(8,128)S(1)} %stage.10), channel_id=1, source_target_pairs={{0,32},{32,0},{64,96},{96,64},{128,160},{160,128},{192,224},{224,1... | collective-permute-start | bytes 884744 | tf_op jit(solution)/shard_map/ppermute | solution.py:324
  37.8 1.2 %stage.13 = f32[72,512]{1,0:T(8,128)S(1)} custom-call(s32[2,48]{1,0:T(2,128)S(1)} %table.1, bf16[8,16,512]{2,1,0:T(8,128)(2,1)S(1)} %vertical.1.v_ref, bf16[20,96,512]{2,1,0:T(8,128)(2,1)S(1)} %get-tuple-element.40.w_ref, s32[20,8,512]{2,1,0:T(8,128)S(1)} %get-tuple-element.41.cols_ref), custom_call_target="tpu_custom_call" | custom-call | flops 200000000 | bytes 500000 | tf_op jit(solution)/shard_map/stage/pallas_call | solution.py:194
  38.9 0.0 collective-permute-done.3.refs_0_
  39.0 3.6 %collective-permute-start.4 = (f32[216,512]{1,0:T(8,128)S(1)}, f32[216,512]{1,0:T(8,128)S(1)}, u32[]{:S(2)}, u32[]{:S(2)}) collective-permute-start(f32[216,512]{1,0:T(8,128)S(1)} %pad_maximum_fusion), channel_id=1, source_target_pairs={{0,64},{32,736},{64,128},{96,32},{128,192},{160,96},{192,256},{224... | collective-permute-start | bytes 1327112 | tf_op jit(solution)/shard_map/ppermute | solution.py:324
  42.7 1.5 %stage.11.dense_ref = f32[256,512]{1,0:T(8,128)S(1)} custom-call(s32[2,48]{1,0:T(2,128)S(1)} %table.1, bf16[8,16,512]{2,1,0:T(8,128)(2,1)S(1)} %vertical.1.v_ref, bf16[20,96,512]{2,1,0:T(8,128)(2,1)S(1)} %get-tuple-element.40.w_ref, s32[20,8,512]{2,1,0:T(8,128)S(1)} %get-tuple-element.41.cols_ref), custom_call_target="tpu_custom_call" | custom-call | flops 200000000 | bytes 500000 | tf_op jit(solution)/shard_map/stage/pallas_call | solution.py:194
  44.1 4.9 %stage.12 = f32[216,512]{1,0:T(8,128)S(1)} custom-call(s32[2,48]{1,0:T(2,128)S(1)} %table.1, bf16[8,16,512]{2,1,0:T(8,128)(2,1)S(1)} %vertical.1.v_ref, bf16[32,16,512]{2,1,0:T(8,128)(2,1)S(1)} %bitcast.19, s32[32,16,512]{2,1,0:T(8,128)S(1)} %bitcast.13), custom_call_target="tpu_custom_call" | custom-call | flops 200000000 | bytes 500000 | tf_op jit(solution)/shard_map/stage/pallas_call | solution.py:194
  49.0 1.9 %collective-permute-start.6 = (f32[216,512]{1,0:T(8,128)S(1)}, f32[216,512]{1,0:T(8,128)S(1)}, u32[]{:S(2)}, u32[]{:S(2)}) collective-permute-start(f32[216,512]{1,0:T(8,128)S(1)} %stage.12), channel_id=1, source_target_pairs={{0,32},{32,0},{64,96},{96,64},{128,160},{160,128},{192,224},{224,1... | collective-permute-start | bytes 1327112 | tf_op jit(solution)/shard_map/ppermute | solution.py:324
  50.9 0.0 collective-permute-done.4.refs_1_
  50.9 0.3 merge.4
  51.3 3.2 %collective-permute-start.8 = (f32[128,512]{1,0:T(8,128)S(1)}, f32[128,512]{1,0:T(8,128)S(1)}, u32[]{:S(2)}, u32[]{:S(2)}) collective-permute-start(f32[128,512]{1,0:T(8,128)S(1)} %get-tuple-element.59), channel_id=1, source_target_pairs={{0,64},{32,736},{64,128},{96,32},{128,192},{160,96},{192,256},{224... | collective-permute-start | bytes 786440 | tf_op jit(solution)/shard_map/ppermute | solution.py:324
  54.5 2.5 %collective-permute-start.5 = (f32[128,512]{1,0:T(8,128)S(1)}, f32[128,512]{1,0:T(8,128)S(1)}, u32[]{:S(2)}, u32[]{:S(2)}) collective-permute-start(f32[128,512]{1,0:T(8,128)S(1)} %get-tuple-element.53), channel_id=1, source_target_pairs={{0,64},{32,736},{64,128},{96,32},{128,192},{160,96},{192,256},{224... | collective-permute-start | bytes 786440 | tf_op jit(solution)/shard_map/ppermute | solution.py:324
  57.1 2.0 %stage.14.dense_ref = f32[256,512]{1,0:T(8,128)S(1)} custom-call(s32[2,48]{1,0:T(2,128)S(1)} %table.1, bf16[8,16,512]{2,1,0:T(8,128)(2,1)S(1)} %vertical.1.v_ref, bf16[32,16,512]{2,1,0:T(8,128)(2,1)S(1)} %bitcast.20, s32[32,16,512]{2,1,0:T(8,128)S(1)} %bitcast.14), custom_call_target="tpu_custom_call" | custom-call | flops 200000000 | bytes 500000 | tf_op jit(solution)/shard_map/stage/pallas_call | solution.py:194
  59.1 0.0 collective-permute-done.6.refs_0_
  59.1 0.1 merge.5
  59.2 0.0 collective-permute-done.8
  59.2 3.7 %collective-permute-start.10 = (f32[128,512]{1,0:T(8,128)S(1)}, f32[128,512]{1,0:T(8,128)S(1)}, u32[]{:S(2)}, u32[]{:S(2)}) collective-permute-start(f32[128,512]{1,0:T(8,128)S(1)} %add.28), channel_id=1, source_target_pairs={{0,64},{32,736},{64,128},{96,32},{128,192},{160,96},{192,256},{224... | collective-permute-start | bytes 786440 | tf_op jit(solution)/shard_map/ppermute | solution.py:324
  62.9 0.0 collective-permute-done.5
  63.0 2.7 %collective-permute-start.7 = (f32[128,512]{1,0:T(8,128)S(1)}, f32[128,512]{1,0:T(8,128)S(1)}, u32[]{:S(2)}, u32[]{:S(2)}) collective-permute-start(f32[128,512]{1,0:T(8,128)S(1)} %add.27), channel_id=1, source_target_pairs={{0,64},{32,736},{64,128},{96,32},{128,192},{160,96},{192,256},{224... | collective-permute-start | bytes 786440 | tf_op jit(solution)/shard_map/ppermute | solution.py:324
  65.7 2.0 %stage.15.dense_ref = f32[256,512]{1,0:T(8,128)S(1)} custom-call(s32[2,48]{1,0:T(2,128)S(1)} %table.1, bf16[8,16,512]{2,1,0:T(8,128)(2,1)S(1)} %vertical.1.v_ref, bf16[32,16,512]{2,1,0:T(8,128)(2,1)S(1)} %bitcast.21, s32[32,16,512]{2,1,0:T(8,128)S(1)} %bitcast.15), custom_call_target="tpu_custom_call" | custom-call | flops 200000000 | bytes 500000 | tf_op jit(solution)/shard_map/stage/pallas_call | solution.py:194
  67.7 0.1 merge.6
  67.8 0.0 collective-permute-done.10
  67.9 3.4 %collective-permute-start.12 = (f32[128,512]{1,0:T(8,128)S(1)}, f32[128,512]{1,0:T(8,128)S(1)}, u32[]{:S(2)}, u32[]{:S(2)}) collective-permute-start(f32[128,512]{1,0:T(8,128)S(1)} %add.30), channel_id=1, source_target_pairs={{0,64},{32,736},{64,128},{96,32},{128,192},{160,96},{192,256},{224... | collective-permute-start | bytes 786440 | tf_op jit(solution)/shard_map/ppermute | solution.py:324
  71.3 0.0 collective-permute-done.7
  71.3 2.7 %collective-permute-start.9 = (f32[128,512]{1,0:T(8,128)S(1)}, f32[128,512]{1,0:T(8,128)S(1)}, u32[]{:S(2)}, u32[]{:S(2)}) collective-permute-start(f32[128,512]{1,0:T(8,128)S(1)} %add.29), channel_id=1, source_target_pairs={{0,64},{32,736},{64,128},{96,32},{128,192},{160,96},{192,256},{224... | collective-permute-start | bytes 786440 | tf_op jit(solution)/shard_map/ppermute | solution.py:324
  74.1 2.0 %stage.16.dense_ref = f32[256,512]{1,0:T(8,128)S(1)} custom-call(s32[2,48]{1,0:T(2,128)S(1)} %table.1, bf16[8,16,512]{2,1,0:T(8,128)(2,1)S(1)} %vertical.1.v_ref, bf16[32,16,512]{2,1,0:T(8,128)(2,1)S(1)} %bitcast.22, s32[32,16,512]{2,1,0:T(8,128)S(1)} %bitcast.16), custom_call_target="tpu_custom_call" | custom-call | flops 200000000 | bytes 500000 | tf_op jit(solution)/shard_map/stage/pallas_call | solution.py:194
  76.1 0.1 merge.7
  76.2 0.0 collective-permute-done.12
  76.2 3.4 %collective-permute-start.13 = (f32[128,512]{1,0:T(8,128)S(1)}, f32[128,512]{1,0:T(8,128)S(1)}, u32[]{:S(2)}, u32[]{:S(2)}) collective-permute-start(f32[128,512]{1,0:T(8,128)S(1)} %add.32), channel_id=1, source_target_pairs={{0,64},{32,736},{64,128},{96,32},{128,192},{160,96},{192,256},{224... | collective-permute-start | bytes 786440 | tf_op jit(solution)/shard_map/ppermute | solution.py:324
  79.6 0.0 collective-permute-done.9
  79.7 2.7 %collective-permute-start.11 = (f32[128,512]{1,0:T(8,128)S(1)}, f32[128,512]{1,0:T(8,128)S(1)}, u32[]{:S(2)}, u32[]{:S(2)}) collective-permute-start(f32[128,512]{1,0:T(8,128)S(1)} %add.31), channel_id=1, source_target_pairs={{0,64},{32,736},{64,128},{96,32},{128,192},{160,96},{192,256},{224... | collective-permute-start | bytes 786440 | tf_op jit(solution)/shard_map/ppermute | solution.py:324
  82.4 1.5 %stage.17 = f32[256,512]{1,0:T(8,128)S(1)} custom-call(s32[2,48]{1,0:T(2,128)S(1)} %table.1, bf16[8,16,512]{2,1,0:T(8,128)(2,1)S(1)} %vertical.1.v_ref, bf16[32,16,512]{2,1,0:T(8,128)(2,1)S(1)} %bitcast.23, s32[32,16,512]{2,1,0:T(8,128)S(1)} %bitcast.17), custom_call_target="tpu_custom_call" | custom-call | flops 200000000 | bytes 500000 | tf_op jit(solution)/shard_map/stage/pallas_call | solution.py:194
  84.0 0.0 collective-permute-done.13
  84.0 7.7 %collective-permute-start.14 = (f32[128,512]{1,0:T(8,128)S(1)}, f32[128,512]{1,0:T(8,128)S(1)}, u32[]{:S(2)}, u32[]{:S(2)}) collective-permute-start(f32[128,512]{1,0:T(8,128)S(1)} %slice_add_fusion), channel_id=1, source_target_pairs={{0,32},{32,0},{64,96},{96,64},{128,160},{160,128},{192,224},{224,1... | collective-permute-start | bytes 786440 | tf_op jit(solution)/shard_map/ppermute | solution.py:324
  91.8 0.0 collective-permute-done.11
  91.8 1.1 %collective-permute-done.14 = f32[128,512]{1,0:T(8,128)S(1)} collective-permute-done((f32[128,512]{1,0:T(8,128)S(1)}, f32[128,512]{1,0:T(8,128)S(1)}, u32[]{:S(2)}, u32[]{:S(2)}) %collective-permute-start.14) | collective-permute-done | bytes 262176 | tf_op jit(solution)/shard_map/ppermute | solution.py:324
  92.9 0.1 fusion
  93.0 0.9 copy.7
  (9 shorter events, 0.3 us)
Async XLA Ops:
  1.5 8.7 %copy-start = (s32[8,4,16,512]{3,2,1,0:T(8,128)S(1)}, s32[8,4,16,512]{3,2,1,0:T(8,128)}, u32[]{:S(2)}) copy-start(s32[8,4,16,512]{3,2,1,0:T(8,128)} %param.9) | copy-start | bytes 3145732
  1.5 8.7 %copy-start.1 = (bf16[8,4,16,512]{3,2,1,0:T(8,128)(2,1)S(1)}, bf16[8,4,16,512]{3,2,1,0:T(8,128)(2,1)}, u32[]{:S(2)}) copy-start(bf16[8,4,16,512]{3,2,1,0:T(8,128)(2,1)} %param.8) | copy-start | bytes 1572868
  1.5 11.4 %collective-permute-start = (f32[1,4,8,512]{3,2,1,0:T(8,128)}, f32[1,4,8,512]{3,2,1,0:T(8,128)S(1)}, u32[]{:S(2)}, u32[]{:S(2)}) collective-permute-start(f32[1,4,8,512]{3,2,1,0:T(8,128)} %get-tuple-element.38), channel_id=1, source_target_pairs={{1,0},{2,1},{3,2},{4,3},{5,4},{6,5},{7,6},{8,7},{9,8},{10,9},{11,1... | collective-permute-start | bytes 196616 | tf_op jit(solution)/shard_map/ppermute | solution.py:302
  5.9 8.5 %collective-permute-start.1 = (f32[1,4,8,512]{3,2,1,0:T(8,128)}, f32[1,4,8,512]{3,2,1,0:T(8,128)S(1)}, u32[]{:S(2)}, u32[]{:S(2)}) collective-permute-start(f32[1,4,8,512]{3,2,1,0:T(8,128)} %get-tuple-element.39), channel_id=1, source_target_pairs={{0,1},{1,2},{2,3},{3,4},{4,5},{5,6},{6,7},{7,8},{8,9},{9,10},{10,1... | collective-permute-start | bytes 196616 | tf_op jit(solution)/shard_map/ppermute | solution.py:303
  10.2 4.3 %copy-start.2 = (f32[4,4,8,512]{3,2,1,0:T(8,128)S(1)}, f32[4,4,8,512]{3,2,1,0:T(8,128)}, u32[]{:S(2)}) copy-start(f32[4,4,8,512]{3,2,1,0:T(8,128)} %adj_ref.1) | copy-start | bytes 786436
  10.2 4.2 %copy-start.3 = (f32[3,4,8,512]{3,2,1,0:T(8,128)S(1)}, f32[3,4,8,512]{3,2,1,0:T(8,128)}, u32[]{:S(2)}) copy-start(f32[3,4,8,512]{3,2,1,0:T(8,128)} %coef_ref.1) | copy-start | bytes 589828
  15.8 16.7 %collective-permute-start.2 = (f32[72,512]{1,0:T(8,128)S(1)}, f32[72,512]{1,0:T(8,128)S(1)}, u32[]{:S(2)}, u32[]{:S(2)}) collective-permute-start(f32[72,512]{1,0:T(8,128)S(1)} %stage.9), channel_id=1, source_target_pairs={{0,64},{32,736},{64,128},{96,32},{128,192},{160,96},{192,256},{224... | collective-permute-start | bytes 442376 | tf_op jit(solution)/shard_map/ppermute | solution.py:324
  32.4 6.5 %collective-permute-start.3 = (f32[144,512]{1,0:T(8,128)S(1)}, f32[144,512]{1,0:T(8,128)S(1)}, u32[]{:S(2)}, u32[]{:S(2)}) collective-permute-start(f32[144,512]{1,0:T(8,128)S(1)} %stage.10), channel_id=1, source_target_pairs={{0,32},{32,0},{64,96},{96,64},{128,160},{160,128},{192,224},{224,1... | collective-permute-start | bytes 884744 | tf_op jit(solution)/shard_map/ppermute | solution.py:324
  39.0 11.9 %collective-permute-start.4 = (f32[216,512]{1,0:T(8,128)S(1)}, f32[216,512]{1,0:T(8,128)S(1)}, u32[]{:S(2)}, u32[]{:S(2)}) collective-permute-start(f32[216,512]{1,0:T(8,128)S(1)} %pad_maximum_fusion), channel_id=1, source_target_pairs={{0,64},{32,736},{64,128},{96,32},{128,192},{160,96},{192,256},{224... | collective-permute-start | bytes 1327112 | tf_op jit(solution)/shard_map/ppermute | solution.py:324
  49.0 10.1 %collective-permute-start.6 = (f32[216,512]{1,0:T(8,128)S(1)}, f32[216,512]{1,0:T(8,128)S(1)}, u32[]{:S(2)}, u32[]{:S(2)}) collective-permute-start(f32[216,512]{1,0:T(8,128)S(1)} %stage.12), channel_id=1, source_target_pairs={{0,32},{32,0},{64,96},{96,64},{128,160},{160,128},{192,224},{224,1... | collective-permute-start | bytes 1327112 | tf_op jit(solution)/shard_map/ppermute | solution.py:324
  51.3 7.9 %collective-permute-start.8 = (f32[128,512]{1,0:T(8,128)S(1)}, f32[128,512]{1,0:T(8,128)S(1)}, u32[]{:S(2)}, u32[]{:S(2)}) collective-permute-start(f32[128,512]{1,0:T(8,128)S(1)} %get-tuple-element.59), channel_id=1, source_target_pairs={{0,64},{32,736},{64,128},{96,32},{128,192},{160,96},{192,256},{224... | collective-permute-start | bytes 786440 | tf_op jit(solution)/shard_map/ppermute | solution.py:324
  54.5 8.4 %collective-permute-start.5 = (f32[128,512]{1,0:T(8,128)S(1)}, f32[128,512]{1,0:T(8,128)S(1)}, u32[]{:S(2)}, u32[]{:S(2)}) collective-permute-start(f32[128,512]{1,0:T(8,128)S(1)} %get-tuple-element.53), channel_id=1, source_target_pairs={{0,64},{32,736},{64,128},{96,32},{128,192},{160,96},{192,256},{224... | collective-permute-start | bytes 786440 | tf_op jit(solution)/shard_map/ppermute | solution.py:324
  59.2 8.6 %collective-permute-start.10 = (f32[128,512]{1,0:T(8,128)S(1)}, f32[128,512]{1,0:T(8,128)S(1)}, u32[]{:S(2)}, u32[]{:S(2)}) collective-permute-start(f32[128,512]{1,0:T(8,128)S(1)} %add.28), channel_id=1, source_target_pairs={{0,64},{32,736},{64,128},{96,32},{128,192},{160,96},{192,256},{224... | collective-permute-start | bytes 786440 | tf_op jit(solution)/shard_map/ppermute | solution.py:324
  63.0 8.3 %collective-permute-start.7 = (f32[128,512]{1,0:T(8,128)S(1)}, f32[128,512]{1,0:T(8,128)S(1)}, u32[]{:S(2)}, u32[]{:S(2)}) collective-permute-start(f32[128,512]{1,0:T(8,128)S(1)} %add.27), channel_id=1, source_target_pairs={{0,64},{32,736},{64,128},{96,32},{128,192},{160,96},{192,256},{224... | collective-permute-start | bytes 786440 | tf_op jit(solution)/shard_map/ppermute | solution.py:324
  67.9 8.3 %collective-permute-start.12 = (f32[128,512]{1,0:T(8,128)S(1)}, f32[128,512]{1,0:T(8,128)S(1)}, u32[]{:S(2)}, u32[]{:S(2)}) collective-permute-start(f32[128,512]{1,0:T(8,128)S(1)} %add.30), channel_id=1, source_target_pairs={{0,64},{32,736},{64,128},{96,32},{128,192},{160,96},{192,256},{224... | collective-permute-start | bytes 786440 | tf_op jit(solution)/shard_map/ppermute | solution.py:324
  71.3 8.3 %collective-permute-start.9 = (f32[128,512]{1,0:T(8,128)S(1)}, f32[128,512]{1,0:T(8,128)S(1)}, u32[]{:S(2)}, u32[]{:S(2)}) collective-permute-start(f32[128,512]{1,0:T(8,128)S(1)} %add.29), channel_id=1, source_target_pairs={{0,64},{32,736},{64,128},{96,32},{128,192},{160,96},{192,256},{224... | collective-permute-start | bytes 786440 | tf_op jit(solution)/shard_map/ppermute | solution.py:324
  76.2 7.8 %collective-permute-start.13 = (f32[128,512]{1,0:T(8,128)S(1)}, f32[128,512]{1,0:T(8,128)S(1)}, u32[]{:S(2)}, u32[]{:S(2)}) collective-permute-start(f32[128,512]{1,0:T(8,128)S(1)} %add.32), channel_id=1, source_target_pairs={{0,64},{32,736},{64,128},{96,32},{128,192},{160,96},{192,256},{224... | collective-permute-start | bytes 786440 | tf_op jit(solution)/shard_map/ppermute | solution.py:324
  79.7 12.1 %collective-permute-start.11 = (f32[128,512]{1,0:T(8,128)S(1)}, f32[128,512]{1,0:T(8,128)S(1)}, u32[]{:S(2)}, u32[]{:S(2)}) collective-permute-start(f32[128,512]{1,0:T(8,128)S(1)} %add.31), channel_id=1, source_target_pairs={{0,64},{32,736},{64,128},{96,32},{128,192},{160,96},{192,256},{224... | collective-permute-start | bytes 786440 | tf_op jit(solution)/shard_map/ppermute | solution.py:324
  84.0 8.9 %collective-permute-start.14 = (f32[128,512]{1,0:T(8,128)S(1)}, f32[128,512]{1,0:T(8,128)S(1)}, u32[]{:S(2)}, u32[]{:S(2)}) collective-permute-start(f32[128,512]{1,0:T(8,128)S(1)} %slice_add_fusion), channel_id=1, source_target_pairs={{0,32},{32,0},{64,96},{96,64},{128,160},{160,128},{192,224},{224,1... | collective-permute-start | bytes 786440 | tf_op jit(solution)/shard_map/ppermute | solution.py:324

commit v8 on v7

--- a/solution.py
+++ b/solution.py
@@ -242,6 +242,22 @@
     )(dense, *(ref for ref, _ in lists)))
 
 
+def finish_kernel(blk, rows, sums_ref, here_ref, swapped_ref, out):
+    for c in range(0, out.shape[-1], LANES):
+        part = slice(c, c + LANES)
+        total = sums_ref[:, part] + here_ref[blk * rows:, part] + swapped_ref[:, part]
+        out[:, :, part] = jnp.swapaxes(total.reshape(blk, rows, LANES), 0, 1)
+
+
+def finish(blk, rows, sums, here, swapped):
+    return pl.pallas_call(
+        functools.partial(finish_kernel, blk, rows),
+        out_shape=jax.ShapeDtypeStruct((rows, blk, sums.shape[1]), jnp.float32),
+        compiler_params=pltpu.CompilerParams(vmem_limit_bytes=6 * MIB),
+        name="finish",
+    )(sums, here, swapped)
+
+
 def edges_kernel(adj0_ref, coef0_ref, adj1_ref, coef1_ref, first_ref, last_ref):
     first_ref[0] = coef0_ref[0] * adj0_ref[0]
     last_ref[0] = coef1_ref[0] * adj1_ref[0]
@@ -335,8 +351,10 @@
     near = far - 2
     (others,) = made(table, ((other_at(far - 1), other_at(near)), True))
     table, others = behind(table, others)
+    (soon,) = made(table, ((own_at(near),), False))
+    table, soon = behind(table, soon)
     (own,) = made(table, ((own_at(far - 1),), True))
-    others, farthest = lax.optimization_barrier((others, farthest))
+    others, farthest, soon = lax.optimization_barrier((others, farthest, soon))
     (given,) = onward([others], sibling)
     table, given = behind(table, given)
     (arrived,) = onward([jnp.concatenate([own, farthest, given[:own.shape[0]]], 0)], ring)
@@ -351,9 +369,8 @@
         return table, *others
 
     for h in range(near, 0, -1):
-        (own,) = made(table, ((own_at(h),), False))
+        (own,) = [soon] if h == near else made(table, ((own_at(h),), False))
         if totals is None:
-            table, own = behind(table, own)
             table, own = exchanged(table, range(near - 1, 0, -1), own)
             totals = merge(blk, rows, own, waiting[h], (arrived, (0, 1, 2)))
         else:
@@ -363,8 +380,7 @@
     sums = onward(totals, ring)
     (here,) = made(table, ((own_at(0),), False))
     (swapped,) = onward([sums[0] + here[:blk * rows]], sibling)
-    result = sums[1] + here[blk * rows:] + swapped
-    result = jnp.transpose(result.reshape(blk, rows, cols), (1, 0, 2))
+    result = finish(blk, rows, sums[1], here, swapped)
     return result.reshape(lev_dev, fields, blk, cols)
 
 

time: 94.4 us -> 93.8 us (level)
  the two profiles are of different devices: /device:TPU:33 before, /device:TPU:31 now
where the time goes in v8:
time: 93.8 us; the launch traced here: 93 us
  starting transfers between devices  64.7 us (69%)
  Pallas kernels  25.6 us (27%)
  waiting for transfers between devices  1.17 us (1%)
  other arithmetic  1 us (1%)
    ppermute x13, starting transfers between devices, onward(): return [lax.ppermute(value, 'tile', pairs) for value in values]  56 us
    pallas_call x9, Pallas kernels, stage(): pl.pallas_call(functools.partial(stage_kernel, groups, deps, rows, ready)...  17.9 us
    ppermute x1, starting transfers between devices, shards(): before = lax.ppermute(last, 'lev', [(i, i + 1) for i in range(levels - 1)])  6.15 us
    pallas_call x1, Pallas kernels, placed(): pl.pallas_call(functools.partial(place_kernel, slots), in_specs=[pl.Block...  3.04 us
    ppermute x1, starting transfers between devices, shards(): after = lax.ppermute(first, 'lev', [(i + 1, i) for i in range(levels - 1)])  2.58 us
  transfers between devices with their start and end apart: 15, of which 1 were waited for; matrix products, arithmetic and copies ran while one was open for 1% of the time, Pallas kernels for 24%

profile of v8, /device:TPU:31, one launch (start us, length us, event | category | flops | bytes accessed | tf_op | source)
XLA Modules:
  0.0 93.0 jit_solution(18300546325251959672)
XLA Ops:
  0.0 1.5 %edges.1 = (f32[1,4,8,512]{3,2,1,0:T(8,128)}, f32[1,4,8,512]{3,2,1,0:T(8,128)}) custom-call(f32[4,4,8,512]{3,2,1,0:T(8,128)} %adj_ref.1, f32[3,4,8,512]{3,2,1,0:T(8,128)} %coef_ref.1, f32[4,4,8,512]{3,2,1,0:T(8,128)} %adj_ref.1, f32[3,4,8,512]{3,2,1,0:T(8,128)} %coef_ref.1), custom_call_target="tpu_custom_call" | custom-call | tf_op jit(solution)/shard_map/edges/pallas_call | solution.py:269
  1.5 0.0 copy-start
  1.5 0.0 copy-start.1
  1.5 2.6 %collective-permute-start = (f32[1,4,8,512]{3,2,1,0:T(8,128)}, f32[1,4,8,512]{3,2,1,0:T(8,128)S(1)}, u32[]{:S(2)}, u32[]{:S(2)}) collective-permute-start(f32[1,4,8,512]{3,2,1,0:T(8,128)} %get-tuple-element.39), channel_id=1, source_target_pairs={{1,0},{2,1},{3,2},{4,3},{5,4},{6,5},{7,6},{8,7},{9,8},{10,9},{11,1... | collective-permute-start | bytes 196616 | tf_op jit(solution)/shard_map/ppermute | solution.py:318
  4.1 6.1 %collective-permute-start.1 = (f32[1,4,8,512]{3,2,1,0:T(8,128)}, f32[1,4,8,512]{3,2,1,0:T(8,128)S(1)}, u32[]{:S(2)}, u32[]{:S(2)}) collective-permute-start(f32[1,4,8,512]{3,2,1,0:T(8,128)} %get-tuple-element.40), channel_id=1, source_target_pairs={{0,1},{1,2},{2,3},{3,4},{4,5},{5,6},{6,7},{7,8},{8,9},{9,10},{10,1... | collective-permute-start | bytes 196616 | tf_op jit(solution)/shard_map/ppermute | solution.py:319
  10.3 0.7 pad_add_fusion.pair_ref
  11.0 1.6 %table.1 = s32[2,48]{1,0:T(2,128)S(1)} custom-call(s32[2,4,8]{2,1,0:T(4,128)S(1)} %pad_add_fusion.pair_ref), custom_call_target="tpu_custom_call" | custom-call | flops 1000000000 | bytes 1000 | tf_op jit(solution)/shard_map/table/pallas_call | solution.py:64
  12.6 0.0 copy-done
  12.6 0.0 copy-done.1
  12.6 0.0 copy-start.2
  12.7 0.0 copy-start.3
  12.7 3.0 %place.1 = (bf16[20,96,512]{2,1,0:T(8,128)(2,1)S(1)}, s32[20,8,512]{2,1,0:T(8,128)S(1)}) custom-call(s32[2,48]{1,0:T(2,128)S(1)} %table.1, bf16[32,16,512]{2,1,0:T(8,128)(2,1)S(1)} %bitcast.15, s32[32,16,512]{2,1,0:T(8,128)S(1)} %bitcast.9), custom_call_target="tpu_custom_call" | custom-call | flops 3000000000 | bytes 1000 | tf_op jit(solution)/shard_map/place/pallas_call | solution.py:113
  15.7 0.0 collective-permute-done.after_ref
  15.7 0.0 collective-permute-done.1.before_ref
  15.7 0.0 copy-done.2
  15.7 0.0 copy-done.3
  15.8 0.1 vertical.1.v_ref
  15.9 1.2 %stage.9 = f32[72,512]{1,0:T(8,128)S(1)} custom-call(s32[2,48]{1,0:T(2,128)S(1)} %table.1, bf16[8,16,512]{2,1,0:T(8,128)(2,1)S(1)} %vertical.1.v_ref, bf16[20,96,512]{2,1,0:T(8,128)(2,1)S(1)} %get-tuple-element.41.w_ref, s32[20,8,512]{2,1,0:T(8,128)S(1)} %get-tuple-element.42.cols_ref), custom_call_target="tpu_custom_call" | custom-call | flops 200000000 | bytes 500000 | tf_op jit(solution)/shard_map/stage/pallas_call | solution.py:194
  17.0 14.1 %collective-permute-start.2 = (f32[72,512]{1,0:T(8,128)S(1)}, f32[72,512]{1,0:T(8,128)S(1)}, u32[]{:S(2)}, u32[]{:S(2)}) collective-permute-start(f32[72,512]{1,0:T(8,128)S(1)} %stage.9), channel_id=1, source_target_pairs={{0,64},{32,736},{64,128},{96,32},{128,192},{160,96},{192,256},{224... | collective-permute-start | bytes 442376 | tf_op jit(solution)/shard_map/ppermute | solution.py:340
  31.2 2.1 %stage.10 = f32[144,512]{1,0:T(8,128)S(1)} custom-call(s32[2,48]{1,0:T(2,128)S(1)} %table.1, bf16[8,16,512]{2,1,0:T(8,128)(2,1)S(1)} %vertical.1.v_ref, bf16[20,96,512]{2,1,0:T(8,128)(2,1)S(1)} %get-tuple-element.41.w_ref, s32[20,8,512]{2,1,0:T(8,128)S(1)} %get-tuple-element.42.cols_ref), custom_call_target="tpu_custom_call" | custom-call | flops 200000000 | bytes 500000 | tf_op jit(solution)/shard_map/stage/pallas_call | solution.py:194
  33.3 1.8 %stage.11.dense_ref = f32[256,512]{1,0:T(8,128)S(1)} custom-call(s32[2,48]{1,0:T(2,128)S(1)} %table.1, bf16[8,16,512]{2,1,0:T(8,128)(2,1)S(1)} %vertical.1.v_ref, bf16[20,96,512]{2,1,0:T(8,128)(2,1)S(1)} %get-tuple-element.41.w_ref, s32[20,8,512]{2,1,0:T(8,128)S(1)} %get-tuple-element.42.cols_ref), custom_call_target="tpu_custom_call" | custom-call | flops 200000000 | bytes 500000 | tf_op jit(solution)/shard_map/stage/pallas_call | solution.py:194
  35.0 0.0 collective-permute-done.2
  35.0 2.7 %collective-permute-start.3 = (f32[144,512]{1,0:T(8,128)S(1)}, f32[144,512]{1,0:T(8,128)S(1)}, u32[]{:S(2)}, u32[]{:S(2)}) collective-permute-start(f32[144,512]{1,0:T(8,128)S(1)} %stage.10), channel_id=1, source_target_pairs={{0,32},{32,0},{64,96},{96,64},{128,160},{160,128},{192,224},{224,1... | collective-permute-start | bytes 884744 | tf_op jit(solution)/shard_map/ppermute | solution.py:340
  37.7 1.4 %stage.13 = f32[72,512]{1,0:T(8,128)S(1)} custom-call(s32[2,48]{1,0:T(2,128)S(1)} %table.1, bf16[8,16,512]{2,1,0:T(8,128)(2,1)S(1)} %vertical.1.v_ref, bf16[20,96,512]{2,1,0:T(8,128)(2,1)S(1)} %get-tuple-element.41.w_ref, s32[20,8,512]{2,1,0:T(8,128)S(1)} %get-tuple-element.42.cols_ref), custom_call_target="tpu_custom_call" | custom-call | flops 200000000 | bytes 500000 | tf_op jit(solution)/shard_map/stage/pallas_call | solution.py:194
  39.2 0.0 collective-permute-done.3.refs_0_
  39.2 3.4 %collective-permute-start.4 = (f32[216,512]{1,0:T(8,128)S(1)}, f32[216,512]{1,0:T(8,128)S(1)}, u32[]{:S(2)}, u32[]{:S(2)}) collective-permute-start(f32[216,512]{1,0:T(8,128)S(1)} %pad_maximum_fusion), channel_id=1, source_target_pairs={{0,64},{32,736},{64,128},{96,32},{128,192},{160,96},{192,256},{224... | collective-permute-start | bytes 1327112 | tf_op jit(solution)/shard_map/ppermute | solution.py:340
  42.6 4.9 %stage.12 = f32[216,512]{1,0:T(8,128)S(1)} custom-call(s32[2,48]{1,0:T(2,128)S(1)} %table.1, bf16[8,16,512]{2,1,0:T(8,128)(2,1)S(1)} %vertical.1.v_ref, bf16[32,16,512]{2,1,0:T(8,128)(2,1)S(1)} %bitcast.16, s32[32,16,512]{2,1,0:T(8,128)S(1)} %bitcast.10), custom_call_target="tpu_custom_call" | custom-call | flops 200000000 | bytes 500000 | tf_op jit(solution)/shard_map/stage/pallas_call | solution.py:194
  47.5 1.9 %collective-permute-start.6 = (f32[216,512]{1,0:T(8,128)S(1)}, f32[216,512]{1,0:T(8,128)S(1)}, u32[]{:S(2)}, u32[]{:S(2)}) collective-permute-start(f32[216,512]{1,0:T(8,128)S(1)} %stage.12), channel_id=1, source_target_pairs={{0,32},{32,0},{64,96},{96,64},{128,160},{160,128},{192,224},{224,1... | collective-permute-start | bytes 1327112 | tf_op jit(solution)/shard_map/ppermute | solution.py:340
  49.4 0.0 collective-permute-done.4.refs_1_
  49.4 0.3 merge.4
  49.8 3.5 %collective-permute-start.8 = (f32[128,512]{1,0:T(8,128)S(1)}, f32[128,512]{1,0:T(8,128)S(1)}, u32[]{:S(2)}, u32[]{:S(2)}) collective-permute-start(f32[128,512]{1,0:T(8,128)S(1)} %get-tuple-element.61), channel_id=1, source_target_pairs={{0,64},{32,736},{64,128},{96,32},{128,192},{160,96},{192,256},{224... | collective-permute-start | bytes 786440 | tf_op jit(solution)/shard_map/ppermute | solution.py:340
  53.3 2.9 %collective-permute-start.5 = (f32[128,512]{1,0:T(8,128)S(1)}, f32[128,512]{1,0:T(8,128)S(1)}, u32[]{:S(2)}, u32[]{:S(2)}) collective-permute-start(f32[128,512]{1,0:T(8,128)S(1)} %get-tuple-element.55), channel_id=1, source_target_pairs={{0,64},{32,736},{64,128},{96,32},{128,192},{160,96},{192,256},{224... | collective-permute-start | bytes 786440 | tf_op jit(solution)/shard_map/ppermute | solution.py:340
  56.2 2.0 %stage.14.dense_ref = f32[256,512]{1,0:T(8,128)S(1)} custom-call(s32[2,48]{1,0:T(2,128)S(1)} %table.1, bf16[8,16,512]{2,1,0:T(8,128)(2,1)S(1)} %vertical.1.v_ref, bf16[32,16,512]{2,1,0:T(8,128)(2,1)S(1)} %bitcast.17, s32[32,16,512]{2,1,0:T(8,128)S(1)} %bitcast.11), custom_call_target="tpu_custom_call" | custom-call | flops 200000000 | bytes 500000 | tf_op jit(solution)/shard_map/stage/pallas_call | solution.py:194
  58.2 0.0 collective-permute-done.6.refs_0_
  58.2 0.1 merge.5
  58.3 0.0 collective-permute-done.8
  58.4 3.3 %collective-permute-start.10 = (f32[128,512]{1,0:T(8,128)S(1)}, f32[128,512]{1,0:T(8,128)S(1)}, u32[]{:S(2)}, u32[]{:S(2)}) collective-permute-start(f32[128,512]{1,0:T(8,128)S(1)} %add.22), channel_id=1, source_target_pairs={{0,64},{32,736},{64,128},{96,32},{128,192},{160,96},{192,256},{224... | collective-permute-start | bytes 786440 | tf_op jit(solution)/shard_map/ppermute | solution.py:340
  61.7 0.0 collective-permute-done.5
  61.7 2.8 %collective-permute-start.7 = (f32[128,512]{1,0:T(8,128)S(1)}, f32[128,512]{1,0:T(8,128)S(1)}, u32[]{:S(2)}, u32[]{:S(2)}) collective-permute-start(f32[128,512]{1,0:T(8,128)S(1)} %add.21), channel_id=1, source_target_pairs={{0,64},{32,736},{64,128},{96,32},{128,192},{160,96},{192,256},{224... | collective-permute-start | bytes 786440 | tf_op jit(solution)/shard_map/ppermute | solution.py:340
  64.6 1.5 %stage.15.dense_ref = f32[256,512]{1,0:T(8,128)S(1)} custom-call(s32[2,48]{1,0:T(2,128)S(1)} %table.1, bf16[8,16,512]{2,1,0:T(8,128)(2,1)S(1)} %vertical.1.v_ref, bf16[32,16,512]{2,1,0:T(8,128)(2,1)S(1)} %bitcast.18, s32[32,16,512]{2,1,0:T(8,128)S(1)} %bitcast.12), custom_call_target="tpu_custom_call" | custom-call | flops 200000000 | bytes 500000 | tf_op jit(solution)/shard_map/stage/pallas_call | solution.py:194
  66.1 0.1 merge.6
  66.2 0.0 collective-permute-done.10
  66.3 3.8 %collective-permute-start.12 = (f32[128,512]{1,0:T(8,128)S(1)}, f32[128,512]{1,0:T(8,128)S(1)}, u32[]{:S(2)}, u32[]{:S(2)}) collective-permute-start(f32[128,512]{1,0:T(8,128)S(1)} %add.24), channel_id=1, source_target_pairs={{0,64},{32,736},{64,128},{96,32},{128,192},{160,96},{192,256},{224... | collective-permute-start | bytes 786440 | tf_op jit(solution)/shard_map/ppermute | solution.py:340
  70.0 0.0 collective-permute-done.7
  70.1 2.8 %collective-permute-start.9 = (f32[128,512]{1,0:T(8,128)S(1)}, f32[128,512]{1,0:T(8,128)S(1)}, u32[]{:S(2)}, u32[]{:S(2)}) collective-permute-start(f32[128,512]{1,0:T(8,128)S(1)} %add.23), channel_id=1, source_target_pairs={{0,64},{32,736},{64,128},{96,32},{128,192},{160,96},{192,256},{224... | collective-permute-start | bytes 786440 | tf_op jit(solution)/shard_map/ppermute | solution.py:340
  72.9 1.5 %stage.16.dense_ref = f32[256,512]{1,0:T(8,128)S(1)} custom-call(s32[2,48]{1,0:T(2,128)S(1)} %table.1, bf16[8,16,512]{2,1,0:T(8,128)(2,1)S(1)} %vertical.1.v_ref, bf16[32,16,512]{2,1,0:T(8,128)(2,1)S(1)} %bitcast.19, s32[32,16,512]{2,1,0:T(8,128)S(1)} %bitcast.13), custom_call_target="tpu_custom_call" | custom-call | flops 200000000 | bytes 500000 | tf_op jit(solution)/shard_map/stage/pallas_call | solution.py:194
  74.5 0.1 merge.7
  74.6 0.0 collective-permute-done.12
  74.6 3.7 %collective-permute-start.13 = (f32[128,512]{1,0:T(8,128)S(1)}, f32[128,512]{1,0:T(8,128)S(1)}, u32[]{:S(2)}, u32[]{:S(2)}) collective-permute-start(f32[128,512]{1,0:T(8,128)S(1)} %add.26), channel_id=1, source_target_pairs={{0,64},{32,736},{64,128},{96,32},{128,192},{160,96},{192,256},{224... | collective-permute-start | bytes 786440 | tf_op jit(solution)/shard_map/ppermute | solution.py:340
  78.4 0.0 collective-permute-done.9
  78.4 2.8 %collective-permute-start.11 = (f32[128,512]{1,0:T(8,128)S(1)}, f32[128,512]{1,0:T(8,128)S(1)}, u32[]{:S(2)}, u32[]{:S(2)}) collective-permute-start(f32[128,512]{1,0:T(8,128)S(1)} %add.25), channel_id=1, source_target_pairs={{0,64},{32,736},{64,128},{96,32},{128,192},{160,96},{192,256},{224... | collective-permute-start | bytes 786440 | tf_op jit(solution)/shard_map/ppermute | solution.py:340
  81.3 1.5 %stage.17.here_ref = f32[256,512]{1,0:T(8,128)S(1)} custom-call(s32[2,48]{1,0:T(2,128)S(1)} %table.1, bf16[8,16,512]{2,1,0:T(8,128)(2,1)S(1)} %vertical.1.v_ref, bf16[32,16,512]{2,1,0:T(8,128)(2,1)S(1)} %bitcast.20, s32[32,16,512]{2,1,0:T(8,128)S(1)} %bitcast.14), custom_call_target="tpu_custom_call" | custom-call | flops 200000000 | bytes 500000 | tf_op jit(solution)/shard_map/stage/pallas_call | solution.py:194
  82.8 0.0 collective-permute-done.13
  82.9 8.2 %collective-permute-start.14 = (f32[128,512]{1,0:T(8,128)S(1)}, f32[128,512]{1,0:T(8,128)S(1)}, u32[]{:S(2)}, u32[]{:S(2)}) collective-permute-start(f32[128,512]{1,0:T(8,128)S(1)} %slice_add_fusion), channel_id=1, source_target_pairs={{0,32},{32,0},{64,96},{96,64},{128,160},{160,128},{192,224},{224,1... | collective-permute-start | bytes 786440 | tf_op jit(solution)/shard_map/ppermute | solution.py:340
  91.1 0.0 collective-permute-done.11.sums_ref
  91.1 1.1 %collective-permute-done.14.swapped_ref = f32[128,512]{1,0:T(8,128)S(1)} collective-permute-done((f32[128,512]{1,0:T(8,128)S(1)}, f32[128,512]{1,0:T(8,128)S(1)}, u32[]{:S(2)}, u32[]{:S(2)}) %collective-permute-start.14) | collective-permute-done | bytes 262176 | tf_op jit(solution)/shard_map/ppermute | solution.py:340
  92.2 0.8 finish.1
  (9 shorter events, 0.3 us)
Async XLA Ops:
  1.5 11.1 %copy-start = (s32[8,4,16,512]{3,2,1,0:T(8,128)S(1)}, s32[8,4,16,512]{3,2,1,0:T(8,128)}, u32[]{:S(2)}) copy-start(s32[8,4,16,512]{3,2,1,0:T(8,128)} %param.9) | copy-start | bytes 3145732
  1.5 11.1 %copy-start.1 = (bf16[8,4,16,512]{3,2,1,0:T(8,128)(2,1)S(1)}, bf16[8,4,16,512]{3,2,1,0:T(8,128)(2,1)}, u32[]{:S(2)}) copy-start(bf16[8,4,16,512]{3,2,1,0:T(8,128)(2,1)} %param.8) | copy-start | bytes 1572868
  1.5 14.2 %collective-permute-start = (f32[1,4,8,512]{3,2,1,0:T(8,128)}, f32[1,4,8,512]{3,2,1,0:T(8,128)S(1)}, u32[]{:S(2)}, u32[]{:S(2)}) collective-permute-start(f32[1,4,8,512]{3,2,1,0:T(8,128)} %get-tuple-element.39), channel_id=1, source_target_pairs={{1,0},{2,1},{3,2},{4,3},{5,4},{6,5},{7,6},{8,7},{9,8},{10,9},{11,1... | collective-permute-start | bytes 196616 | tf_op jit(solution)/shard_map/ppermute | solution.py:318
  4.1 11.6 %collective-permute-start.1 = (f32[1,4,8,512]{3,2,1,0:T(8,128)}, f32[1,4,8,512]{3,2,1,0:T(8,128)S(1)}, u32[]{:S(2)}, u32[]{:S(2)}) collective-permute-start(f32[1,4,8,512]{3,2,1,0:T(8,128)} %get-tuple-element.40), channel_id=1, source_target_pairs={{0,1},{1,2},{2,3},{3,4},{4,5},{5,6},{6,7},{7,8},{8,9},{9,10},{10,1... | collective-permute-start | bytes 196616 | tf_op jit(solution)/shard_map/ppermute | solution.py:319
  12.6 3.1 %copy-start.2 = (f32[4,4,8,512]{3,2,1,0:T(8,128)S(1)}, f32[4,4,8,512]{3,2,1,0:T(8,128)}, u32[]{:S(2)}) copy-start(f32[4,4,8,512]{3,2,1,0:T(8,128)} %adj_ref.1) | copy-start | bytes 786436
  12.7 3.1 %copy-start.3 = (f32[3,4,8,512]{3,2,1,0:T(8,128)S(1)}, f32[3,4,8,512]{3,2,1,0:T(8,128)}, u32[]{:S(2)}) copy-start(f32[3,4,8,512]{3,2,1,0:T(8,128)} %coef_ref.1) | copy-start | bytes 589828
  17.0 18.0 %collective-permute-start.2 = (f32[72,512]{1,0:T(8,128)S(1)}, f32[72,512]{1,0:T(8,128)S(1)}, u32[]{:S(2)}, u32[]{:S(2)}) collective-permute-start(f32[72,512]{1,0:T(8,128)S(1)} %stage.9), channel_id=1, source_target_pairs={{0,64},{32,736},{64,128},{96,32},{128,192},{160,96},{192,256},{224... | collective-permute-start | bytes 442376 | tf_op jit(solution)/shard_map/ppermute | solution.py:340
  35.0 4.2 %collective-permute-start.3 = (f32[144,512]{1,0:T(8,128)S(1)}, f32[144,512]{1,0:T(8,128)S(1)}, u32[]{:S(2)}, u32[]{:S(2)}) collective-permute-start(f32[144,512]{1,0:T(8,128)S(1)} %stage.10), channel_id=1, source_target_pairs={{0,32},{32,0},{64,96},{96,64},{128,160},{160,128},{192,224},{224,1... | collective-permute-start | bytes 884744 | tf_op jit(solution)/shard_map/ppermute | solution.py:340
  39.2 10.2 %collective-permute-start.4 = (f32[216,512]{1,0:T(8,128)S(1)}, f32[216,512]{1,0:T(8,128)S(1)}, u32[]{:S(2)}, u32[]{:S(2)}) collective-permute-start(f32[216,512]{1,0:T(8,128)S(1)} %pad_maximum_fusion), channel_id=1, source_target_pairs={{0,64},{32,736},{64,128},{96,32},{128,192},{160,96},{192,256},{224... | collective-permute-start | bytes 1327112 | tf_op jit(solution)/shard_map/ppermute | solution.py:340
  47.5 10.7 %collective-permute-start.6 = (f32[216,512]{1,0:T(8,128)S(1)}, f32[216,512]{1,0:T(8,128)S(1)}, u32[]{:S(2)}, u32[]{:S(2)}) collective-permute-start(f32[216,512]{1,0:T(8,128)S(1)} %stage.12), channel_id=1, source_target_pairs={{0,32},{32,0},{64,96},{96,64},{128,160},{160,128},{192,224},{224,1... | collective-permute-start | bytes 1327112 | tf_op jit(solution)/shard_map/ppermute | solution.py:340
  49.8 8.5 %collective-permute-start.8 = (f32[128,512]{1,0:T(8,128)S(1)}, f32[128,512]{1,0:T(8,128)S(1)}, u32[]{:S(2)}, u32[]{:S(2)}) collective-permute-start(f32[128,512]{1,0:T(8,128)S(1)} %get-tuple-element.61), channel_id=1, source_target_pairs={{0,64},{32,736},{64,128},{96,32},{128,192},{160,96},{192,256},{224... | collective-permute-start | bytes 786440 | tf_op jit(solution)/shard_map/ppermute | solution.py:340
  53.3 8.4 %collective-permute-start.5 = (f32[128,512]{1,0:T(8,128)S(1)}, f32[128,512]{1,0:T(8,128)S(1)}, u32[]{:S(2)}, u32[]{:S(2)}) collective-permute-start(f32[128,512]{1,0:T(8,128)S(1)} %get-tuple-element.55), channel_id=1, source_target_pairs={{0,64},{32,736},{64,128},{96,32},{128,192},{160,96},{192,256},{224... | collective-permute-start | bytes 786440 | tf_op jit(solution)/shard_map/ppermute | solution.py:340
  58.4 7.8 %collective-permute-start.10 = (f32[128,512]{1,0:T(8,128)S(1)}, f32[128,512]{1,0:T(8,128)S(1)}, u32[]{:S(2)}, u32[]{:S(2)}) collective-permute-start(f32[128,512]{1,0:T(8,128)S(1)} %add.22), channel_id=1, source_target_pairs={{0,64},{32,736},{64,128},{96,32},{128,192},{160,96},{192,256},{224... | collective-permute-start | bytes 786440 | tf_op jit(solution)/shard_map/ppermute | solution.py:340
  61.7 8.3 %collective-permute-start.7 = (f32[128,512]{1,0:T(8,128)S(1)}, f32[128,512]{1,0:T(8,128)S(1)}, u32[]{:S(2)}, u32[]{:S(2)}) collective-permute-start(f32[128,512]{1,0:T(8,128)S(1)} %add.21), channel_id=1, source_target_pairs={{0,64},{32,736},{64,128},{96,32},{128,192},{160,96},{192,256},{224... | collective-permute-start | bytes 786440 | tf_op jit(solution)/shard_map/ppermute | solution.py:340
  66.3 8.3 %collective-permute-start.12 = (f32[128,512]{1,0:T(8,128)S(1)}, f32[128,512]{1,0:T(8,128)S(1)}, u32[]{:S(2)}, u32[]{:S(2)}) collective-permute-start(f32[128,512]{1,0:T(8,128)S(1)} %add.24), channel_id=1, source_target_pairs={{0,64},{32,736},{64,128},{96,32},{128,192},{160,96},{192,256},{224... | collective-permute-start | bytes 786440 | tf_op jit(solution)/shard_map/ppermute | solution.py:340
  70.1 8.3 %collective-permute-start.9 = (f32[128,512]{1,0:T(8,128)S(1)}, f32[128,512]{1,0:T(8,128)S(1)}, u32[]{:S(2)}, u32[]{:S(2)}) collective-permute-start(f32[128,512]{1,0:T(8,128)S(1)} %add.23), channel_id=1, source_target_pairs={{0,64},{32,736},{64,128},{96,32},{128,192},{160,96},{192,256},{224... | collective-permute-start | bytes 786440 | tf_op jit(solution)/shard_map/ppermute | solution.py:340
  74.6 8.2 %collective-permute-start.13 = (f32[128,512]{1,0:T(8,128)S(1)}, f32[128,512]{1,0:T(8,128)S(1)}, u32[]{:S(2)}, u32[]{:S(2)}) collective-permute-start(f32[128,512]{1,0:T(8,128)S(1)} %add.26), channel_id=1, source_target_pairs={{0,64},{32,736},{64,128},{96,32},{128,192},{160,96},{192,256},{224... | collective-permute-start | bytes 786440 | tf_op jit(solution)/shard_map/ppermute | solution.py:340
  78.4 12.6 %collective-permute-start.11 = (f32[128,512]{1,0:T(8,128)S(1)}, f32[128,512]{1,0:T(8,128)S(1)}, u32[]{:S(2)}, u32[]{:S(2)}) collective-permute-start(f32[128,512]{1,0:T(8,128)S(1)} %add.25), channel_id=1, source_target_pairs={{0,64},{32,736},{64,128},{96,32},{128,192},{160,96},{192,256},{224... | collective-permute-start | bytes 786440 | tf_op jit(solution)/shard_map/ppermute | solution.py:340
  82.9 9.3 %collective-permute-start.14 = (f32[128,512]{1,0:T(8,128)S(1)}, f32[128,512]{1,0:T(8,128)S(1)}, u32[]{:S(2)}, u32[]{:S(2)}) collective-permute-start(f32[128,512]{1,0:T(8,128)S(1)} %slice_add_fusion), channel_id=1, source_target_pairs={{0,32},{32,0},{64,96},{96,64},{128,160},{160,128},{192,224},{224,1... | collective-permute-start | bytes 786440 | tf_op jit(solution)/shard_map/ppermute | solution.py:340
